TPU v7x, 512 devices: a whole 4x8x8 slice. The times are simulated.
512 devices in a mesh: inner: 32 (over x, y), outer: 16 (over z, core).
Axes of the slice: x: 4, y: 8, z: 8, core: 2. Of those that a mesh axis runs over, the one named last changes fastest.
Arguments:
- grad_first: bfloat16 [16, 32, 32, 16, 6, 128], P('outer', 'inner'), may hold values from -1 to 1
- grad_second: bfloat16 [16, 32, 32, 16, 6, 128], P('outer', 'inner'), may hold values from -1 to 1
- master: float32 [2, 32, 16, 6, 128], P(None, 'inner', 'outer'), may hold values from -0.12 to 0.12
- first_moment: float32 [2, 32, 16, 6, 128], P(None, 'inner', 'outer'), may hold values from -1.2 to 1.2
- second_moment: float32 [2, 32, 16, 6, 128], P(None, 'inner', 'outer'), may hold values from 0.01 to 1
Outputs:
- new_master: float32 [2, 32, 16, 6, 128], P(None, 'inner', 'outer')
- new_first: float32 [2, 32, 16, 6, 128], P(None, 'inner', 'outer')
- new_second: float32 [2, 32, 16, 6, 128], P(None, 'inner', 'outer')
- weight_codes: bfloat16 [2, 32, 16, 6, 128], P(None, None, 'outer')
- weight_scales: bfloat16 [2, 32, 16, 6], P(None, None, 'outer')
All inputs are finite; a program needn't handle non-finite values.
Results may differ from a plain program's by a relative error of at most 0.012.
Values may be sent and summed in bfloat16 or wider, within the bound.
No kernel may reach another device: no remote copies, remote signals or barrier semaphores. Data moves between devices by JAX's collectives and lax.ppermute only.
A program may use at most 64 MiB of HBM per device.

v0:
```python
import jax
import jax.numpy as jnp
from jax import lax
from jax.sharding import PartitionSpec as P

EPSILON = 1e-06
CODE_RANGE = 448.0
BETA_ONE = 0.9
BETA_TWO = 0.95
LEARN_RATE = 0.01
WEIGHT_DECAY = 0.1
ADAM_EPSILON = 1e-08
steps_done = 10.0


def quantize(values):
    widened = values.astype(jnp.float32)
    block_scale = ((jnp.max(jnp.abs(widened), axis=-1) + EPSILON) / CODE_RANGE).astype(jnp.bfloat16)
    quant_codes = (widened / block_scale.astype(jnp.float32)[..., None]).astype(jnp.bfloat16)
    return (quant_codes, block_scale)


def restore(quant_codes, block_scale):
    return quant_codes.astype(jnp.float32) * block_scale.astype(jnp.float32)[..., None]


def adamw(reduced, params, first, second):
    first_next = BETA_ONE * first + (1.0 - BETA_ONE) * reduced
    second_next = BETA_TWO * second + (1.0 - BETA_TWO) * reduced * reduced
    first_hat = first_next / (1.0 - BETA_ONE**steps_done)
    second_hat = second_next / (1.0 - BETA_TWO**steps_done)
    params_next = params - LEARN_RATE * (
        first_hat / (jnp.sqrt(second_hat) + ADAM_EPSILON) + WEIGHT_DECAY * params
    )
    return (params_next, first_next, second_next)


def local(grad_first, grad_second, master, first_moment, second_moment):
    masters, firsts, seconds, all_codes, all_scales = ([], [], [], [], [])
    for bucket, gradient in enumerate((grad_first, grad_second)):
        codes_one, scale_one = quantize(gradient[0, 0])
        summed = lax.psum_scatter(
            restore(codes_one, scale_one), "inner", scatter_dimension=0, tiled=True
        )[0]
        codes_two, scale_two = quantize(summed)
        reduced = lax.psum_scatter(
            restore(codes_two, scale_two), "outer", scatter_dimension=0, tiled=True
        )[0]
        params_next, first_next, second_next = adamw(
            reduced, master[bucket, 0, 0], first_moment[bucket, 0, 0], second_moment[bucket, 0, 0]
        )
        weight_code, weight_scale = quantize(params_next)
        group_codes, group_scales = (
            lax.all_gather(weight_code[None], "inner", axis=0, tiled=True),
            lax.all_gather(weight_scale[None], "inner", axis=0, tiled=True),
        )
        masters.append(params_next)
        firsts.append(first_next)
        seconds.append(second_next)
        all_codes.append(group_codes)
        all_scales.append(group_scales)
    return (
        jnp.stack(masters)[:, None, None],
        jnp.stack(firsts)[:, None, None],
        jnp.stack(seconds)[:, None, None],
        jnp.stack(all_codes)[:, :, None],
        jnp.stack(all_scales)[:, :, None],
    )


def solution(mesh):
    return jax.shard_map(
        local,
        mesh=mesh,
        in_specs=(
            P("outer", "inner", None, None, None, None),
            P("outer", "inner", None, None, None, None),
            P(None, "inner", "outer", None, None),
            P(None, "inner", "outer", None, None),
            P(None, "inner", "outer", None, None),
        ),
        out_specs=(
            P(None, "inner", "outer", None, None),
            P(None, "inner", "outer", None, None),
            P(None, "inner", "outer", None, None),
            P(None, None, "outer", None, None),
            P(None, None, "outer", None),
        ),
        check_vma=False,
    )
```

profile of v0, /device:TPU:4, one launch (start us, length us, event | category | flops | bytes accessed | tf_op | source)
XLA Modules:
  0.0 763.9 jit_solution(18268727877442711213)
XLA Ops:
  7.2 0.0 copy-start
  7.2 0.0 reduce-scatter.3.cloned.1.call-start
  7.2 1.8 fusion
  9.1 0.2 copy.94
  9.3 0.2 copy.95
  9.5 0.0 copy-done
  9.5 0.0 copy-start.1
  9.5 1.8 convert_multiply_fusion.1
  11.3 0.0 reduce-scatter.3.cloned.1.call-update
  11.3 0.0 reduce-scatter.5.cloned.1.call-start
  11.3 0.0 copy-done.1
  11.3 0.6 fusion.2
  12.0 0.2 copy.100
  12.2 0.2 copy.101
  12.4 0.0 copy-start.3
  12.4 0.0 copy-start.4
  12.4 1.7 convert_multiply_fusion
  14.1 0.0 copy-start.2
  14.1 0.0 reduce-scatter.5.cloned.1.call-update
  14.2 0.0 all-reduce.8.cloned.1.call-start
  14.2 0.0 copy-done.3
  14.2 0.0 copy-done.4
  14.2 223.1 %reduce-scatter.3.cloned.1.call-done = f32[1,16,6,128]{3,2,1,0:T(8,128)} async-done(((f32[32,16,6,128]{3,2,1,0:T(8,128)}), f32[1,16,6,128]{3,2,1,0:T(8,128)}) %reduce-scatter.3.cloned.1.call-update) | async-done | bytes 49168 | tf_op jit(solution)/shard_map/reduce_scatter | solution.py:42
  237.3 0.9 fusion.6
  238.2 224.3 %reduce-scatter.5.cloned.1.call-done = f32[1,16,6,128]{3,2,1,0:T(8,128)} async-done(((f32[32,16,6,128]{3,2,1,0:T(8,128)}), f32[1,16,6,128]{3,2,1,0:T(8,128)}) %reduce-scatter.5.cloned.1.call-update) | async-done | bytes 49168 | tf_op jit(solution)/shard_map/reduce_scatter | solution.py:42
  462.5 0.9 fusion.4
  463.4 1.6 convert_multiply_fusion.3
  465.0 1.6 convert_multiply_fusion.2
  466.5 0.0 all-reduce.8.cloned.1.call-update
  466.6 0.0 copy-done.2
  466.6 1.3 dynamic-slice.2
  467.9 1.3 dynamic-slice
  469.8 110.5 %all-reduce.8.cloned.1.call-done = (f32[16,6,128]{2,1,0:T(8,128)}, f32[16,6,128]{2,1,0:T(8,128)}) async-done(((f32[16,6,128]{2,1,0:T(8,128)}, f32[16,6,128]{2,1,0:T(8,128)}), (f32[16,6,128]{2,1,0:T(8,128)}, f32[16,6,128]{2,1,0:T(8,128)})) %all-reduce.8.cloned.1.call-update) | async-done | bytes 98320
  580.3 1.4 fusion.21
  581.8 1.5 fusion.27
  583.2 0.2 dynamic-update-slice
  583.5 0.2 dynamic-update-slice.1
  583.7 62.8 %all-reduce.5 = (bf16[192]{0:T(256)(128)(2,1)S(1)}, bf16[192]{0:T(256)(128)(2,1)S(1)}) all-reduce(bf16[192]{0:T(256)(128)(2,1)S(1)} %dynamic-update-slice.1, bf16[192]{0:T(256)(128)(2,1)S(1)} %dynamic-update-slice), channel_id=3, replica_groups=mesh['inner'=32,'outer'=16] {'inner'}, use_global_device_ids=true, to_apply=%add.1 | all-reduce | flops 384 | bytes 1536
  646.5 0.1 stack.39
  646.6 0.1 copy.106
  646.7 0.1 stack.40
  646.9 0.1 copy.107
  647.0 1.4 divide_convert_fusion.1
  648.4 55.8 %all_gather.12 = bf16[32,6,128]{2,1,0:T(8,128)(2,1)S(1)} all-gather(bf16[1,6,128]{2,1,0:T(8,128)(2,1)S(1)} %get-tuple-element.29), channel_id=1, replica_groups=mesh['inner'=32,'outer'=16] {'inner'}, dimensions={0}, use_global_device_ids=true | all-gather | bytes 50688 | tf_op jit(solution)/shard_map/all_gather | solution.py:54
  704.2 1.4 divide_convert_fusion
  705.5 48.7 %all_gather.13 = bf16[32,6,128]{2,1,0:T(8,128)(2,1)S(1)} all-gather(bf16[1,6,128]{2,1,0:T(8,128)(2,1)S(1)} %get-tuple-element.33), channel_id=1, replica_groups=mesh['inner'=32,'outer'=16] {'inner'}, dimensions={0}, use_global_device_ids=true | all-gather | bytes 50688 | tf_op jit(solution)/shard_map/all_gather | solution.py:54
  754.3 0.7 copy.111
  754.9 0.6 copy.110
  755.6 0.6 copy.109
  756.2 0.6 copy.108
  756.8 0.6 maximum_bitcast_fusion.4
  (14 shorter events, 0.1 us)
Async XLA Ops:
  7.2 2.3 copy-start
  7.2 230.1 %reduce-scatter.3.cloned.1.call-start = ((), (), s32[]{:S(2)}) async-start(), calls=%async_computation.2 | async-start | bytes 2162688 | tf_op jit(solution)/shard_map/reduce_scatter | solution.py:42
  9.5 1.9 copy-start.1
  11.3 451.2 %reduce-scatter.5.cloned.1.call-start = ((), (), s32[]{:S(2)}) async-start(), calls=%async_computation.3 | async-start | bytes 2162688 | tf_op jit(solution)/shard_map/reduce_scatter | solution.py:42
  12.4 1.8 copy-start.3
  12.4 1.8 copy-start.4
  14.1 452.4 %copy-start.2 = (f32[2,1,1,6,128]{4,2,3,1,0:T(1,128)S(1)}, f32[2,1,1,6,128]{4,2,3,1,0:T(1,128)}, u32[]{:S(2)}) copy-start(f32[2,1,1,6,128]{4,2,3,1,0:T(1,128)} %param.7) | copy-start | bytes 18436
  14.2 566.2 %all-reduce.8.cloned.1.call-start = ((), (), s32[]{:S(2)}) async-start(), calls=%async_computation.4 | async-start | bytes 262144
Sparse Core Ops, SparseCore 0:
  12.4 224.8 reduce-scatter.2
  242.3 220.1 reduce-scatter.4
  466.7 113.5 all-reduce.7
where the time goes:
time: 764 us
  waiting for transfers between devices  558 us (73%)
  blocking collectives  167 us (22%)
  other arithmetic  17.3 us (2%)
  between operations  14.6 us (2%)
    reduce_scatter x2, waiting for transfers between devices, local(): lax.psum_scatter(restore(codes_one, scale_one), 'inner', scatter_dimensio...  447 us
    unnamed x4, waiting for transfers between devices  111 us
    all_gather x2, blocking collectives, local(): lax.all_gather(weight_code[None], 'inner', axis=0, tiled=True)  105 us
    unnamed x1, blocking collectives  62.8 us
  transfers between devices with their start and end apart: 3, of which 3 were waited for; matrix products, arithmetic and copies ran while one was open for 1% of the time, Pallas kernels for 0%

commit v1 on v0

v1 whole, which is shorter than its diff:
```python
import jax
import jax.numpy as jnp
from jax import lax
from jax.sharding import PartitionSpec as P

EPSILON = 1e-06
CODE_RANGE = 448.0
BETA_ONE = 0.9
BETA_TWO = 0.95
LEARN_RATE = 0.01
WEIGHT_DECAY = 0.1
ADAM_EPSILON = 1e-08
steps_done = 10.0


def quantize(values):
    block_scale = ((jnp.max(jnp.abs(values), axis=-1) + EPSILON) / CODE_RANGE).astype(jnp.bfloat16)
    quant_codes = (values / block_scale.astype(jnp.float32)[..., None]).astype(jnp.bfloat16)
    return (quant_codes, block_scale)


def adamw(reduced, params, first, second):
    first_next = BETA_ONE * first + (1.0 - BETA_ONE) * reduced
    second_next = BETA_TWO * second + (1.0 - BETA_TWO) * reduced * reduced
    first_hat = first_next / (1.0 - BETA_ONE**steps_done)
    second_hat = second_next / (1.0 - BETA_TWO**steps_done)
    params_next = params - LEARN_RATE * (
        first_hat / (jnp.sqrt(second_hat) + ADAM_EPSILON) + WEIGHT_DECAY * params
    )
    return (params_next, first_next, second_next)


def local(grad_first, grad_second, master, first_moment, second_moment):
    _, _, inner, outer, rows, width = grad_first.shape
    every = inner * outer
    sent = jnp.concatenate(
        [g.reshape(every, rows, width) for g in (grad_first, grad_second)], axis=1
    )
    held = lax.all_to_all(sent, ("inner", "outer"), 0, 0, tiled=True)
    reduced = jnp.sum(held.astype(jnp.float32), axis=0).reshape(2, rows, width)
    params_next, first_next, second_next = adamw(
        reduced, master[:, 0, 0], first_moment[:, 0, 0], second_moment[:, 0, 0]
    )
    weight_code, weight_scale = quantize(params_next)
    scale_row = jnp.pad(weight_scale.reshape(1, 2 * rows), ((0, 0), (0, width - 2 * rows)))
    packed = jnp.concatenate([weight_code.reshape(2 * rows, width), scale_row], axis=0)
    spread = jnp.broadcast_to(packed[None], (inner,) + packed.shape)
    group = lax.all_to_all(spread, "inner", 0, 0, tiled=True)
    group_codes = group[:, : 2 * rows].reshape(inner, 2, rows, width).transpose(1, 0, 2, 3)
    group_scales = group[:, 2 * rows, : 2 * rows].reshape(inner, 2, rows).transpose(1, 0, 2)
    return (
        params_next[:, None, None],
        first_next[:, None, None],
        second_next[:, None, None],
        group_codes[:, :, None],
        group_scales[:, :, None],
    )


def solution(mesh):
    return jax.shard_map(
        local,
        mesh=mesh,
        in_specs=(
            P("outer", "inner", None, None, None, None),
            P("outer", "inner", None, None, None, None),
            P(None, "inner", "outer", None, None),
            P(None, "inner", "outer", None, None),
            P(None, "inner", "outer", None, None),
        ),
        out_specs=(
            P(None, "inner", "outer", None, None),
            P(None, "inner", "outer", None, None),
            P(None, "inner", "outer", None, None),
            P(None, None, "outer", None, None),
            P(None, None, "outer", None),
        ),
        check_vma=False,
    )
```

time: 764 us -> 98.9 us (0.13)
  the two profiles are of different devices: /device:TPU:4 before, /device:TPU:8 now
where the time goes in v1:
time: 98.9 us; the launch traced here: 98.6 us
  waiting for transfers between devices  61.7 us (62%)
  starting transfers between devices  27.3 us (28%)
  local copies, waits for them, and re-layouts  7.99 us (8%)
    all_to_all x1, waiting for transfers between devices, local(): held = lax.all_to_all(sent, ('inner', 'outer'), 0, 0, tiled=True)  53.8 us
    all_to_all x1, starting transfers between devices, local(): held = lax.all_to_all(sent, ('inner', 'outer'), 0, 0, tiled=True)  21.1 us
    all_to_all x1, waiting for transfers between devices, local(): group = lax.all_to_all(spread, 'inner', 0, 0, tiled=True)  7.9 us
    all_to_all x1, starting transfers between devices, local(): group = lax.all_to_all(spread, 'inner', 0, 0, tiled=True)  6.17 us
    unnamed x16, local copies, waits for them, and re-layouts  4.58 us
    concatenate x1, local copies, waits for them, and re-layouts, local(): jnp.concatenate([g.reshape(every, rows, width) for g in (grad_first, grad...  2.43 us
  transfers between devices with their start and end apart: 2, of which 2 were waited for; matrix products, arithmetic and copies ran while one was open for 2% of the time, Pallas kernels for 0%

profile of v1, /device:TPU:8, one launch (start us, length us, event | category | flops | bytes accessed | tf_op | source)
XLA Modules:
  0.0 98.6 jit_solution(10271438472911541661)
XLA Ops:
  0.6 0.0 copy-start
  0.6 1.3 %copy.67 = bf16[1,1,32,16,6,128]{5,3,2,4,1,0:T(8,128)(2,1)S(1)} copy(bf16[1,1,32,16,6,128]{5,3,4,2,1,0:T(8,128)(2,1)} %param.5) | data formatting | bytes 1572864 | tf_op args[0]
  2.0 0.0 copy-done
  2.0 0.1 copy.68
  2.1 0.1 pad_maximum_fusion
  2.3 2.4 %copy.69 = bf16[512,12,128]{2,1,0:T(8,128)(2,1)} copy(bf16[512,12,128]{2,0,1:T(8,128)(2,1)S(1)} %pad_maximum_fusion) | data formatting | bytes 3145728 | tf_op jit(solution)/shard_map/concatenate | solution.py:36
  4.7 0.0 copy-start.1
  4.7 21.1 %all-to-all-start = ((bf16[512,12,128]{2,1,0:T(8,128)(2,1)}), bf16[512,12,128]{2,1,0:T(8,128)(2,1)S(1)}, u32[]{:S(2)}, u32[]{:S(2)}) async-start(bf16[512,12,128]{2,1,0:T(8,128)(2,1)} %copy.69), calls=%async_computation | async-start | bytes 4194304 | tf_op jit(solution)/shard_map/all_to_all | solution.py:39
  25.8 0.0 copy-done.1
  25.8 0.0 copy-start.2
  25.9 0.0 copy-start.3
  25.9 53.8 %all-to-all-done = bf16[512,12,128]{2,1,0:T(8,128)(2,1)S(1)} async-done(((bf16[512,12,128]{2,1,0:T(8,128)(2,1)}), bf16[512,12,128]{2,1,0:T(8,128)(2,1)S(1)}, u32[]{:S(2)}, u32[]{:S(2)}) %all-to-all-start) | async-done | bytes 1572896 | tf_op jit(solution)/shard_map/all_to_all | solution.py:39
  79.7 0.5 convert_reduce_fusion
  80.3 0.0 copy-done.2
  80.3 0.0 copy-done.3
  80.3 0.1 fusion.3
  80.4 0.1 reshape.110
  80.5 0.1 convert_element_type.42
  80.6 0.1 divide_convert_fusion
  80.7 0.7 broadcast_in_dim.6
  81.4 6.2 %all-to-all-start.1 = ((bf16[32,13,128]{2,1,0:T(8,128)(2,1)}), bf16[32,13,128]{2,1,0:T(8,128)(2,1)S(1)}, u32[]{:S(2)}, u32[]{:S(2)}) async-start(bf16[32,13,128]{2,1,0:T(8,128)(2,1)} %broadcast_in_dim.6), calls=%async_computation.1 | async-start | bytes 262144 | tf_op jit(solution)/shard_map/all_to_all | solution.py:48
  87.6 0.6 copy.80
  88.2 0.6 copy.81
  88.8 0.6 copy.82
  89.4 7.9 %all-to-all-done.1 = bf16[32,13,128]{2,1,0:T(8,128)(2,1)S(1)} async-done(((bf16[32,13,128]{2,1,0:T(8,128)(2,1)}), bf16[32,13,128]{2,1,0:T(8,128)(2,1)S(1)}, u32[]{:S(2)}, u32[]{:S(2)}) %all-to-all-start.1) | async-done | bytes 106528 | tf_op jit(solution)/shard_map/all_to_all | solution.py:48
  97.3 0.7 copy.87
  97.9 0.1 copy.79
  98.0 0.6 copy.84
  (12 shorter events, 0.1 us)
Async XLA Ops:
  0.6 1.4 %copy-start = (bf16[1,1,32,16,6,128]{5,3,4,2,1,0:T(8,128)(2,1)S(1)}, bf16[1,1,32,16,6,128]{5,3,4,2,1,0:T(8,128)(2,1)}, u32[]{:S(2)}) copy-start(bf16[1,1,32,16,6,128]{5,3,4,2,1,0:T(8,128)(2,1)} %param.6) | copy-start | bytes 2359300
  4.7 21.1 %copy-start.1 = (f32[2,1,1,6,128]{4,2,3,1,0:T(1,128)S(1)}, f32[2,1,1,6,128]{4,2,3,1,0:T(1,128)}, u32[]{:S(2)}) copy-start(f32[2,1,1,6,128]{4,2,3,1,0:T(1,128)} %param.7) | copy-start | bytes 18436
  4.7 75.0 %all-to-all-start = ((bf16[512,12,128]{2,1,0:T(8,128)(2,1)}), bf16[512,12,128]{2,1,0:T(8,128)(2,1)S(1)}, u32[]{:S(2)}, u32[]{:S(2)}) async-start(bf16[512,12,128]{2,1,0:T(8,128)(2,1)} %copy.69), calls=%async_computation | async-start | bytes 4194304 | tf_op jit(solution)/shard_map/all_to_all | solution.py:39
  25.8 54.4 %copy-start.2 = (f32[2,1,1,6,128]{4,2,3,1,0:T(1,128)S(1)}, f32[2,1,1,6,128]{4,2,3,1,0:T(1,128)}, u32[]{:S(2)}) copy-start(f32[2,1,1,6,128]{4,2,3,1,0:T(1,128)} %param.8) | copy-start | bytes 18436
  25.9 54.4 %copy-start.3 = (f32[2,1,1,6,128]{4,2,3,1,0:T(1,128)S(1)}, f32[2,1,1,6,128]{4,2,3,1,0:T(1,128)}, u32[]{:S(2)}) copy-start(f32[2,1,1,6,128]{4,2,3,1,0:T(1,128)} %param.9) | copy-start | bytes 18436
  81.4 15.9 %all-to-all-start.1 = ((bf16[32,13,128]{2,1,0:T(8,128)(2,1)}), bf16[32,13,128]{2,1,0:T(8,128)(2,1)S(1)}, u32[]{:S(2)}, u32[]{:S(2)}) async-start(bf16[32,13,128]{2,1,0:T(8,128)(2,1)} %broadcast_in_dim.6), calls=%async_computation.1 | async-start | bytes 262144 | tf_op jit(solution)/shard_map/all_to_all | solution.py:48

commit v2 on v1

v2 whole, which is shorter than its diff:
```python
import jax
import jax.numpy as jnp
from jax import lax
from jax.sharding import Mesh
from jax.sharding import PartitionSpec as P

EPSILON = 1e-06
CODE_RANGE = 448.0
BETA_ONE = 0.9
BETA_TWO = 0.95
LEARN_RATE = 0.01
WEIGHT_DECAY = 0.1
ADAM_EPSILON = 1e-08
steps_done = 10.0


def quantize(values):
    block_scale = ((jnp.max(jnp.abs(values), axis=-1) + EPSILON) / CODE_RANGE).astype(jnp.bfloat16)
    quant_codes = (values / block_scale.astype(jnp.float32)[..., None]).astype(jnp.bfloat16)
    return (quant_codes, block_scale)


def adamw(reduced, params, first, second):
    first_next = BETA_ONE * first + (1.0 - BETA_ONE) * reduced
    second_next = BETA_TWO * second + (1.0 - BETA_TWO) * reduced * reduced
    first_hat = first_next / (1.0 - BETA_ONE**steps_done)
    second_hat = second_next / (1.0 - BETA_TWO**steps_done)
    params_next = params - LEARN_RATE * (
        first_hat / (jnp.sqrt(second_hat) + ADAM_EPSILON) + WEIGHT_DECAY * params
    )
    return (params_next, first_next, second_next)


INNER = ("x", "y_far", "y_near")
OUTER = ("z_far", "z_near", "core")


def exchange(pieces, axes):
    return lax.all_to_all(pieces, axes, 0, 0, tiled=True).astype(jnp.float32)


def local(grad_first, grad_second, master, first_moment, second_moment):
    inner, outer, rows, width = grad_first.shape[2:]
    x, y_far, y_near = (lax.axis_size(name) for name in INNER)
    z_far, z_near, core = (lax.axis_size(name) for name in OUTER)
    grads = jnp.stack([grad_first[0, 0], grad_second[0, 0]])
    grads = grads.reshape(2, x, y_far, y_near, z_far, z_near, core, rows, width)
    pieces = grads.transpose(6, 1, 5, 2, 3, 4, 0, 7, 8).reshape(core, -1, width)
    pair = jnp.sum(exchange(pieces, "core"), axis=0).astype(jnp.bfloat16)
    cross = exchange(pair.reshape(x * z_near, -1, width), ("x", "z_near"))
    cross = jnp.sum(cross, axis=0).astype(jnp.bfloat16)
    last = exchange(
        cross.reshape(y_far * y_near * z_far, 2 * rows, width), ("y_far", "y_near", "z_far")
    )
    reduced = jnp.sum(last, axis=0).reshape(2, rows, width)
    params_next, first_next, second_next = adamw(
        reduced, master[:, 0, 0], first_moment[:, 0, 0], second_moment[:, 0, 0]
    )
    weight_code, weight_scale = quantize(params_next)
    scale_row = jnp.pad(weight_scale.reshape(1, 2 * rows), ((0, 0), (0, width - 2 * rows)))
    packed = jnp.concatenate([weight_code.reshape(2 * rows, width), scale_row], axis=0)
    spread = jnp.broadcast_to(packed[None], (inner,) + packed.shape)
    group = lax.all_to_all(spread, INNER, 0, 0, tiled=True)
    group_codes = group[:, : 2 * rows].reshape(inner, 2, rows, width).transpose(1, 0, 2, 3)
    group_scales = group[:, 2 * rows, : 2 * rows].reshape(inner, 2, rows).transpose(1, 0, 2)
    return (
        params_next[:, None, None],
        first_next[:, None, None],
        second_next[:, None, None],
        group_codes[:, :, None],
        group_scales[:, :, None],
    )


def solution(mesh):
    inner, outer = mesh.devices.shape
    split = Mesh(
        mesh.devices.reshape(inner // 8, 4, 2, outer // 4, 2, 2),
        INNER + OUTER,
    )
    return jax.shard_map(
        local,
        mesh=split,
        in_specs=(P(OUTER, INNER), P(OUTER, INNER)) + (P(None, INNER, OUTER),) * 3,
        out_specs=(P(None, INNER, OUTER),) * 3 + (P(None, None, OUTER),) * 2,
        check_vma=False,
    )
```

time: 98.9 us -> 76.3 us (0.77)
  waiting for transfers between devices: 61.7 us -> 19.8 us
  blocking collectives: 0 us -> 24.2 us
  starting transfers between devices: 27.3 us -> 19.6 us
  other arithmetic: 0.93 us -> 4.93 us
  local copies, waits for them, and re-layouts: 7.99 us -> 6.59 us
    all_to_all x2, waiting for transfers between devices: 61.7 us -> 19.8 us  [the longest x1 11.9 us: exchange(): return lax.all_to_all(pieces, axes, 0, 0, tiled=True).astype(jnp.float32)]
    all_to_all x0 -> x2, blocking collectives: none -> 24.2 us  [exchange(): return lax.all_to_all(pieces, axes, 0, 0, tiled=True).astype(jnp.float32)]
    all_to_all x2, starting transfers between devices: 27.3 us -> 19.6 us  [the longest x1 15.3 us: exchange(): return lax.all_to_all(pieces, axes, 0, 0, tiled=True).astype(jnp.float32)]
    another operation x0 -> x1, other arithmetic: none -> 3.73 us  [local(): grads = jnp.stack([grad_first[0, 0], grad_second[0, 0]])]
    concatenate x1 -> x0, local copies, waits for them, and re-layouts: 2.43 us -> none  [local(): jnp.concatenate([g.reshape(every, rows, width) for g in (grad_first, grad...]
    another operation x0 -> x1, local copies, waits for them, and re-layouts: none -> 1.67 us  [local(): grads = jnp.stack([grad_first[0, 0], grad_second[0, 0]])]
    unnamed x16 -> x12, local copies, waits for them, and re-layouts: 4.58 us -> 3.09 us
where the time goes in v2:
time: 76.3 us; the launch traced here: 75.9 us
  blocking collectives  24.2 us (32%)
  waiting for transfers between devices  19.8 us (26%)
  starting transfers between devices  19.6 us (26%)
  local copies, waits for them, and re-layouts  6.59 us (9%)
  other arithmetic  4.93 us (6%)
  between operations  0.81 us (1%)
    all_to_all x2, blocking collectives, exchange(): return lax.all_to_all(pieces, axes, 0, 0, tiled=True).astype(jnp.float32)  24.2 us
    all_to_all x1, starting transfers between devices, exchange(): return lax.all_to_all(pieces, axes, 0, 0, tiled=True).astype(jnp.float32)  15.3 us
    all_to_all x1, waiting for transfers between devices, exchange(): return lax.all_to_all(pieces, axes, 0, 0, tiled=True).astype(jnp.float32)  11.9 us
    all_to_all x1, waiting for transfers between devices, local(): group = lax.all_to_all(spread, INNER, 0, 0, tiled=True)  7.91 us
    all_to_all x1, starting transfers between devices, local(): group = lax.all_to_all(spread, INNER, 0, 0, tiled=True)  4.28 us
    another operation x1, other arithmetic, local(): grads = jnp.stack([grad_first[0, 0], grad_second[0, 0]])  3.73 us
    unnamed x12, local copies, waits for them, and re-layouts  3.09 us
    another operation x1, local copies, waits for them, and re-layouts, local(): grads = jnp.stack([grad_first[0, 0], grad_second[0, 0]])  1.67 us
  transfers between devices with their start and end apart: 2, of which 2 were waited for; matrix products, arithmetic and copies ran while one was open for 2% of the time, Pallas kernels for 0%

profile of v2, /device:TPU:8, one launch (start us, length us, event | category | flops | bytes accessed | tf_op | source)
XLA Modules:
  0.0 75.9 jit_solution(1063233371116590482)
XLA Ops:
  0.6 3.7 %pad_maximum_fusion = bf16[2,4,4,2,4,2,2,6,128]{8,6,5,4,7,3,2,1,0:T(2,128)(2,1)S(1)} fusion(bf16[1,4,4,2,4,2,2,6,128]{8,6,5,4,7,3,2,1,0:T(2,128)(2,1)} %bitcast.36, bf16[1,4,4,2,4,2,2,6,128]{8,6,5,4,7,3,2,1,0:T(2,128)(2,1)} %bitcast.37), kind=kLoop, calls=%fused_computation | loop fusion | flops 786432 | bytes 3145728 | tf_op jit(solution)/shard_map/stack | solution.py:46
  4.4 1.7 %copy.104 = bf16[2,4,4,2,4,2,2,6,128]{8,6,7,0,4,3,2,5,1:T(2,128)(2,1)S(1)} copy(bf16[2,4,4,2,4,2,2,6,128]{8,6,5,4,7,3,2,1,0:T(2,128)(2,1)S(1)} %pad_maximum_fusion) | data formatting | bytes 3145728 | tf_op jit(solution)/shard_map/stack | solution.py:46
  6.0 0.2 copy.88
  6.2 5.0 %all_to_all.20 = bf16[2,3072,128]{2,1,0:T(8,128)(2,1)S(1)} all-to-all(bf16[2,3072,128]{2,1,0:T(8,128)(2,1)S(1)} %copy.88), channel_id=1, replica_groups=mesh['x'=4,'y_far'=4,'y_near'=2,'z_far'=4,'z_near'=2,'core'=2] {'core'}, dimensions={0} | all-to-all | bytes 3145728 | tf_op jit(solution)/shard_map/all_to_all | solution.py:39
  11.2 0.8 %reduce_sum.33 = bf16[3072,128]{1,0:T(8,128)(2,1)S(1)} reduce(bf16[2,3072,128]{2,1,0:T(8,128)(2,1)S(1)} %all_to_all.20, bf16[]{:T(256)} %constant.7.clone.1), dimensions={0}, to_apply=%region_0.0 | reduce | flops 393216 | bytes 2359298 | tf_op jit(solution)/shard_map/reduce_sum | solution.py:49
  12.1 0.0 copy-start
  12.1 0.0 copy-start.1
  12.1 0.0 copy-start.2
  12.1 19.2 %all_to_all.21 = bf16[8,384,128]{2,1,0:T(8,128)(2,1)S(1)} all-to-all(bf16[8,384,128]{2,1,0:T(8,128)(2,1)S(1)} %bitcast.35), channel_id=1, replica_groups=mesh['x'=4,'y_far'=4,'y_near'=2,'z_far'=4,'z_near'=2,'core'=2] {'x','z_n..., dimensions={0} | all-to-all | bytes 1572864 | tf_op jit(solution)/shard_map/all_to_all | solution.py:39
  31.3 0.1 reduce_sum.34
  31.4 0.7 reshape.115
  32.1 15.3 %all-to-all-start.2 = ((bf16[32,12,128]{2,1,0:T(8,128)(2,1)}), bf16[32,12,128]{2,1,0:T(8,128)(2,1)S(1)}, u32[]{:S(2)}, u32[]{:S(2)}) async-start(bf16[32,12,128]{2,1,0:T(8,128)(2,1)} %reshape.115), calls=%async_computation.2 | async-start | bytes 262144 | tf_op jit(solution)/shard_map/all_to_all | solution.py:39
  47.4 0.0 copy-done
  47.4 11.9 %all-to-all-done.2 = bf16[32,12,128]{2,1,0:T(8,128)(2,1)S(1)} async-done(((bf16[32,12,128]{2,1,0:T(8,128)(2,1)}), bf16[32,12,128]{2,1,0:T(8,128)(2,1)S(1)}, u32[]{:S(2)}, u32[]{:S(2)}) %all-to-all-start.2) | async-done | bytes 98336 | tf_op jit(solution)/shard_map/all_to_all | solution.py:39
  59.4 0.0 copy-done.1
  59.4 0.0 copy-done.2
  59.4 0.1 fusion.3
  59.5 0.1 reshape.119
  59.6 0.1 convert_element_type.46
  59.8 0.1 divide_convert_fusion
  59.9 0.7 broadcast_in_dim.6
  60.5 4.3 %all-to-all-start.3 = ((bf16[32,13,128]{2,1,0:T(8,128)(2,1)}), bf16[32,13,128]{2,1,0:T(8,128)(2,1)S(1)}, u32[]{:S(2)}, u32[]{:S(2)}) async-start(bf16[32,13,128]{2,1,0:T(8,128)(2,1)} %broadcast_in_dim.6), calls=%async_computation.3 | async-start | bytes 262144 | tf_op jit(solution)/shard_map/all_to_all | solution.py:63
  64.8 0.6 copy.100
  65.4 0.6 copy.101
  66.0 0.6 copy.99
  66.6 7.9 %all-to-all-done.3 = bf16[32,13,128]{2,1,0:T(8,128)(2,1)S(1)} async-done(((bf16[32,13,128]{2,1,0:T(8,128)(2,1)}), bf16[32,13,128]{2,1,0:T(8,128)(2,1)S(1)}, u32[]{:S(2)}, u32[]{:S(2)}) %all-to-all-start.3) | async-done | bytes 106528 | tf_op jit(solution)/shard_map/all_to_all | solution.py:63
  74.5 0.7 copy.107
  75.2 0.1 copy.98
  75.3 0.6 copy.103
  (13 shorter events, 0.2 us)
Async XLA Ops:
  12.1 35.3 %copy-start = (f32[2,1,1,6,128]{4,2,3,1,0:T(1,128)S(1)}, f32[2,1,1,6,128]{4,2,3,1,0:T(1,128)}, u32[]{:S(2)}) copy-start(f32[2,1,1,6,128]{4,2,3,1,0:T(1,128)} %param.7) | copy-start | bytes 18436
  12.1 47.3 %copy-start.1 = (f32[2,1,1,6,128]{4,2,3,1,0:T(1,128)S(1)}, f32[2,1,1,6,128]{4,2,3,1,0:T(1,128)}, u32[]{:S(2)}) copy-start(f32[2,1,1,6,128]{4,2,3,1,0:T(1,128)} %param.8) | copy-start | bytes 18436
  12.1 47.3 %copy-start.2 = (f32[2,1,1,6,128]{4,2,3,1,0:T(1,128)S(1)}, f32[2,1,1,6,128]{4,2,3,1,0:T(1,128)}, u32[]{:S(2)}) copy-start(f32[2,1,1,6,128]{4,2,3,1,0:T(1,128)} %param.9) | copy-start | bytes 18436
  32.1 27.2 %all-to-all-start.2 = ((bf16[32,12,128]{2,1,0:T(8,128)(2,1)}), bf16[32,12,128]{2,1,0:T(8,128)(2,1)S(1)}, u32[]{:S(2)}, u32[]{:S(2)}) async-start(bf16[32,12,128]{2,1,0:T(8,128)(2,1)} %reshape.115), calls=%async_computation.2 | async-start | bytes 262144 | tf_op jit(solution)/shard_map/all_to_all | solution.py:39
  60.5 14.0 %all-to-all-start.3 = ((bf16[32,13,128]{2,1,0:T(8,128)(2,1)}), bf16[32,13,128]{2,1,0:T(8,128)(2,1)S(1)}, u32[]{:S(2)}, u32[]{:S(2)}) async-start(bf16[32,13,128]{2,1,0:T(8,128)(2,1)} %broadcast_in_dim.6), calls=%async_computation.3 | async-start | bytes 262144 | tf_op jit(solution)/shard_map/all_to_all | solution.py:63

commit v3 on v2

--- a/solution.py
+++ b/solution.py
@@ -1,6 +1,10 @@
+import functools
+
 import jax
 import jax.numpy as jnp
 from jax import lax
+from jax.experimental import pallas as pl
+from jax.experimental.pallas import tpu as pltpu
 from jax.sharding import Mesh
 from jax.sharding import PartitionSpec as P
 
@@ -39,14 +43,92 @@
     return lax.all_to_all(pieces, axes, 0, 0, tiled=True).astype(jnp.float32)
 
 
+def sort_kernel(split, core_ref, first_ref, second_ref, keep_ref, send_ref, held, kept, sent, in_sem, out_sem):
+    x, z_far, z_near = split
+    inner, rows, outer, width = first_ref.shape
+    span = inner // x
+    half = rows * outer
+    quarter = half // 2
+
+    def load(i, k):
+        part = pl.ds(i * span, span)
+        return pltpu.make_async_copy(
+            (first_ref, second_ref)[k].at[part], held.at[k, part], in_sem.at[i, k]
+        )
+
+    def store(i, k):
+        return pltpu.make_async_copy(
+            (kept, sent)[k].at[i], (keep_ref, send_ref)[k].at[i], out_sem.at[i, k]
+        )
+
+    for i in range(x):
+        for k in range(2):
+            load(i, k).start()
+    to = lax.broadcasted_iota(jnp.int32, (2 * half, 2 * half), 0)
+    at = lax.broadcasted_iota(jnp.int32, (2 * half, 2 * half), 1)
+    core, near = at & 1, (at >> 1) & (z_near - 1)
+    far, block = (at >> 2) & (z_far - 1), at >> 4
+    place = (core ^ core_ref[0]) * half + near * quarter + far * (2 * rows) + block
+    sort = jnp.where(to == place, 1.0, 0.0).astype(jnp.bfloat16)
+    for i in range(x):
+        for k in range(2):
+            load(i, k).wait()
+        for a in range(0, span, 2):
+            pair = [
+                jnp.concatenate(
+                    [held[k, i * span + a + n].reshape(half, width) for k in range(2)], axis=0
+                )
+                for n in range(2)
+            ]
+            out = jnp.dot(
+                sort, jnp.concatenate(pair, axis=1), preferred_element_type=jnp.float32
+            ).astype(jnp.bfloat16)
+            for n in range(2):
+                for z in range(z_near):
+                    lanes = slice(n * width, (n + 1) * width)
+                    kept[i, z, a + n] = out[z * quarter : (z + 1) * quarter, lanes]
+                    sent[i, z, a + n] = out[half + z * quarter : half + (z + 1) * quarter, lanes]
+        for k in range(2):
+            store(i, k).start()
+    for i in range(x):
+        for k in range(2):
+            store(i, k).wait()
+
+
+def sort_rows(core, first, second, split):
+    x, z_far, z_near = split
+    inner, rows, outer, width = first.shape
+    shape = (x, z_near, inner // x, rows * outer // z_near, width)
+    result = jax.ShapeDtypeStruct(shape, first.dtype)
+    anywhere = pl.BlockSpec(memory_space=pl.ANY)
+    return pl.pallas_call(
+        functools.partial(sort_kernel, split),
+        out_shape=(result, result),
+        in_specs=[pl.BlockSpec(memory_space=pltpu.SMEM), anywhere, anywhere],
+        out_specs=(anywhere, anywhere),
+        scratch_shapes=[
+            pltpu.VMEM((2,) + first.shape, first.dtype),
+            pltpu.VMEM(shape, first.dtype),
+            pltpu.VMEM(shape, first.dtype),
+            pltpu.SemaphoreType.DMA((x, 2)),
+            pltpu.SemaphoreType.DMA((x, 2)),
+        ],
+        compiler_params=pltpu.CompilerParams(vmem_limit_bytes=60 * 2**20),
+    )(core, first, second)
+
+
 def local(grad_first, grad_second, master, first_moment, second_moment):
     inner, outer, rows, width = grad_first.shape[2:]
     x, y_far, y_near = (lax.axis_size(name) for name in INNER)
-    z_far, z_near, core = (lax.axis_size(name) for name in OUTER)
-    grads = jnp.stack([grad_first[0, 0], grad_second[0, 0]])
-    grads = grads.reshape(2, x, y_far, y_near, z_far, z_near, core, rows, width)
-    pieces = grads.transpose(6, 1, 5, 2, 3, 4, 0, 7, 8).reshape(core, -1, width)
-    pair = jnp.sum(exchange(pieces, "core"), axis=0).astype(jnp.bfloat16)
+    z_far, z_near, _ = (lax.axis_size(name) for name in OUTER)
+    keep, send = sort_rows(
+        lax.axis_index("core")[None],
+        grad_first[0, 0].transpose(0, 2, 1, 3),
+        grad_second[0, 0].transpose(0, 2, 1, 3),
+        (x, z_far, z_near),
+    )
+    other = lax.ppermute(send, "core", [(0, 1), (1, 0)])
+    pair = (keep.astype(jnp.float32) + other.astype(jnp.float32)).astype(jnp.bfloat16)
     cross = exchange(pair.reshape(x * z_near, -1, width), ("x", "z_near"))
     cross = jnp.sum(cross, axis=0).astype(jnp.bfloat16)
     last = exchange(

time: 76.3 us -> 73.4 us (0.962)
  blocking collectives: 24.2 us -> 19.1 us
  other arithmetic: 4.93 us -> 1.73 us
  Pallas kernels: 0 us -> 2.94 us
  waiting for transfers between devices: 19.8 us -> 22.3 us
  starting transfers between devices: 19.6 us -> 21.5 us
  local copies, waits for them, and re-layouts: 6.59 us -> 4.71 us
    all_to_all x2 -> x1, blocking collectives: 24.2 us -> 19.1 us  [exchange(): return lax.all_to_all(pieces, axes, 0, 0, tiled=True).astype(jnp.float32)]
    another operation x1 -> x0, other arithmetic: 3.73 us -> none  [local(): grads = jnp.stack([grad_first[0, 0], grad_second[0, 0]])]
    pallas_call x0 -> x1, Pallas kernels: none -> 2.94 us  [sort_rows(): pl.pallas_call(functools.partial(sort_kernel, split), out_shape=(result,...]
    ppermute x0 -> x1, waiting for transfers between devices: none -> 2.46 us  [local(): other = lax.ppermute(send, 'core', [(0, 1), (1, 0)])]
    ppermute x0 -> x1, starting transfers between devices: none -> 1.92 us  [local(): other = lax.ppermute(send, 'core', [(0, 1), (1, 0)])]
    another operation x1 -> x0, local copies, waits for them, and re-layouts: 1.67 us -> none  [local(): grads = jnp.stack([grad_first[0, 0], grad_second[0, 0]])]
    convert_element_type x0 -> x1, other arithmetic: none -> 1.34 us  [local(): (keep.astype(jnp.float32) + other.astype(jnp.float32)).astype(jnp.bfloat16)]
    reduce_sum x1 -> x0, other arithmetic: 0.81 us -> none  [local(): pair = jnp.sum(exchange(pieces, 'core'), axis=0).astype(jnp.bfloat16)]
  transfers between devices with their start and end apart: 2 -> 3, of which waited for: 2 -> 3; matrix products, arithmetic and copies ran while one was open for 2% -> 3% of each run, Pallas kernels for 0% -> 0%
where the time goes in v3:
time: 73.4 us; the launch traced here: 73 us
  waiting for transfers between devices  22.3 us (30%)
  starting transfers between devices  21.5 us (29%)
  blocking collectives  19.1 us (26%)
  local copies, waits for them, and re-layouts  4.71 us (6%)
  Pallas kernels  2.94 us (4%)
  other arithmetic  1.73 us (2%)
  between operations  0.78 us (1%)
    all_to_all x1, blocking collectives, exchange(): return lax.all_to_all(pieces, axes, 0, 0, tiled=True).astype(jnp.float32)  19.1 us
    all_to_all x1, starting transfers between devices, exchange(): return lax.all_to_all(pieces, axes, 0, 0, tiled=True).astype(jnp.float32)  15.3 us
    all_to_all x1, waiting for transfers between devices, exchange(): return lax.all_to_all(pieces, axes, 0, 0, tiled=True).astype(jnp.float32)  11.9 us
    all_to_all x1, waiting for transfers between devices, local(): group = lax.all_to_all(spread, INNER, 0, 0, tiled=True)  7.91 us
    all_to_all x1, starting transfers between devices, local(): group = lax.all_to_all(spread, INNER, 0, 0, tiled=True)  4.29 us
    unnamed x12, local copies, waits for them, and re-layouts  3.08 us
    pallas_call x1, Pallas kernels, sort_rows(): pl.pallas_call(functools.partial(sort_kernel, split), out_shape=(result,...  2.94 us
    ppermute x1, waiting for transfers between devices, local(): other = lax.ppermute(send, 'core', [(0, 1), (1, 0)])  2.46 us
  transfers between devices with their start and end apart: 3, of which 3 were waited for; matrix products, arithmetic and copies ran while one was open for 3% of the time, Pallas kernels for 0%

profile of v3, /device:TPU:8, one launch (start us, length us, event | category | flops | bytes accessed | tf_op | source)
XLA Modules:
  0.0 73.0 jit_solution(17678530811660317890)
XLA Ops:
  0.6 2.9 %shard_map.92 = (bf16[4,2,8,48,128]{4,3,2,1,0:T(8,128)(2,1)}, bf16[4,2,8,48,128]{4,3,2,1,0:T(8,128)(2,1)}) custom-call(s32[1]{0:T(128)} %bitcast.core_ref, bf16[32,6,16,128]{3,2,1,0:T(8,128)(2,1)} %bitcast.37, bf16[32,6,16,128]{3,2,1,0:T(8,128)(2,1)} %bitcast.38), custom_call_target="tpu_custom_call" | custom-call | tf_op jit(solution)/shard_map/pallas_call | solution.py:104
  3.6 1.9 %collective-permute-start = (bf16[4,2,8,48,128]{4,3,2,1,0:T(8,128)(2,1)}, bf16[4,2,8,48,128]{4,3,2,1,0:T(8,128)(2,1)S(1)}, u32[]{:S(2)}, u32[]{:S(2)}) collective-permute-start(bf16[4,2,8,48,128]{4,3,2,1,0:T(8,128)(2,1)} %get-tuple-element.8), channel_id=1, source_target_pairs={{0,1},{1,0},{2,3},{3,2},{4,5},{5,4},{6,7},{7,6},{8,9},{9,8},{10,11... | collective-permute-start | bytes 2359304 | tf_op jit(solution)/shard_map/ppermute | solution.py:130
  5.5 2.5 %collective-permute-done = bf16[4,2,8,48,128]{4,3,2,1,0:T(8,128)(2,1)S(1)} collective-permute-done((bf16[4,2,8,48,128]{4,3,2,1,0:T(8,128)(2,1)}, bf16[4,2,8,48,128]{4,3,2,1,0:T(8,128)(2,1)S(1)}, u32[]{:S(2)}, u32[]{:S(2)}) %collective-permute-start) | collective-permute-done | bytes 786464 | tf_op jit(solution)/shard_map/ppermute | solution.py:130
  8.0 1.3 %add_convert_fusion = bf16[4,2,8,48,128]{4,3,2,1,0:T(8,128)(2,1)S(1)} fusion(bf16[4,2,8,48,128]{4,3,2,1,0:T(8,128)(2,1)S(1)} %collective-permute-done, bf16[4,2,8,48,128]{4,3,2,1,0:T(8,128)(2,1)} %get-tuple-element.7), kind=kLoop, calls=%fused_computation | loop fusion | flops 1572864 | bytes 2359296 | tf_op jit(solution)/shard_map/convert_element_type | solution.py:131
  9.3 19.1 %all_to_all.15 = bf16[8,384,128]{2,1,0:T(8,128)(2,1)S(1)} all-to-all(bf16[8,384,128]{2,1,0:T(8,128)(2,1)S(1)} %bitcast.36), channel_id=1, replica_groups=mesh['x'=4,'y_far'=4,'y_near'=2,'z_far'=4,'z_near'=2,'core'=2] {'x','z_n..., dimensions={0} | all-to-all | bytes 1572864 | tf_op jit(solution)/shard_map/all_to_all | solution.py:43
  28.4 0.0 copy-start
  28.4 0.0 copy-start.1
  28.4 0.0 copy-start.2
  28.4 0.1 reduce_sum.21
  28.5 0.7 reshape.106
  29.2 15.3 %all-to-all-start.1 = ((bf16[32,12,128]{2,1,0:T(8,128)(2,1)}), bf16[32,12,128]{2,1,0:T(8,128)(2,1)S(1)}, u32[]{:S(2)}, u32[]{:S(2)}) async-start(bf16[32,12,128]{2,1,0:T(8,128)(2,1)} %reshape.106), calls=%async_computation.1 | async-start | bytes 262144 | tf_op jit(solution)/shard_map/all_to_all | solution.py:43
  44.5 0.0 copy-done
  44.5 11.9 %all-to-all-done.1 = bf16[32,12,128]{2,1,0:T(8,128)(2,1)S(1)} async-done(((bf16[32,12,128]{2,1,0:T(8,128)(2,1)}), bf16[32,12,128]{2,1,0:T(8,128)(2,1)S(1)}, u32[]{:S(2)}, u32[]{:S(2)}) %all-to-all-start.1) | async-done | bytes 98336 | tf_op jit(solution)/shard_map/all_to_all | solution.py:43
  56.5 0.0 copy-done.1
  56.5 0.0 copy-done.2
  56.5 0.1 fusion.3
  56.6 0.1 reshape.110
  56.7 0.1 convert_element_type.56
  56.9 0.1 divide_convert_fusion
  57.0 0.7 broadcast_in_dim.9
  57.6 4.3 %all-to-all-start.2 = ((bf16[32,13,128]{2,1,0:T(8,128)(2,1)}), bf16[32,13,128]{2,1,0:T(8,128)(2,1)S(1)}, u32[]{:S(2)}, u32[]{:S(2)}) async-start(bf16[32,13,128]{2,1,0:T(8,128)(2,1)} %broadcast_in_dim.9), calls=%async_computation.2 | async-start | bytes 262144 | tf_op jit(solution)/shard_map/all_to_all | solution.py:145
  61.9 0.6 copy.70
  62.5 0.6 copy.71
  63.1 0.6 copy.72
  63.7 7.9 %all-to-all-done.2 = bf16[32,13,128]{2,1,0:T(8,128)(2,1)S(1)} async-done(((bf16[32,13,128]{2,1,0:T(8,128)(2,1)}), bf16[32,13,128]{2,1,0:T(8,128)(2,1)S(1)}, u32[]{:S(2)}, u32[]{:S(2)}) %all-to-all-start.2) | async-done | bytes 106528 | tf_op jit(solution)/shard_map/all_to_all | solution.py:145
  71.6 0.7 copy.77
  72.3 0.1 copy.69
  72.4 0.6 copy.74
  (13 shorter events, 0.2 us)
Async XLA Ops:
  3.6 4.4 %collective-permute-start = (bf16[4,2,8,48,128]{4,3,2,1,0:T(8,128)(2,1)}, bf16[4,2,8,48,128]{4,3,2,1,0:T(8,128)(2,1)S(1)}, u32[]{:S(2)}, u32[]{:S(2)}) collective-permute-start(bf16[4,2,8,48,128]{4,3,2,1,0:T(8,128)(2,1)} %get-tuple-element.8), channel_id=1, source_target_pairs={{0,1},{1,0},{2,3},{3,2},{4,5},{5,4},{6,7},{7,6},{8,9},{9,8},{10,11... | collective-permute-start | bytes 2359304 | tf_op jit(solution)/shard_map/ppermute | solution.py:130
  28.4 16.1 %copy-start = (f32[2,1,1,6,128]{4,2,3,1,0:T(1,128)S(1)}, f32[2,1,1,6,128]{4,2,3,1,0:T(1,128)}, u32[]{:S(2)}) copy-start(f32[2,1,1,6,128]{4,2,3,1,0:T(1,128)} %param.7) | copy-start | bytes 18436
  28.4 28.1 %copy-start.1 = (f32[2,1,1,6,128]{4,2,3,1,0:T(1,128)S(1)}, f32[2,1,1,6,128]{4,2,3,1,0:T(1,128)}, u32[]{:S(2)}) copy-start(f32[2,1,1,6,128]{4,2,3,1,0:T(1,128)} %param.8) | copy-start | bytes 18436
  28.4 28.1 %copy-start.2 = (f32[2,1,1,6,128]{4,2,3,1,0:T(1,128)S(1)}, f32[2,1,1,6,128]{4,2,3,1,0:T(1,128)}, u32[]{:S(2)}) copy-start(f32[2,1,1,6,128]{4,2,3,1,0:T(1,128)} %param.9) | copy-start | bytes 18436
  29.2 27.3 %all-to-all-start.1 = ((bf16[32,12,128]{2,1,0:T(8,128)(2,1)}), bf16[32,12,128]{2,1,0:T(8,128)(2,1)S(1)}, u32[]{:S(2)}, u32[]{:S(2)}) async-start(bf16[32,12,128]{2,1,0:T(8,128)(2,1)} %reshape.106), calls=%async_computation.1 | async-start | bytes 262144 | tf_op jit(solution)/shard_map/all_to_all | solution.py:43
  57.6 14.0 %all-to-all-start.2 = ((bf16[32,13,128]{2,1,0:T(8,128)(2,1)}), bf16[32,13,128]{2,1,0:T(8,128)(2,1)S(1)}, u32[]{:S(2)}, u32[]{:S(2)}) async-start(bf16[32,13,128]{2,1,0:T(8,128)(2,1)} %broadcast_in_dim.9), calls=%async_computation.2 | async-start | bytes 262144 | tf_op jit(solution)/shard_map/all_to_all | solution.py:145

commit v4 on v2

v4 whole, which is shorter than its diff:
```python
import jax
import jax.numpy as jnp
from jax import lax
from jax.experimental import pallas as pl
from jax.experimental.pallas import tpu as pltpu
from jax.sharding import Mesh
from jax.sharding import PartitionSpec as P

EPSILON = 1e-06
CODE_RANGE = 448.0
BETA_ONE = 0.9
BETA_TWO = 0.95
LEARN_RATE = 0.01
WEIGHT_DECAY = 0.1
ADAM_EPSILON = 1e-08
steps_done = 10.0

INNER = ("x", "y_far", "y_near")
OUTER = ("z_far", "z_near", "core")
Z_FAR, Z_NEAR, OUTERS = 4, 2, 16
PACKED = 16
ANYWHERE = pl.BlockSpec(memory_space=pl.ANY)
SCALAR = pl.BlockSpec(memory_space=pltpu.SMEM)
VECTOR = pl.BlockSpec(memory_space=pltpu.VMEM)
f32, bf16 = jnp.float32, jnp.bfloat16


def adamw(reduced, params, first, second):
    first_next = BETA_ONE * first + (1.0 - BETA_ONE) * reduced
    second_next = BETA_TWO * second + (1.0 - BETA_TWO) * reduced * reduced
    first_hat = first_next / (1.0 - BETA_ONE**steps_done)
    second_hat = second_next / (1.0 - BETA_TWO**steps_done)
    params_next = params - LEARN_RATE * (
        first_hat / (jnp.sqrt(second_hat) + ADAM_EPSILON) + WEIGHT_DECAY * params
    )
    return (params_next, first_next, second_next)


def sorter(core, rows):
    half = rows * OUTERS
    to = lax.broadcasted_iota(jnp.int32, (half, 2 * half), 0)
    at = lax.broadcasted_iota(jnp.int32, (half, 2 * half), 1)
    near, far, block = (at >> 1) & (Z_NEAR - 1), (at >> 2) & (Z_FAR - 1), at >> 4
    place = near * (half // Z_NEAR) + far * (2 * rows) + block
    return jnp.where((to == place) & ((at & 1) == core), 1.0, 0.0).astype(bf16)


def sort_two(sort, first, second, a):
    half, width = first.shape[1] * first.shape[2], first.shape[3]
    columns = [
        jnp.concatenate([ref[a + n].reshape(half, width) for ref in (first, second)], axis=0)
        for n in range(2)
    ]
    return jnp.dot(sort, jnp.concatenate(columns, axis=1), preferred_element_type=f32)


def places(values, a, per_x, width):
    part = values.shape[0] // Z_NEAR
    for n in range(2):
        for z in range(Z_NEAR):
            yield (
                ((a + n) // per_x, z, (a + n) % per_x),
                values[z * part : (z + 1) * part, n * width : (n + 1) * width],
            )


def send_kernel(core_ref, first_ref, second_ref, send_ref, first, second, sent, in_sem, out_sem):
    inner, rows, _, width = first_ref.shape
    x, _, per_x, _, _ = send_ref.shape
    loads = in_sem.shape[0]
    span = inner // loads

    def load(i, k):
        part = pl.ds(i * span, span)
        return pltpu.make_async_copy(
            (first_ref, second_ref)[k].at[part], (first, second)[k].at[part], in_sem.at[i, k]
        )

    def store(i):
        return pltpu.make_async_copy(sent.at[i], send_ref.at[i], out_sem.at[i])

    for i in range(loads):
        for k in range(2):
            load(i, k).start()
    sort = sorter(1 - core_ref[0], rows)
    for a in range(0, inner, 2):
        if a % span == 0:
            for k in range(2):
                load(a // span, k).wait()
        values = sort_two(sort, first, second, a).astype(bf16)
        for place, piece in places(values, a, per_x, width):
            sent[place] = piece
        if (a + 2) % per_x == 0:
            store(a // per_x).start()
    for i in range(x):
        store(i).wait()


def rows_to_send(core, first, second, x):
    inner, rows, outer, width = first.shape
    shape = (x, Z_NEAR, inner // x, rows * outer // 2, width)
    return pl.pallas_call(
        send_kernel,
        out_shape=jax.ShapeDtypeStruct(shape, bf16),
        in_specs=[SCALAR, ANYWHERE, ANYWHERE],
        out_specs=ANYWHERE,
        scratch_shapes=[
            pltpu.VMEM(first.shape, bf16),
            pltpu.VMEM(first.shape, bf16),
            pltpu.VMEM(shape, bf16),
            pltpu.SemaphoreType.DMA((2, 2)),
            pltpu.SemaphoreType.DMA((x,)),
        ],
        compiler_params=pltpu.CompilerParams(vmem_limit_bytes=60 * 2**20),
    )(core, first, second)


def add_kernel(core_ref, first_ref, second_ref, other_ref, out_ref):
    inner, rows, _, width = first_ref.shape
    per_x = other_ref.shape[2]
    sort = sorter(core_ref[0], rows)
    for a in range(0, inner, 2):
        values = sort_two(sort, first_ref, second_ref, a)
        for place, piece in places(values, a, per_x, width):
            out_ref[place] = (piece + other_ref[place].astype(f32)).astype(bf16)


def add_own_rows(core, first, second, other):
    return pl.pallas_call(
        add_kernel,
        out_shape=jax.ShapeDtypeStruct(other.shape, bf16),
        in_specs=[SCALAR, VECTOR, VECTOR, VECTOR],
        out_specs=VECTOR,
        compiler_params=pltpu.CompilerParams(vmem_limit_bytes=16 * 2**20),
    )(core, first, second, other)


def fold_kernel(terms_ref, out_ref):
    total = jnp.sum(terms_ref[...].astype(f32), axis=0)
    pieces, rows, _ = out_ref.shape
    for i in range(pieces):
        out_ref[i] = total[i * rows : (i + 1) * rows].astype(bf16)


def fold(terms, shape):
    return pl.pallas_call(
        fold_kernel,
        out_shape=jax.ShapeDtypeStruct(shape, bf16),
        in_specs=[VECTOR],
        out_specs=VECTOR,
        compiler_params=pltpu.CompilerParams(vmem_limit_bytes=8 * 2**20),
    )(terms)


def update_kernel(terms_ref, master_ref, first_ref, second_ref, *out_refs):
    _, blocks, width = terms_ref.shape
    reduced = jnp.sum(terms_ref[...].astype(f32), axis=0)
    state = (
        jnp.concatenate([ref[k] for k in range(blocks)], axis=0)
        for ref in (master_ref, first_ref, second_ref)
    )
    updated = adamw(reduced, *state)
    for ref, value in zip(out_refs, updated):
        for k in range(blocks):
            ref[k] = value[k : k + 1]
    params_next = updated[0]
    largest = jnp.max(jnp.abs(params_next), axis=-1, keepdims=True)
    scale = ((largest + EPSILON) / CODE_RANGE).astype(bf16).astype(f32)
    row = lax.broadcasted_iota(jnp.int32, (blocks, width), 0)
    lane = lax.broadcasted_iota(jnp.int32, (blocks, width), 1)
    scale_row = jnp.sum(jnp.where(row == lane, scale, 0.0), axis=0, keepdims=True)
    filling = jnp.zeros((PACKED - blocks - 1, width), f32)
    packed = jnp.concatenate([params_next / scale, scale_row, filling], axis=0).astype(bf16)
    spread_ref = out_refs[3]
    for i in range(spread_ref.shape[0]):
        spread_ref[i] = packed


def update(terms, master, first, second, members):
    state = jax.ShapeDtypeStruct(master.shape, f32)
    spread = jax.ShapeDtypeStruct((members, PACKED, master.shape[-1]), bf16)
    return pl.pallas_call(
        update_kernel,
        out_shape=(state, state, state, spread),
        in_specs=[VECTOR] * 4,
        out_specs=(VECTOR,) * 4,
        compiler_params=pltpu.CompilerParams(vmem_limit_bytes=8 * 2**20),
    )(terms, master, first, second)


def unpack_kernel(group_ref, codes_ref, scales_ref):
    members, packed, width = group_ref.shape
    blocks = codes_ref.shape[0]
    shape = ((blocks + 1) * members, members * packed)
    to = lax.broadcasted_iota(jnp.int32, shape, 0)
    at = lax.broadcasted_iota(jnp.int32, shape, 1)
    sort = jnp.where(to == (at & (PACKED - 1)) * members + (at >> 4), 1.0, 0.0).astype(bf16)
    rows = jnp.dot(sort, group_ref[...].reshape(members * packed, width), preferred_element_type=f32)
    for k in range(blocks):
        codes_ref[k] = rows[k * members : (k + 1) * members].astype(bf16)
    scales = rows[blocks * members :].T
    half = blocks // 2
    for j in range(half):
        scales_ref[j] = jnp.concatenate(
            [scales[k : k + 1] for k in (j, half + j)], axis=0
        ).astype(bf16)


def unpack(group, blocks):
    members, _, width = group.shape
    return pl.pallas_call(
        unpack_kernel,
        out_shape=(
            jax.ShapeDtypeStruct((blocks, members, width), bf16),
            jax.ShapeDtypeStruct((blocks // 2, 2, members), bf16),
        ),
        in_specs=[VECTOR],
        out_specs=(VECTOR, VECTOR),
        compiler_params=pltpu.CompilerParams(vmem_limit_bytes=8 * 2**20),
    )(group)


def exchange(pieces, axes):
    return lax.all_to_all(pieces, axes, 0, 0, tiled=True)


def local(grad_first, grad_second, master, first_moment, second_moment):
    inner, _, rows, width = grad_first.shape[2:]
    blocks = 2 * rows
    x = lax.axis_size("x")
    core = lax.axis_index("core")[None]
    grads = [g[0, 0].transpose(0, 2, 1, 3) for g in (grad_first, grad_second)]
    other = lax.ppermute(rows_to_send(core, *grads, x), "core", [(0, 1), (1, 0)])
    pair = add_own_rows(core, *grads, other)
    cross = exchange(pair.reshape(x * Z_NEAR, -1, width), ("x", "z_near"))
    cross = fold(cross, (inner // x * Z_FAR, blocks, width))
    last = exchange(cross, ("y_far", "y_near", "z_far"))
    state = [v.reshape(blocks, 1, width) for v in (master, first_moment, second_moment)]
    *updated, spread = update(last, *state, inner)
    codes, scales = unpack(exchange(spread, INNER), blocks)
    codes = codes.reshape(2, rows, inner, width).transpose(0, 2, 1, 3)
    return (
        *(v.reshape(master.shape) for v in updated),
        codes[:, :, None],
        scales.transpose(1, 2, 0)[:, :, None],
    )


def solution(mesh):
    inner, outer = mesh.devices.shape
    split = Mesh(
        mesh.devices.reshape(inner // 8, 4, 2, outer // 4, Z_NEAR, 2),
        INNER + OUTER,
    )
    return jax.shard_map(
        local,
        mesh=split,
        in_specs=(P(OUTER, INNER), P(OUTER, INNER)) + (P(None, INNER, OUTER),) * 3,
        out_specs=(P(None, INNER, OUTER),) * 3 + (P(None, None, OUTER),) * 2,
        check_vma=False,
    )
```

time: 76.3 us -> 70 us (0.917)
  blocking collectives: 24.2 us -> 60 us
  starting transfers between devices: 19.6 us -> 1.92 us
  waiting for transfers between devices: 19.8 us -> 2.46 us
  local copies, waits for them, and re-layouts: 6.59 us -> 0.03 us
  other arithmetic: 4.93 us -> 0 us
  Pallas kernels: 0 us -> 4.62 us
    all_to_all x2 -> x3, blocking collectives: 24.2 us -> 60 us  [exchange(): return lax.all_to_all(pieces, axes, 0, 0, tiled=True)]
    all_to_all x2 -> x0, waiting for transfers between devices: 19.8 us -> none  [the longest x1 11.9 us: exchange(): return lax.all_to_all(pieces, axes, 0, 0, tiled=True).astype(jnp.float32)]
    all_to_all x2 -> x0, starting transfers between devices: 19.6 us -> none  [the longest x1 15.3 us: exchange(): return lax.all_to_all(pieces, axes, 0, 0, tiled=True).astype(jnp.float32)]
    pallas_call x0 -> x5, Pallas kernels: none -> 4.62 us  [the longest x1 2.54 us: rows_to_send(): pl.pallas_call(send_kernel, out_shape=jax.ShapeDtypeStruct(shape, bf16),...]
    another operation x1 -> x0, other arithmetic: 3.73 us -> none  [local(): grads = jnp.stack([grad_first[0, 0], grad_second[0, 0]])]
    unnamed x12 -> x10, local copies, waits for them, and re-layouts: 3.09 us -> 0.03 us
    ppermute x0 -> x1, waiting for transfers between devices: none -> 2.46 us  [local(): lax.ppermute(rows_to_send(core, *grads, x), 'core', [(0, 1), (1, 0)])]
    ppermute x0 -> x1, starting transfers between devices: none -> 1.92 us  [local(): lax.ppermute(rows_to_send(core, *grads, x), 'core', [(0, 1), (1, 0)])]
  transfers between devices with their start and end apart: 2 -> 1, of which waited for: 2 -> 1; matrix products, arithmetic and copies ran while one was open for 2% -> 0% of each run, Pallas kernels for 0% -> 0%
where the time goes in v4:
time: 70 us; the launch traced here: 69.7 us
  blocking collectives  60 us (86%)
  Pallas kernels  4.62 us (7%)
  waiting for transfers between devices  2.46 us (4%)
  starting transfers between devices  1.92 us (3%)
  between operations  0.71 us (1%)
    all_to_all x3, blocking collectives, exchange(): return lax.all_to_all(pieces, axes, 0, 0, tiled=True)  60 us
    pallas_call x1, Pallas kernels, rows_to_send(): pl.pallas_call(send_kernel, out_shape=jax.ShapeDtypeStruct(shape, bf16),...  2.54 us
    ppermute x1, waiting for transfers between devices, local(): lax.ppermute(rows_to_send(core, *grads, x), 'core', [(0, 1), (1, 0)])  2.46 us
    ppermute x1, starting transfers between devices, local(): lax.ppermute(rows_to_send(core, *grads, x), 'core', [(0, 1), (1, 0)])  1.92 us
  transfers between devices with their start and end apart: 1, of which 1 were waited for; matrix products, arithmetic and copies ran while one was open for 0% of the time, Pallas kernels for 0%

profile of v4, /device:TPU:8, one launch (start us, length us, event | category | flops | bytes accessed | tf_op | source)
XLA Modules:
  0.0 69.7 jit_solution(2025436872800436378)
XLA Ops:
  0.6 0.0 copy-start
  0.6 0.0 copy-start.1
  0.7 2.5 %shard_map.92 = bf16[4,2,8,48,128]{4,3,2,1,0:T(8,128)(2,1)} custom-call(s32[1]{0:T(128)} %bitcast.core_ref, bf16[32,6,16,128]{3,2,1,0:T(8,128)(2,1)} %bitcast.28, bf16[32,6,16,128]{3,2,1,0:T(8,128)(2,1)} %bitcast.30), custom_call_target="tpu_custom_call" | custom-call | tf_op jit(solution)/shard_map/pallas_call | solution.py:102
  3.2 1.9 %collective-permute-start = (bf16[4,2,8,48,128]{4,3,2,1,0:T(8,128)(2,1)}, bf16[4,2,8,48,128]{4,3,2,1,0:T(8,128)(2,1)S(1)}, u32[]{:S(2)}, u32[]{:S(2)}) collective-permute-start(bf16[4,2,8,48,128]{4,3,2,1,0:T(8,128)(2,1)} %shard_map.92), channel_id=1, source_target_pairs={{0,1},{1,0},{2,3},{3,2},{4,5},{5,4},{6,7},{7,6},{8,9},{9,8},{10,11... | collective-permute-start | bytes 2359304 | tf_op jit(solution)/shard_map/ppermute | solution.py:233
  5.1 2.5 %collective-permute-done.other_ref = bf16[4,2,8,48,128]{4,3,2,1,0:T(8,128)(2,1)S(1)} collective-permute-done((bf16[4,2,8,48,128]{4,3,2,1,0:T(8,128)(2,1)}, bf16[4,2,8,48,128]{4,3,2,1,0:T(8,128)(2,1)S(1)}, u32[]{:S(2)}, u32[]{:S(2)}) %collective-permute-start) | collective-permute-done | bytes 786464 | tf_op jit(solution)/shard_map/ppermute | solution.py:233
  7.6 0.0 copy-done
  7.6 0.0 copy-done.1
  7.6 0.4 shard_map.93
  8.0 19.1 %all_to_all.15.terms_ref = bf16[8,384,128]{2,1,0:T(8,128)(2,1)S(1)} all-to-all(bf16[8,384,128]{2,1,0:T(8,128)(2,1)S(1)} %bitcast.32), channel_id=1, replica_groups=mesh['x'=4,'y_far'=4,'y_near'=2,'z_far'=4,'z_near'=2,'core'=2] {'x','z_n..., dimensions={0} | all-to-all | bytes 1572864 | tf_op jit(solution)/shard_map/all_to_all | solution.py:224
  27.1 0.1 shard_map.94
  27.2 0.0 copy-start.2
  27.2 0.0 copy-start.3
  27.2 0.0 copy-start.4
  27.2 27.2 %all_to_all.16.terms_ref = bf16[32,12,128]{2,1,0:T(8,128)(2,1)S(1)} all-to-all(bf16[32,12,128]{2,1,0:T(8,128)(2,1)S(1)} %shard_map.94), channel_id=1, replica_groups=mesh['x'=4,'y_far'=4,'y_near'=2,'z_far'=4,'z_near'=2,'core'=2] {'y_far',..., dimensions={0} | all-to-all | bytes 196608 | tf_op jit(solution)/shard_map/all_to_all | solution.py:224
  54.4 0.0 copy-done.2
  54.4 0.0 copy-done.3
  54.4 0.0 copy-done.4
  54.4 0.7 shard_map.95
  55.1 13.7 %all_to_all.17.group_ref = bf16[32,16,128]{2,1,0:T(8,128)(2,1)S(1)} all-to-all(bf16[32,16,128]{2,1,0:T(8,128)(2,1)S(1)} %get-tuple-element.14), channel_id=1, replica_groups=mesh['x'=4,'y_far'=4,'y_near'=2,'z_far'=4,'z_near'=2,'core'=2] {'x','y_f..., dimensions={0} | all-to-all | bytes 262144 | tf_op jit(solution)/shard_map/all_to_all | solution.py:224
  68.8 0.9 %shard_map.96 = (bf16[12,32,128]{2,1,0:T(8,128)(2,1)}, bf16[6,2,32]{2,1,0:T(2,128)(2,1)}) custom-call(bf16[32,16,128]{2,1,0:T(8,128)(2,1)S(1)} %all_to_all.17.group_ref), custom_call_target="tpu_custom_call" | custom-call | tf_op jit(solution)/shard_map/pallas_call | solution.py:211
Async XLA Ops:
  0.6 7.0 %copy-start = (bf16[1,1,32,16,6,128]{5,3,4,2,1,0:T(8,128)(2,1)S(1)}, bf16[1,1,32,16,6,128]{5,3,4,2,1,0:T(8,128)(2,1)}, u32[]{:S(2)}) copy-start(bf16[1,1,32,16,6,128]{5,3,4,2,1,0:T(8,128)(2,1)} %param.5) | copy-start | bytes 2359300
  0.6 6.9 %copy-start.1 = (bf16[1,1,32,16,6,128]{5,3,4,2,1,0:T(8,128)(2,1)S(1)}, bf16[1,1,32,16,6,128]{5,3,4,2,1,0:T(8,128)(2,1)}, u32[]{:S(2)}) copy-start(bf16[1,1,32,16,6,128]{5,3,4,2,1,0:T(8,128)(2,1)} %param.6) | copy-start | bytes 2359300
  3.2 4.4 %collective-permute-start = (bf16[4,2,8,48,128]{4,3,2,1,0:T(8,128)(2,1)}, bf16[4,2,8,48,128]{4,3,2,1,0:T(8,128)(2,1)S(1)}, u32[]{:S(2)}, u32[]{:S(2)}) collective-permute-start(bf16[4,2,8,48,128]{4,3,2,1,0:T(8,128)(2,1)} %shard_map.92), channel_id=1, source_target_pairs={{0,1},{1,0},{2,3},{3,2},{4,5},{5,4},{6,7},{7,6},{8,9},{9,8},{10,11... | collective-permute-start | bytes 2359304 | tf_op jit(solution)/shard_map/ppermute | solution.py:233
  27.2 27.2 %copy-start.2 = (f32[2,1,1,6,128]{4,2,3,1,0:T(1,128)S(1)}, f32[2,1,1,6,128]{4,2,3,1,0:T(1,128)}, u32[]{:S(2)}) copy-start(f32[2,1,1,6,128]{4,2,3,1,0:T(1,128)} %param.7) | copy-start | bytes 18436
  27.2 27.2 %copy-start.3 = (f32[2,1,1,6,128]{4,2,3,1,0:T(1,128)S(1)}, f32[2,1,1,6,128]{4,2,3,1,0:T(1,128)}, u32[]{:S(2)}) copy-start(f32[2,1,1,6,128]{4,2,3,1,0:T(1,128)} %param.8) | copy-start | bytes 18436
  27.2 27.2 %copy-start.4 = (f32[2,1,1,6,128]{4,2,3,1,0:T(1,128)S(1)}, f32[2,1,1,6,128]{4,2,3,1,0:T(1,128)}, u32[]{:S(2)}) copy-start(f32[2,1,1,6,128]{4,2,3,1,0:T(1,128)} %param.9) | copy-start | bytes 18436

commit v5 on v4

--- a/solution.py
+++ b/solution.py
@@ -64,20 +64,17 @@
             )
 
 
-def send_kernel(core_ref, first_ref, second_ref, send_ref, first, second, sent, in_sem, out_sem):
+def send_kernel(core_ref, first_ref, second_ref, send_ref, first, second, sem):
     inner, rows, _, width = first_ref.shape
-    x, _, per_x, _, _ = send_ref.shape
-    loads = in_sem.shape[0]
+    per_x = send_ref.shape[2]
+    loads = sem.shape[0]
     span = inner // loads
 
     def load(i, k):
         part = pl.ds(i * span, span)
         return pltpu.make_async_copy(
-            (first_ref, second_ref)[k].at[part], (first, second)[k].at[part], in_sem.at[i, k]
+            (first_ref, second_ref)[k].at[part], (first, second)[k].at[part], sem.at[i, k]
         )
-
-    def store(i):
-        return pltpu.make_async_copy(sent.at[i], send_ref.at[i], out_sem.at[i])
 
     for i in range(loads):
         for k in range(2):
@@ -89,11 +86,7 @@
                 load(a // span, k).wait()
         values = sort_two(sort, first, second, a).astype(bf16)
         for place, piece in places(values, a, per_x, width):
-            sent[place] = piece
-        if (a + 2) % per_x == 0:
-            store(a // per_x).start()
-    for i in range(x):
-        store(i).wait()
+            send_ref[place] = piece
 
 
 def rows_to_send(core, first, second, x):
@@ -103,16 +96,14 @@
         send_kernel,
         out_shape=jax.ShapeDtypeStruct(shape, bf16),
         in_specs=[SCALAR, ANYWHERE, ANYWHERE],
-        out_specs=ANYWHERE,
+        out_specs=VECTOR,
         scratch_shapes=[
             pltpu.VMEM(first.shape, bf16),
             pltpu.VMEM(first.shape, bf16),
-            pltpu.VMEM(shape, bf16),
             pltpu.SemaphoreType.DMA((2, 2)),
-            pltpu.SemaphoreType.DMA((x,)),
         ],
-        compiler_params=pltpu.CompilerParams(vmem_limit_bytes=60 * 2**20),
-    )(core, first, second)
+        compiler_params=pltpu.CompilerParams(vmem_limit_bytes=16 * 2**20),
+    )(core, *(pltpu.with_memory_space_constraint(g, pltpu.HBM) for g in (first, second)))
 
 
 def add_kernel(core_ref, first_ref, second_ref, other_ref, out_ref):
@@ -188,17 +179,17 @@
     )(terms, master, first, second)
 
 
-def unpack_kernel(group_ref, codes_ref, scales_ref):
+def unpack_kernel(group_ref, codes_ref, scales_ref, wide):
     members, packed, width = group_ref.shape
     blocks = codes_ref.shape[0]
-    shape = ((blocks + 1) * members, members * packed)
-    to = lax.broadcasted_iota(jnp.int32, shape, 0)
-    at = lax.broadcasted_iota(jnp.int32, shape, 1)
-    sort = jnp.where(to == (at & (PACKED - 1)) * members + (at >> 4), 1.0, 0.0).astype(bf16)
-    rows = jnp.dot(sort, group_ref[...].reshape(members * packed, width), preferred_element_type=f32)
+    wide[...] = group_ref[...].astype(f32).reshape(members * packed, width)
+
+    def row(k):
+        return wide[pl.ds(k, members, stride=packed), :]
+
     for k in range(blocks):
-        codes_ref[k] = rows[k * members : (k + 1) * members].astype(bf16)
-    scales = rows[blocks * members :].T
+        codes_ref[k] = row(k).astype(bf16)
+    scales = row(blocks).T
     half = blocks // 2
     for j in range(half):
         scales_ref[j] = jnp.concatenate(
@@ -207,7 +198,7 @@
 
 
 def unpack(group, blocks):
-    members, _, width = group.shape
+    members, packed, width = group.shape
     return pl.pallas_call(
         unpack_kernel,
         out_shape=(
@@ -216,6 +207,7 @@
         ),
         in_specs=[VECTOR],
         out_specs=(VECTOR, VECTOR),
+        scratch_shapes=[pltpu.VMEM((members * packed, width), f32)],
         compiler_params=pltpu.CompilerParams(vmem_limit_bytes=8 * 2**20),
     )(group)
 

time: 70 us -> 68.8 us (0.983)
  Pallas kernels: 4.62 us -> 3.69 us
    pallas_call x1, Pallas kernels: 2.54 us -> 1.8 us  [rows_to_send(): pl.pallas_call(send_kernel, out_shape=jax.ShapeDtypeStruct(shape, bf16),...]
where the time goes in v5:
time: 68.8 us; the launch traced here: 68.6 us
  blocking collectives  60 us (87%)
  Pallas kernels  3.69 us (5%)
  waiting for transfers between devices  2.25 us (3%)
  starting transfers between devices  1.92 us (3%)
  between operations  0.71 us (1%)
    all_to_all x3, blocking collectives, exchange(): return lax.all_to_all(pieces, axes, 0, 0, tiled=True)  60 us
    ppermute x1, waiting for transfers between devices, local(): lax.ppermute(rows_to_send(core, *grads, x), 'core', [(0, 1), (1, 0)])  2.25 us
    ppermute x1, starting transfers between devices, local(): lax.ppermute(rows_to_send(core, *grads, x), 'core', [(0, 1), (1, 0)])  1.92 us
    pallas_call x1, Pallas kernels, rows_to_send(): pl.pallas_call(send_kernel, out_shape=jax.ShapeDtypeStruct(shape, bf16),...  1.8 us
  transfers between devices with their start and end apart: 1, of which 1 were waited for; matrix products, arithmetic and copies ran while one was open for 0% of the time, Pallas kernels for 0%

profile of v5, /device:TPU:8, one launch (start us, length us, event | category | flops | bytes accessed | tf_op | source)
XLA Modules:
  0.0 68.6 jit_solution(3868375668536772372)
XLA Ops:
  0.6 0.0 copy-start
  0.6 0.0 copy-start.1
  0.7 1.8 %shard_map.92 = bf16[4,2,8,48,128]{4,3,2,1,0:T(8,128)(2,1)S(1)} custom-call(s32[1]{0:T(128)} %bitcast.core_ref, bf16[32,6,16,128]{3,2,1,0:T(8,128)(2,1)} %bitcast.28, bf16[32,6,16,128]{3,2,1,0:T(8,128)(2,1)} %bitcast.30), custom_call_target="tpu_custom_call" | custom-call | tf_op jit(solution)/shard_map/pallas_call | solution.py:95
  2.5 1.9 %collective-permute-start = (bf16[4,2,8,48,128]{4,3,2,1,0:T(8,128)(2,1)S(1)}, bf16[4,2,8,48,128]{4,3,2,1,0:T(8,128)(2,1)S(1)}, u32[]{:S(2)}, u32[]{:S(2)}) collective-permute-start(bf16[4,2,8,48,128]{4,3,2,1,0:T(8,128)(2,1)S(1)} %shard_map.92), channel_id=1, source_target_pairs={{0,1},{1,0},{2,3},{3,2},{4,5},{5,4},{6,7},{7,6},{8,9},{9,8},{10,11... | collective-permute-start | bytes 2359304 | tf_op jit(solution)/shard_map/ppermute | solution.py:225
  4.4 2.3 %collective-permute-done.other_ref = bf16[4,2,8,48,128]{4,3,2,1,0:T(8,128)(2,1)S(1)} collective-permute-done((bf16[4,2,8,48,128]{4,3,2,1,0:T(8,128)(2,1)S(1)}, bf16[4,2,8,48,128]{4,3,2,1,0:T(8,128)(2,1)S(1)}, u32[]{:S(2)}, u32[]{:S(2)}) %collective-permute-start) | collective-permute-done | bytes 786464 | tf_op jit(solution)/shard_map/ppermute | solution.py:225
  6.6 0.0 copy-done
  6.6 0.0 copy-done.1
  6.7 0.4 shard_map.93
  7.0 19.1 %all_to_all.15.terms_ref = bf16[8,384,128]{2,1,0:T(8,128)(2,1)S(1)} all-to-all(bf16[8,384,128]{2,1,0:T(8,128)(2,1)S(1)} %bitcast.32), channel_id=1, replica_groups=mesh['x'=4,'y_far'=4,'y_near'=2,'z_far'=4,'z_near'=2,'core'=2] {'x','z_n..., dimensions={0} | all-to-all | bytes 1572864 | tf_op jit(solution)/shard_map/all_to_all | solution.py:216
  26.1 0.1 shard_map.94
  26.2 0.0 copy-start.2
  26.3 0.0 copy-start.3
  26.3 0.0 copy-start.4
  26.3 27.2 %all_to_all.16.terms_ref = bf16[32,12,128]{2,1,0:T(8,128)(2,1)S(1)} all-to-all(bf16[32,12,128]{2,1,0:T(8,128)(2,1)S(1)} %shard_map.94), channel_id=1, replica_groups=mesh['x'=4,'y_far'=4,'y_near'=2,'z_far'=4,'z_near'=2,'core'=2] {'y_far',..., dimensions={0} | all-to-all | bytes 196608 | tf_op jit(solution)/shard_map/all_to_all | solution.py:216
  53.5 0.0 copy-done.2
  53.5 0.0 copy-done.3
  53.5 0.0 copy-done.4
  53.5 0.7 shard_map.95
  54.1 13.7 %all_to_all.17.group_ref = bf16[32,16,128]{2,1,0:T(8,128)(2,1)S(1)} all-to-all(bf16[32,16,128]{2,1,0:T(8,128)(2,1)S(1)} %get-tuple-element.14), channel_id=1, replica_groups=mesh['x'=4,'y_far'=4,'y_near'=2,'z_far'=4,'z_near'=2,'core'=2] {'x','y_f..., dimensions={0} | all-to-all | bytes 262144 | tf_op jit(solution)/shard_map/all_to_all | solution.py:216
  67.9 0.7 %shard_map.96 = (bf16[12,32,128]{2,1,0:T(8,128)(2,1)}, bf16[6,2,32]{2,1,0:T(2,128)(2,1)}) custom-call(bf16[32,16,128]{2,1,0:T(8,128)(2,1)S(1)} %all_to_all.17.group_ref), custom_call_target="tpu_custom_call" | custom-call | tf_op jit(solution)/shard_map/pallas_call | solution.py:202
Async XLA Ops:
  0.6 6.0 %copy-start = (bf16[1,1,32,16,6,128]{5,3,4,2,1,0:T(8,128)(2,1)S(1)}, bf16[1,1,32,16,6,128]{5,3,4,2,1,0:T(8,128)(2,1)}, u32[]{:S(2)}) copy-start(bf16[1,1,32,16,6,128]{5,3,4,2,1,0:T(8,128)(2,1)} %param.5) | copy-start | bytes 2359300
  0.6 6.0 %copy-start.1 = (bf16[1,1,32,16,6,128]{5,3,4,2,1,0:T(8,128)(2,1)S(1)}, bf16[1,1,32,16,6,128]{5,3,4,2,1,0:T(8,128)(2,1)}, u32[]{:S(2)}) copy-start(bf16[1,1,32,16,6,128]{5,3,4,2,1,0:T(8,128)(2,1)} %param.6) | copy-start | bytes 2359300
  2.5 4.2 %collective-permute-start = (bf16[4,2,8,48,128]{4,3,2,1,0:T(8,128)(2,1)S(1)}, bf16[4,2,8,48,128]{4,3,2,1,0:T(8,128)(2,1)S(1)}, u32[]{:S(2)}, u32[]{:S(2)}) collective-permute-start(bf16[4,2,8,48,128]{4,3,2,1,0:T(8,128)(2,1)S(1)} %shard_map.92), channel_id=1, source_target_pairs={{0,1},{1,0},{2,3},{3,2},{4,5},{5,4},{6,7},{7,6},{8,9},{9,8},{10,11... | collective-permute-start | bytes 2359304 | tf_op jit(solution)/shard_map/ppermute | solution.py:225
  26.2 27.2 %copy-start.2 = (f32[2,1,1,6,128]{4,2,3,1,0:T(1,128)S(1)}, f32[2,1,1,6,128]{4,2,3,1,0:T(1,128)}, u32[]{:S(2)}) copy-start(f32[2,1,1,6,128]{4,2,3,1,0:T(1,128)} %param.7) | copy-start | bytes 18436
  26.3 27.2 %copy-start.3 = (f32[2,1,1,6,128]{4,2,3,1,0:T(1,128)S(1)}, f32[2,1,1,6,128]{4,2,3,1,0:T(1,128)}, u32[]{:S(2)}) copy-start(f32[2,1,1,6,128]{4,2,3,1,0:T(1,128)} %param.8) | copy-start | bytes 18436
  26.3 27.2 %copy-start.4 = (f32[2,1,1,6,128]{4,2,3,1,0:T(1,128)S(1)}, f32[2,1,1,6,128]{4,2,3,1,0:T(1,128)}, u32[]{:S(2)}) copy-start(f32[2,1,1,6,128]{4,2,3,1,0:T(1,128)} %param.9) | copy-start | bytes 18436

commit v6 on v5

--- a/solution.py
+++ b/solution.py
@@ -54,19 +54,19 @@
     return jnp.dot(sort, jnp.concatenate(columns, axis=1), preferred_element_type=f32)
 
 
-def places(values, a, per_x, width):
+def places(values, a, y_far, width):
     part = values.shape[0] // Z_NEAR
     for n in range(2):
         for z in range(Z_NEAR):
             yield (
-                ((a + n) // per_x, z, (a + n) % per_x),
+                (a // (2 * y_far), n, z, a // 2 % y_far),
                 values[z * part : (z + 1) * part, n * width : (n + 1) * width],
             )
 
 
 def send_kernel(core_ref, first_ref, second_ref, send_ref, first, second, sem):
     inner, rows, _, width = first_ref.shape
-    per_x = send_ref.shape[2]
+    y_far = send_ref.shape[3]
     loads = sem.shape[0]
     span = inner // loads
 
@@ -85,13 +85,13 @@
             for k in range(2):
                 load(a // span, k).wait()
         values = sort_two(sort, first, second, a).astype(bf16)
-        for place, piece in places(values, a, per_x, width):
+        for place, piece in places(values, a, y_far, width):
             send_ref[place] = piece
 
 
 def rows_to_send(core, first, second, x):
     inner, rows, outer, width = first.shape
-    shape = (x, Z_NEAR, inner // x, rows * outer // 2, width)
+    shape = (x, 2, Z_NEAR, inner // x // 2, rows * outer // 2, width)
     return pl.pallas_call(
         send_kernel,
         out_shape=jax.ShapeDtypeStruct(shape, bf16),
@@ -108,11 +108,11 @@
 
 def add_kernel(core_ref, first_ref, second_ref, other_ref, out_ref):
     inner, rows, _, width = first_ref.shape
-    per_x = other_ref.shape[2]
+    y_far = other_ref.shape[3]
     sort = sorter(core_ref[0], rows)
     for a in range(0, inner, 2):
         values = sort_two(sort, first_ref, second_ref, a)
-        for place, piece in places(values, a, per_x, width):
+        for place, piece in places(values, a, y_far, width):
             out_ref[place] = (piece + other_ref[place].astype(f32)).astype(bf16)
 
 
@@ -224,9 +224,9 @@
     grads = [g[0, 0].transpose(0, 2, 1, 3) for g in (grad_first, grad_second)]
     other = lax.ppermute(rows_to_send(core, *grads, x), "core", [(0, 1), (1, 0)])
     pair = add_own_rows(core, *grads, other)
-    cross = exchange(pair.reshape(x * Z_NEAR, -1, width), ("x", "z_near"))
-    cross = fold(cross, (inner // x * Z_FAR, blocks, width))
-    last = exchange(cross, ("y_far", "y_near", "z_far"))
+    near = exchange(pair.reshape(x * 2 * Z_NEAR, -1, width), ("x", "y_near", "z_near"))
+    near = fold(near, (inner // x // 2 * Z_FAR, blocks, width))
+    last = exchange(near, ("y_far", "z_far"))
     state = [v.reshape(blocks, 1, width) for v in (master, first_moment, second_moment)]
     *updated, spread = update(last, *state, inner)
     codes, scales = unpack(exchange(spread, INNER), blocks)

time: 68.8 us -> 69 us (level)
  no operation moved by 1% of the time
where the time goes in v6:
time: 69 us; the launch traced here: 68.8 us
  blocking collectives  60.2 us (87%)
  Pallas kernels  3.66 us (5%)
  waiting for transfers between devices  2.25 us (3%)
  starting transfers between devices  1.92 us (3%)
  between operations  0.71 us (1%)
    all_to_all x3, blocking collectives, exchange(): return lax.all_to_all(pieces, axes, 0, 0, tiled=True)  60.2 us
    ppermute x1, waiting for transfers between devices, local(): lax.ppermute(rows_to_send(core, *grads, x), 'core', [(0, 1), (1, 0)])  2.25 us
    ppermute x1, starting transfers between devices, local(): lax.ppermute(rows_to_send(core, *grads, x), 'core', [(0, 1), (1, 0)])  1.92 us
    pallas_call x1, Pallas kernels, rows_to_send(): pl.pallas_call(send_kernel, out_shape=jax.ShapeDtypeStruct(shape, bf16),...  1.8 us
  transfers between devices with their start and end apart: 1, of which 1 were waited for; matrix products, arithmetic and copies ran while one was open for 0% of the time, Pallas kernels for 0%

profile of v6, /device:TPU:8, one launch (start us, length us, event | category | flops | bytes accessed | tf_op | source)
XLA Modules:
  0.0 68.8 jit_solution(17920629063396207085)
XLA Ops:
  0.6 0.0 copy-start
  0.6 0.0 copy-start.1
  0.7 1.8 %shard_map.92 = bf16[4,2,2,4,48,128]{5,4,3,2,1,0:T(8,128)(2,1)S(1)} custom-call(s32[1]{0:T(128)} %bitcast.core_ref, bf16[32,6,16,128]{3,2,1,0:T(8,128)(2,1)} %bitcast.28, bf16[32,6,16,128]{3,2,1,0:T(8,128)(2,1)} %bitcast.30), custom_call_target="tpu_custom_call" | custom-call | tf_op jit(solution)/shard_map/pallas_call | solution.py:95
  2.5 1.9 %collective-permute-start = (bf16[4,2,2,4,48,128]{5,4,3,2,1,0:T(8,128)(2,1)S(1)}, bf16[4,2,2,4,48,128]{5,4,3,2,1,0:T(8,128)(2,1)S(1)}, u32[]{:S(2)}, u32[]{:S(2)}) collective-permute-start(bf16[4,2,2,4,48,128]{5,4,3,2,1,0:T(8,128)(2,1)S(1)} %shard_map.92), channel_id=1, source_target_pairs={{0,1},{1,0},{2,3},{3,2},{4,5},{5,4},{6,7},{7,6},{8,9},{9,8},{10,11... | collective-permute-start | bytes 2359304 | tf_op jit(solution)/shard_map/ppermute | solution.py:225
  4.4 2.3 %collective-permute-done.other_ref = bf16[4,2,2,4,48,128]{5,4,3,2,1,0:T(8,128)(2,1)S(1)} collective-permute-done((bf16[4,2,2,4,48,128]{5,4,3,2,1,0:T(8,128)(2,1)S(1)}, bf16[4,2,2,4,48,128]{5,4,3,2,1,0:T(8,128)(2,1)S(1)}, u32[]{:S(2)}, u32[]{:S(2)}) %collective-permute-start) | collective-permute-done | bytes 786464 | tf_op jit(solution)/shard_map/ppermute | solution.py:225
  6.6 0.0 copy-done
  6.6 0.0 copy-done.1
  6.7 0.4 shard_map.93
  7.0 21.2 %all_to_all.15.terms_ref = bf16[16,192,128]{2,1,0:T(8,128)(2,1)S(1)} all-to-all(bf16[16,192,128]{2,1,0:T(8,128)(2,1)S(1)} %bitcast.32), channel_id=1, replica_groups=mesh['x'=4,'y_far'=4,'y_near'=2,'z_far'=4,'z_near'=2,'core'=2] {'x','y_n..., dimensions={0} | all-to-all | bytes 1572864 | tf_op jit(solution)/shard_map/all_to_all | solution.py:216
  28.3 0.1 shard_map.94
  28.4 0.0 copy-start.2
  28.4 0.0 copy-start.3
  28.4 0.0 copy-start.4
  28.4 25.0 %all_to_all.16.terms_ref = bf16[16,12,128]{2,1,0:T(8,128)(2,1)S(1)} all-to-all(bf16[16,12,128]{2,1,0:T(8,128)(2,1)S(1)} %shard_map.94), channel_id=1, replica_groups=mesh['x'=4,'y_far'=4,'y_near'=2,'z_far'=4,'z_near'=2,'core'=2] {'y_far',..., dimensions={0} | all-to-all | bytes 98304 | tf_op jit(solution)/shard_map/all_to_all | solution.py:216
  53.5 0.0 copy-done.2
  53.5 0.0 copy-done.3
  53.5 0.0 copy-done.4
  53.5 0.6 shard_map.95
  54.1 13.9 %all_to_all.17.group_ref = bf16[32,16,128]{2,1,0:T(8,128)(2,1)S(1)} all-to-all(bf16[32,16,128]{2,1,0:T(8,128)(2,1)S(1)} %get-tuple-element.14), channel_id=1, replica_groups=mesh['x'=4,'y_far'=4,'y_near'=2,'z_far'=4,'z_near'=2,'core'=2] {'x','y_f..., dimensions={0} | all-to-all | bytes 262144 | tf_op jit(solution)/shard_map/all_to_all | solution.py:216
  68.0 0.7 %shard_map.96 = (bf16[12,32,128]{2,1,0:T(8,128)(2,1)}, bf16[6,2,32]{2,1,0:T(2,128)(2,1)}) custom-call(bf16[32,16,128]{2,1,0:T(8,128)(2,1)S(1)} %all_to_all.17.group_ref), custom_call_target="tpu_custom_call" | custom-call | tf_op jit(solution)/shard_map/pallas_call | solution.py:202
Async XLA Ops:
  0.6 6.0 %copy-start = (bf16[1,1,32,16,6,128]{5,3,4,2,1,0:T(8,128)(2,1)S(1)}, bf16[1,1,32,16,6,128]{5,3,4,2,1,0:T(8,128)(2,1)}, u32[]{:S(2)}) copy-start(bf16[1,1,32,16,6,128]{5,3,4,2,1,0:T(8,128)(2,1)} %param.5) | copy-start | bytes 2359300
  0.6 6.0 %copy-start.1 = (bf16[1,1,32,16,6,128]{5,3,4,2,1,0:T(8,128)(2,1)S(1)}, bf16[1,1,32,16,6,128]{5,3,4,2,1,0:T(8,128)(2,1)}, u32[]{:S(2)}) copy-start(bf16[1,1,32,16,6,128]{5,3,4,2,1,0:T(8,128)(2,1)} %param.6) | copy-start | bytes 2359300
  2.5 4.2 %collective-permute-start = (bf16[4,2,2,4,48,128]{5,4,3,2,1,0:T(8,128)(2,1)S(1)}, bf16[4,2,2,4,48,128]{5,4,3,2,1,0:T(8,128)(2,1)S(1)}, u32[]{:S(2)}, u32[]{:S(2)}) collective-permute-start(bf16[4,2,2,4,48,128]{5,4,3,2,1,0:T(8,128)(2,1)S(1)} %shard_map.92), channel_id=1, source_target_pairs={{0,1},{1,0},{2,3},{3,2},{4,5},{5,4},{6,7},{7,6},{8,9},{9,8},{10,11... | collective-permute-start | bytes 2359304 | tf_op jit(solution)/shard_map/ppermute | solution.py:225
  28.4 25.1 %copy-start.2 = (f32[2,1,1,6,128]{4,2,3,1,0:T(1,128)S(1)}, f32[2,1,1,6,128]{4,2,3,1,0:T(1,128)}, u32[]{:S(2)}) copy-start(f32[2,1,1,6,128]{4,2,3,1,0:T(1,128)} %param.7) | copy-start | bytes 18436
  28.4 25.1 %copy-start.3 = (f32[2,1,1,6,128]{4,2,3,1,0:T(1,128)S(1)}, f32[2,1,1,6,128]{4,2,3,1,0:T(1,128)}, u32[]{:S(2)}) copy-start(f32[2,1,1,6,128]{4,2,3,1,0:T(1,128)} %param.8) | copy-start | bytes 18436
  28.4 25.1 %copy-start.4 = (f32[2,1,1,6,128]{4,2,3,1,0:T(1,128)S(1)}, f32[2,1,1,6,128]{4,2,3,1,0:T(1,128)}, u32[]{:S(2)}) copy-start(f32[2,1,1,6,128]{4,2,3,1,0:T(1,128)} %param.9) | copy-start | bytes 18436

commit v7 on v6

--- a/solution.py
+++ b/solution.py
@@ -168,8 +168,8 @@
 
 
 def update(terms, master, first, second, members):
-    state = jax.ShapeDtypeStruct(master.shape, f32)
-    spread = jax.ShapeDtypeStruct((members, PACKED, master.shape[-1]), bf16)
+    state = pltpu.VMEM(master.shape, f32)
+    spread = pltpu.VMEM((members, PACKED, master.shape[-1]), bf16)
     return pl.pallas_call(
         update_kernel,
         out_shape=(state, state, state, spread),
@@ -179,7 +179,15 @@
     )(terms, master, first, second)
 
 
-def unpack_kernel(group_ref, codes_ref, scales_ref, wide):
+def finish_kernel(group_ref, *refs):
+    state_refs, (codes_ref, scales_ref), stored_refs = refs[:3], refs[3:5], refs[5:8]
+    wide, sem = refs[8:]
+    copies = [
+        pltpu.make_async_copy(new, stored, sem.at[i])
+        for i, (new, stored) in enumerate(zip(state_refs, stored_refs))
+    ]
+    for copy in copies:
+        copy.start()
     members, packed, width = group_ref.shape
     blocks = codes_ref.shape[0]
     wide[...] = group_ref[...].astype(f32).reshape(members * packed, width)
@@ -195,21 +203,31 @@
         scales_ref[j] = jnp.concatenate(
             [scales[k : k + 1] for k in (j, half + j)], axis=0
         ).astype(bf16)
-
-
-def unpack(group, blocks):
+    for copy in copies:
+        copy.wait()
+
+
+def finish(group, state):
     members, packed, width = group.shape
-    return pl.pallas_call(
-        unpack_kernel,
+    blocks = state[0].shape[0]
+    stored = jax.ShapeDtypeStruct(state[0].shape, f32)
+    return pl.pallas_call(
+        finish_kernel,
         out_shape=(
             jax.ShapeDtypeStruct((blocks, members, width), bf16),
             jax.ShapeDtypeStruct((blocks // 2, 2, members), bf16),
+            stored,
+            stored,
+            stored,
         ),
-        in_specs=[VECTOR],
-        out_specs=(VECTOR, VECTOR),
-        scratch_shapes=[pltpu.VMEM((members * packed, width), f32)],
+        in_specs=[VECTOR] * 4,
+        out_specs=(VECTOR, VECTOR, ANYWHERE, ANYWHERE, ANYWHERE),
+        scratch_shapes=[
+            pltpu.VMEM((members * packed, width), f32),
+            pltpu.SemaphoreType.DMA((3,)),
+        ],
         compiler_params=pltpu.CompilerParams(vmem_limit_bytes=8 * 2**20),
-    )(group)
+    )(group, *state)
 
 
 def exchange(pieces, axes):
@@ -229,7 +247,7 @@
     last = exchange(near, ("y_far", "z_far"))
     state = [v.reshape(blocks, 1, width) for v in (master, first_moment, second_moment)]
     *updated, spread = update(last, *state, inner)
-    codes, scales = unpack(exchange(spread, INNER), blocks)
+    codes, scales, *updated = finish(exchange(spread, INNER), updated)
     codes = codes.reshape(2, rows, inner, width).transpose(0, 2, 1, 3)
     return (
         *(v.reshape(master.shape) for v in updated),

time: 69 us -> 69.1 us (level)
  no operation moved by 1% of the time
where the time goes in v7:
time: 69.1 us; the launch traced here: 68.8 us
  blocking collectives  60.2 us (87%)
  Pallas kernels  3.72 us (5%)
  waiting for transfers between devices  2.25 us (3%)
  starting transfers between devices  1.92 us (3%)
  between operations  0.71 us (1%)
    all_to_all x3, blocking collectives, exchange(): return lax.all_to_all(pieces, axes, 0, 0, tiled=True)  60.2 us
    ppermute x1, waiting for transfers between devices, local(): lax.ppermute(rows_to_send(core, *grads, x), 'core', [(0, 1), (1, 0)])  2.25 us
    ppermute x1, starting transfers between devices, local(): lax.ppermute(rows_to_send(core, *grads, x), 'core', [(0, 1), (1, 0)])  1.92 us
    pallas_call x1, Pallas kernels, rows_to_send(): pl.pallas_call(send_kernel, out_shape=jax.ShapeDtypeStruct(shape, bf16),...  1.8 us
  transfers between devices with their start and end apart: 1, of which 1 were waited for; matrix products, arithmetic and copies ran while one was open for 0% of the time, Pallas kernels for 0%

profile of v7, /device:TPU:8, one launch (start us, length us, event | category | flops | bytes accessed | tf_op | source)
XLA Modules:
  0.0 68.8 jit_solution(13999134900596177622)
XLA Ops:
  0.6 0.0 copy-start
  0.6 0.0 copy-start.1
  0.7 1.8 %shard_map.92 = bf16[4,2,2,4,48,128]{5,4,3,2,1,0:T(8,128)(2,1)S(1)} custom-call(s32[1]{0:T(128)} %bitcast.core_ref, bf16[32,6,16,128]{3,2,1,0:T(8,128)(2,1)} %bitcast.28, bf16[32,6,16,128]{3,2,1,0:T(8,128)(2,1)} %bitcast.30), custom_call_target="tpu_custom_call" | custom-call | tf_op jit(solution)/shard_map/pallas_call | solution.py:95
  2.5 1.9 %collective-permute-start = (bf16[4,2,2,4,48,128]{5,4,3,2,1,0:T(8,128)(2,1)S(1)}, bf16[4,2,2,4,48,128]{5,4,3,2,1,0:T(8,128)(2,1)S(1)}, u32[]{:S(2)}, u32[]{:S(2)}) collective-permute-start(bf16[4,2,2,4,48,128]{5,4,3,2,1,0:T(8,128)(2,1)S(1)} %shard_map.92), channel_id=1, source_target_pairs={{0,1},{1,0},{2,3},{3,2},{4,5},{5,4},{6,7},{7,6},{8,9},{9,8},{10,11... | collective-permute-start | bytes 2359304 | tf_op jit(solution)/shard_map/ppermute | solution.py:243
  4.4 2.3 %collective-permute-done.other_ref = bf16[4,2,2,4,48,128]{5,4,3,2,1,0:T(8,128)(2,1)S(1)} collective-permute-done((bf16[4,2,2,4,48,128]{5,4,3,2,1,0:T(8,128)(2,1)S(1)}, bf16[4,2,2,4,48,128]{5,4,3,2,1,0:T(8,128)(2,1)S(1)}, u32[]{:S(2)}, u32[]{:S(2)}) %collective-permute-start) | collective-permute-done | bytes 786464 | tf_op jit(solution)/shard_map/ppermute | solution.py:243
  6.6 0.0 copy-done
  6.6 0.0 copy-done.1
  6.6 0.4 shard_map.93
  7.0 21.2 %all_to_all.15.terms_ref = bf16[16,192,128]{2,1,0:T(8,128)(2,1)S(1)} all-to-all(bf16[16,192,128]{2,1,0:T(8,128)(2,1)S(1)} %bitcast.32), channel_id=1, replica_groups=mesh['x'=4,'y_far'=4,'y_near'=2,'z_far'=4,'z_near'=2,'core'=2] {'x','y_n..., dimensions={0} | all-to-all | bytes 1572864 | tf_op jit(solution)/shard_map/all_to_all | solution.py:234
  28.3 0.1 shard_map.94
  28.4 0.0 copy-start.2
  28.4 0.0 copy-start.3
  28.4 0.0 copy-start.4
  28.4 25.1 %all_to_all.16.terms_ref = bf16[16,12,128]{2,1,0:T(8,128)(2,1)S(1)} all-to-all(bf16[16,12,128]{2,1,0:T(8,128)(2,1)S(1)} %shard_map.94), channel_id=1, replica_groups=mesh['x'=4,'y_far'=4,'y_near'=2,'z_far'=4,'z_near'=2,'core'=2] {'y_far',..., dimensions={0} | all-to-all | bytes 98304 | tf_op jit(solution)/shard_map/all_to_all | solution.py:234
  53.5 0.0 copy-done.2
  53.5 0.0 copy-done.3
  53.5 0.0 copy-done.4
  53.5 0.1 shard_map.95
  53.6 13.9 %all_to_all.17.group_ref = bf16[32,16,128]{2,1,0:T(8,128)(2,1)S(1)} all-to-all(bf16[32,16,128]{2,1,0:T(8,128)(2,1)S(1)} %get-tuple-element.14), channel_id=1, replica_groups=mesh['x'=4,'y_far'=4,'y_near'=2,'z_far'=4,'z_near'=2,'core'=2] {'x','y_f..., dimensions={0} | all-to-all | bytes 262144 | tf_op jit(solution)/shard_map/all_to_all | solution.py:234
  67.6 1.3 %shard_map.96 = (bf16[12,32,128]{2,1,0:T(8,128)(2,1)}, bf16[6,2,32]{2,1,0:T(2,128)(2,1)}, f32[12,1,128]{2,1,0:T(1,128)}, f32[12,1,128]{2,1,0:T(1,128)}, f32[12,1,128]{2,1,0:T(1,128)}) custom-call(bf16[32,16,128]{2,1,0:T(8,128)(2,1)S(1)} %all_to_all.17.group_ref, f32[12,1,128]{2,1,0:T(1,128)S(1)} %get-tuple-element.15.refs_0_, ...), custom_call_target="tpu_custom_call" | custom-call | tf_op jit(solution)/shard_map/pallas_call | solution.py:214
Async XLA Ops:
  0.6 6.0 %copy-start = (bf16[1,1,32,16,6,128]{5,3,4,2,1,0:T(8,128)(2,1)S(1)}, bf16[1,1,32,16,6,128]{5,3,4,2,1,0:T(8,128)(2,1)}, u32[]{:S(2)}) copy-start(bf16[1,1,32,16,6,128]{5,3,4,2,1,0:T(8,128)(2,1)} %param.5) | copy-start | bytes 2359300
  0.6 6.0 %copy-start.1 = (bf16[1,1,32,16,6,128]{5,3,4,2,1,0:T(8,128)(2,1)S(1)}, bf16[1,1,32,16,6,128]{5,3,4,2,1,0:T(8,128)(2,1)}, u32[]{:S(2)}) copy-start(bf16[1,1,32,16,6,128]{5,3,4,2,1,0:T(8,128)(2,1)} %param.6) | copy-start | bytes 2359300
  2.5 4.2 %collective-permute-start = (bf16[4,2,2,4,48,128]{5,4,3,2,1,0:T(8,128)(2,1)S(1)}, bf16[4,2,2,4,48,128]{5,4,3,2,1,0:T(8,128)(2,1)S(1)}, u32[]{:S(2)}, u32[]{:S(2)}) collective-permute-start(bf16[4,2,2,4,48,128]{5,4,3,2,1,0:T(8,128)(2,1)S(1)} %shard_map.92), channel_id=1, source_target_pairs={{0,1},{1,0},{2,3},{3,2},{4,5},{5,4},{6,7},{7,6},{8,9},{9,8},{10,11... | collective-permute-start | bytes 2359304 | tf_op jit(solution)/shard_map/ppermute | solution.py:243
  28.4 25.1 %copy-start.2 = (f32[2,1,1,6,128]{4,2,3,1,0:T(1,128)S(1)}, f32[2,1,1,6,128]{4,2,3,1,0:T(1,128)}, u32[]{:S(2)}) copy-start(f32[2,1,1,6,128]{4,2,3,1,0:T(1,128)} %param.7) | copy-start | bytes 18436
  28.4 25.1 %copy-start.3 = (f32[2,1,1,6,128]{4,2,3,1,0:T(1,128)S(1)}, f32[2,1,1,6,128]{4,2,3,1,0:T(1,128)}, u32[]{:S(2)}) copy-start(f32[2,1,1,6,128]{4,2,3,1,0:T(1,128)} %param.8) | copy-start | bytes 18436
  28.4 25.1 %copy-start.4 = (f32[2,1,1,6,128]{4,2,3,1,0:T(1,128)S(1)}, f32[2,1,1,6,128]{4,2,3,1,0:T(1,128)}, u32[]{:S(2)}) copy-start(f32[2,1,1,6,128]{4,2,3,1,0:T(1,128)} %param.9) | copy-start | bytes 18436

commit v8 on v5

--- a/solution.py
+++ b/solution.py
@@ -106,41 +106,52 @@
     )(core, *(pltpu.with_memory_space_constraint(g, pltpu.HBM) for g in (first, second)))
 
 
-def add_kernel(core_ref, first_ref, second_ref, other_ref, out_ref):
-    inner, rows, _, width = first_ref.shape
-    per_x = other_ref.shape[2]
+def add_kernel(core_ref, x_ref, first_ref, second_ref, other_ref, *out_refs):
+    rows, width = first_ref.shape[1], first_ref.shape[3]
+    x, near, per_x, part, _ = other_ref.shape
     sort = sorter(core_ref[0], rows)
-    for a in range(0, inner, 2):
-        values = sort_two(sort, first_ref, second_ref, a)
-        for place, piece in places(values, a, per_x, width):
-            out_ref[place] = (piece + other_ref[place].astype(f32)).astype(bf16)
-
-
-def add_own_rows(core, first, second, other):
+    for step, out_ref in enumerate(out_refs):
+        owner = lax.rem(x_ref[0] + step, x)
+        for y in range(0, per_x, 2):
+            values = sort_two(sort, first_ref, second_ref, owner * per_x + y)
+            for n in range(2):
+                for z in range(near):
+                    piece = values[z * part : (z + 1) * part, n * width : (n + 1) * width]
+                    out_ref[z, y + n] = (piece + other_ref[owner, z, y + n].astype(f32)).astype(bf16)
+
+
+def add_own_rows(core, my_x, first, second, other):
+    piece = jax.ShapeDtypeStruct(other.shape[1:], bf16)
     return pl.pallas_call(
         add_kernel,
-        out_shape=jax.ShapeDtypeStruct(other.shape, bf16),
-        in_specs=[SCALAR, VECTOR, VECTOR, VECTOR],
-        out_specs=VECTOR,
+        out_shape=(piece,) * other.shape[0],
+        in_specs=[SCALAR, SCALAR, VECTOR, VECTOR, VECTOR],
+        out_specs=(VECTOR,) * other.shape[0],
         compiler_params=pltpu.CompilerParams(vmem_limit_bytes=16 * 2**20),
-    )(core, first, second, other)
-
-
-def fold_kernel(terms_ref, out_ref):
-    total = jnp.sum(terms_ref[...].astype(f32), axis=0)
-    pieces, rows, _ = out_ref.shape
-    for i in range(pieces):
-        out_ref[i] = total[i * rows : (i + 1) * rows].astype(bf16)
-
-
-def fold(terms, shape):
+    )(core, my_x, first, second, other)
+
+
+def fold_kernel(*refs):
+    *term_refs, out_ref = refs
+    near, per_x, part, _ = term_refs[0].shape
+    rows = out_ref.shape[1]
+    pieces = part // rows
+    for z in range(near):
+        for y in range(per_x):
+            total = sum(ref[z, y].astype(f32) for ref in term_refs)
+            for far in range(pieces):
+                out_ref[(z * per_x + y) * pieces + far] = total[far * rows : (far + 1) * rows].astype(bf16)
+
+
+def fold(terms, rows):
+    near, per_x, part, width = terms[0].shape
     return pl.pallas_call(
         fold_kernel,
-        out_shape=jax.ShapeDtypeStruct(shape, bf16),
-        in_specs=[VECTOR],
+        out_shape=jax.ShapeDtypeStruct((near * per_x * part // rows, rows, width), bf16),
+        in_specs=[VECTOR] * len(terms),
         out_specs=VECTOR,
         compiler_params=pltpu.CompilerParams(vmem_limit_bytes=8 * 2**20),
-    )(terms)
+    )(*terms)
 
 
 def update_kernel(terms_ref, master_ref, first_ref, second_ref, *out_refs):
@@ -223,10 +234,12 @@
     core = lax.axis_index("core")[None]
     grads = [g[0, 0].transpose(0, 2, 1, 3) for g in (grad_first, grad_second)]
     other = lax.ppermute(rows_to_send(core, *grads, x), "core", [(0, 1), (1, 0)])
-    pair = add_own_rows(core, *grads, other)
-    cross = exchange(pair.reshape(x * Z_NEAR, -1, width), ("x", "z_near"))
-    cross = fold(cross, (inner // x * Z_FAR, blocks, width))
-    last = exchange(cross, ("y_far", "y_near", "z_far"))
+    mine, *others = add_own_rows(core, lax.axis_index("x")[None], *grads, other)
+    terms = [mine] + [
+        lax.ppermute(piece, "x", [(i, (i + step) % x) for i in range(x)])
+        for step, piece in enumerate(others, start=1)
+    ]
+    last = exchange(fold(terms, blocks), ("z_near", "y_far", "y_near", "z_far"))
     state = [v.reshape(blocks, 1, width) for v in (master, first_moment, second_moment)]
     *updated, spread = update(last, *state, inner)
     codes, scales = unpack(exchange(spread, INNER), blocks)

time: 68.8 us -> 72.1 us (1.048)
  blocking collectives: 60 us -> 46.4 us
  starting transfers between devices: 1.92 us -> 13.3 us
  waiting for transfers between devices: 2.25 us -> 7.58 us
    all_to_all x3 -> x2, blocking collectives: 60 us -> 46.4 us  [exchange(): return lax.all_to_all(pieces, axes, 0, 0, tiled=True)]
    ppermute x0 -> x3, starting transfers between devices: none -> 11.4 us  [local(): lax.ppermute(piece, 'x', [(i, (i + step) % x) for i in range(x)])]
    ppermute x0 -> x3, waiting for transfers between devices: none -> 5.33 us  [local(): lax.ppermute(piece, 'x', [(i, (i + step) % x) for i in range(x)])]
  transfers between devices with their start and end apart: 1 -> 4, of which waited for: 1 -> 3; matrix products, arithmetic and copies ran while one was open for 0% -> 0% of each run, Pallas kernels for 0% -> 0%
where the time goes in v8:
time: 72.1 us; the launch traced here: 71.8 us
  blocking collectives  46.4 us (64%)
  starting transfers between devices  13.3 us (18%)
  waiting for transfers between devices  7.58 us (11%)
  Pallas kernels  3.73 us (5%)
  between operations  0.74 us (1%)
    all_to_all x2, blocking collectives, exchange(): return lax.all_to_all(pieces, axes, 0, 0, tiled=True)  46.4 us
    ppermute x3, starting transfers between devices, local(): lax.ppermute(piece, 'x', [(i, (i + step) % x) for i in range(x)])  11.4 us
    ppermute x3, waiting for transfers between devices, local(): lax.ppermute(piece, 'x', [(i, (i + step) % x) for i in range(x)])  5.33 us
    ppermute x1, waiting for transfers between devices, local(): lax.ppermute(rows_to_send(core, *grads, x), 'core', [(0, 1), (1, 0)])  2.25 us
    ppermute x1, starting transfers between devices, local(): lax.ppermute(rows_to_send(core, *grads, x), 'core', [(0, 1), (1, 0)])  1.92 us
    pallas_call x1, Pallas kernels, rows_to_send(): pl.pallas_call(send_kernel, out_shape=jax.ShapeDtypeStruct(shape, bf16),...  1.8 us
  transfers between devices with their start and end apart: 4, of which 3 were waited for; matrix products, arithmetic and copies ran while one was open for 0% of the time, Pallas kernels for 0%

profile of v8, /device:TPU:8, one launch (start us, length us, event | category | flops | bytes accessed | tf_op | source)
XLA Modules:
  0.0 71.8 jit_solution(10949355893514585729)
XLA Ops:
  0.6 0.0 copy-start
  0.6 0.0 copy-start.1
  0.7 1.8 %shard_map.92 = bf16[4,2,8,48,128]{4,3,2,1,0:T(8,128)(2,1)S(1)} custom-call(s32[1]{0:T(128)} %bitcast.core_ref, bf16[32,6,16,128]{3,2,1,0:T(8,128)(2,1)} %bitcast.28, bf16[32,6,16,128]{3,2,1,0:T(8,128)(2,1)} %bitcast.30), custom_call_target="tpu_custom_call" | custom-call | tf_op jit(solution)/shard_map/pallas_call | solution.py:95
  2.5 1.9 %collective-permute-start = (bf16[4,2,8,48,128]{4,3,2,1,0:T(8,128)(2,1)S(1)}, bf16[4,2,8,48,128]{4,3,2,1,0:T(8,128)(2,1)S(1)}, u32[]{:S(2)}, u32[]{:S(2)}) collective-permute-start(bf16[4,2,8,48,128]{4,3,2,1,0:T(8,128)(2,1)S(1)} %shard_map.92), channel_id=1, source_target_pairs={{0,1},{1,0},{2,3},{3,2},{4,5},{5,4},{6,7},{7,6},{8,9},{9,8},{10,11... | collective-permute-start | bytes 2359304 | tf_op jit(solution)/shard_map/ppermute | solution.py:236
  4.4 2.2 %collective-permute-done.other_ref = bf16[4,2,8,48,128]{4,3,2,1,0:T(8,128)(2,1)S(1)} collective-permute-done((bf16[4,2,8,48,128]{4,3,2,1,0:T(8,128)(2,1)S(1)}, bf16[4,2,8,48,128]{4,3,2,1,0:T(8,128)(2,1)S(1)}, u32[]{:S(2)}, u32[]{:S(2)}) %collective-permute-start) | collective-permute-done | bytes 786464 | tf_op jit(solution)/shard_map/ppermute | solution.py:236
  6.6 0.0 copy-done
  6.6 0.0 copy-done.1
  6.6 0.4 shard_map.93
  7.0 3.4 %collective-permute-start.1 = (bf16[2,8,48,128]{3,2,1,0:T(8,128)(2,1)S(1)}, bf16[2,8,48,128]{3,2,1,0:T(8,128)(2,1)S(1)}, u32[]{:S(2)}, u32[]{:S(2)}) collective-permute-start(bf16[2,8,48,128]{3,2,1,0:T(8,128)(2,1)S(1)} %get-tuple-element.16), channel_id=1, source_target_pairs={{0,128},{128,256},{256,384},{384,0},{1,129},{129,257},{257,385},{3... | collective-permute-start | bytes 589832 | tf_op jit(solution)/shard_map/ppermute | solution.py:239
  10.4 4.6 %collective-permute-start.2 = (bf16[2,8,48,128]{3,2,1,0:T(8,128)(2,1)S(1)}, bf16[2,8,48,128]{3,2,1,0:T(8,128)(2,1)S(1)}, u32[]{:S(2)}, u32[]{:S(2)}) collective-permute-start(bf16[2,8,48,128]{3,2,1,0:T(8,128)(2,1)S(1)} %get-tuple-element.17), channel_id=1, source_target_pairs={{0,256},{128,384},{256,0},{384,128},{1,257},{129,385},{257,1},{385... | collective-permute-start | bytes 589832 | tf_op jit(solution)/shard_map/ppermute | solution.py:239
  15.1 3.3 %collective-permute-start.3 = (bf16[2,8,48,128]{3,2,1,0:T(8,128)(2,1)S(1)}, bf16[2,8,48,128]{3,2,1,0:T(8,128)(2,1)S(1)}, u32[]{:S(2)}, u32[]{:S(2)}) collective-permute-start(bf16[2,8,48,128]{3,2,1,0:T(8,128)(2,1)S(1)} %get-tuple-element.18), channel_id=1, source_target_pairs={{0,384},{128,0},{256,128},{384,256},{1,385},{129,1},{257,129},{385... | collective-permute-start | bytes 589832 | tf_op jit(solution)/shard_map/ppermute | solution.py:239
  18.4 0.0 collective-permute-done.1.refs_1_
  18.5 3.8 %collective-permute-done.2.refs_2_ = bf16[2,8,48,128]{3,2,1,0:T(8,128)(2,1)S(1)} collective-permute-done((bf16[2,8,48,128]{3,2,1,0:T(8,128)(2,1)S(1)}, bf16[2,8,48,128]{3,2,1,0:T(8,128)(2,1)S(1)}, u32[]{:S(2)}, u32[]{:S(2)}) %collective-permute-start.2) | collective-permute-done | bytes 196640 | tf_op jit(solution)/shard_map/ppermute | solution.py:239
  22.3 1.5 %collective-permute-done.3.refs_3_ = bf16[2,8,48,128]{3,2,1,0:T(8,128)(2,1)S(1)} collective-permute-done((bf16[2,8,48,128]{3,2,1,0:T(8,128)(2,1)S(1)}, bf16[2,8,48,128]{3,2,1,0:T(8,128)(2,1)S(1)}, u32[]{:S(2)}, u32[]{:S(2)}) %collective-permute-start.3) | collective-permute-done | bytes 196640 | tf_op jit(solution)/shard_map/ppermute | solution.py:239
  23.8 0.1 shard_map.94
  23.9 0.0 copy-start.2
  23.9 0.0 copy-start.3
  23.9 0.0 copy-start.4
  24.0 29.5 %all_to_all.10.terms_ref = bf16[64,12,128]{2,1,0:T(8,128)(2,1)S(1)} all-to-all(bf16[64,12,128]{2,1,0:T(8,128)(2,1)S(1)} %shard_map.94), channel_id=1, replica_groups=mesh['x'=4,'y_far'=4,'y_near'=2,'z_far'=4,'z_near'=2,'core'=2] {'z_near'..., dimensions={0} | all-to-all | bytes 393216 | tf_op jit(solution)/shard_map/all_to_all | solution.py:227
  53.5 0.0 copy-done.2
  53.5 0.0 copy-done.3
  53.5 0.0 copy-done.4
  53.5 0.7 shard_map.95
  54.2 16.9 %all_to_all.11.group_ref = bf16[32,16,128]{2,1,0:T(8,128)(2,1)S(1)} all-to-all(bf16[32,16,128]{2,1,0:T(8,128)(2,1)S(1)} %get-tuple-element.22), channel_id=1, replica_groups=mesh['x'=4,'y_far'=4,'y_near'=2,'z_far'=4,'z_near'=2,'core'=2] {'x','y_f..., dimensions={0} | all-to-all | bytes 262144 | tf_op jit(solution)/shard_map/all_to_all | solution.py:227
  71.1 0.7 %shard_map.96 = (bf16[12,32,128]{2,1,0:T(8,128)(2,1)}, bf16[6,2,32]{2,1,0:T(2,128)(2,1)}) custom-call(bf16[32,16,128]{2,1,0:T(8,128)(2,1)S(1)} %all_to_all.11.group_ref), custom_call_target="tpu_custom_call" | custom-call | tf_op jit(solution)/shard_map/pallas_call | solution.py:213
Async XLA Ops:
  0.6 6.0 %copy-start = (bf16[1,1,32,16,6,128]{5,3,4,2,1,0:T(8,128)(2,1)S(1)}, bf16[1,1,32,16,6,128]{5,3,4,2,1,0:T(8,128)(2,1)}, u32[]{:S(2)}) copy-start(bf16[1,1,32,16,6,128]{5,3,4,2,1,0:T(8,128)(2,1)} %param.5) | copy-start | bytes 2359300
  0.6 6.0 %copy-start.1 = (bf16[1,1,32,16,6,128]{5,3,4,2,1,0:T(8,128)(2,1)S(1)}, bf16[1,1,32,16,6,128]{5,3,4,2,1,0:T(8,128)(2,1)}, u32[]{:S(2)}) copy-start(bf16[1,1,32,16,6,128]{5,3,4,2,1,0:T(8,128)(2,1)} %param.6) | copy-start | bytes 2359300
  2.5 4.2 %collective-permute-start = (bf16[4,2,8,48,128]{4,3,2,1,0:T(8,128)(2,1)S(1)}, bf16[4,2,8,48,128]{4,3,2,1,0:T(8,128)(2,1)S(1)}, u32[]{:S(2)}, u32[]{:S(2)}) collective-permute-start(bf16[4,2,8,48,128]{4,3,2,1,0:T(8,128)(2,1)S(1)} %shard_map.92), channel_id=1, source_target_pairs={{0,1},{1,0},{2,3},{3,2},{4,5},{5,4},{6,7},{7,6},{8,9},{9,8},{10,11... | collective-permute-start | bytes 2359304 | tf_op jit(solution)/shard_map/ppermute | solution.py:236
  7.0 11.4 %collective-permute-start.1 = (bf16[2,8,48,128]{3,2,1,0:T(8,128)(2,1)S(1)}, bf16[2,8,48,128]{3,2,1,0:T(8,128)(2,1)S(1)}, u32[]{:S(2)}, u32[]{:S(2)}) collective-permute-start(bf16[2,8,48,128]{3,2,1,0:T(8,128)(2,1)S(1)} %get-tuple-element.16), channel_id=1, source_target_pairs={{0,128},{128,256},{256,384},{384,0},{1,129},{129,257},{257,385},{3... | collective-permute-start | bytes 589832 | tf_op jit(solution)/shard_map/ppermute | solution.py:239
  10.4 11.8 %collective-permute-start.2 = (bf16[2,8,48,128]{3,2,1,0:T(8,128)(2,1)S(1)}, bf16[2,8,48,128]{3,2,1,0:T(8,128)(2,1)S(1)}, u32[]{:S(2)}, u32[]{:S(2)}) collective-permute-start(bf16[2,8,48,128]{3,2,1,0:T(8,128)(2,1)S(1)} %get-tuple-element.17), channel_id=1, source_target_pairs={{0,256},{128,384},{256,0},{384,128},{1,257},{129,385},{257,1},{385... | collective-permute-start | bytes 589832 | tf_op jit(solution)/shard_map/ppermute | solution.py:239
  15.1 8.7 %collective-permute-start.3 = (bf16[2,8,48,128]{3,2,1,0:T(8,128)(2,1)S(1)}, bf16[2,8,48,128]{3,2,1,0:T(8,128)(2,1)S(1)}, u32[]{:S(2)}, u32[]{:S(2)}) collective-permute-start(bf16[2,8,48,128]{3,2,1,0:T(8,128)(2,1)S(1)} %get-tuple-element.18), channel_id=1, source_target_pairs={{0,384},{128,0},{256,128},{384,256},{1,385},{129,1},{257,129},{385... | collective-permute-start | bytes 589832 | tf_op jit(solution)/shard_map/ppermute | solution.py:239
  23.9 29.6 %copy-start.2 = (f32[2,1,1,6,128]{4,2,3,1,0:T(1,128)S(1)}, f32[2,1,1,6,128]{4,2,3,1,0:T(1,128)}, u32[]{:S(2)}) copy-start(f32[2,1,1,6,128]{4,2,3,1,0:T(1,128)} %param.7) | copy-start | bytes 18436
  23.9 29.5 %copy-start.3 = (f32[2,1,1,6,128]{4,2,3,1,0:T(1,128)S(1)}, f32[2,1,1,6,128]{4,2,3,1,0:T(1,128)}, u32[]{:S(2)}) copy-start(f32[2,1,1,6,128]{4,2,3,1,0:T(1,128)} %param.8) | copy-start | bytes 18436
  23.9 29.5 %copy-start.4 = (f32[2,1,1,6,128]{4,2,3,1,0:T(1,128)S(1)}, f32[2,1,1,6,128]{4,2,3,1,0:T(1,128)}, u32[]{:S(2)}) copy-start(f32[2,1,1,6,128]{4,2,3,1,0:T(1,128)} %param.9) | copy-start | bytes 18436

commit v9 on v6

--- a/solution.py
+++ b/solution.py
@@ -67,23 +67,22 @@
 def send_kernel(core_ref, first_ref, second_ref, send_ref, first, second, sem):
     inner, rows, _, width = first_ref.shape
     y_far = send_ref.shape[3]
-    loads = sem.shape[0]
-    span = inner // loads
+    starts = (0, inner // 4 * 3)
 
     def load(i, k):
-        part = pl.ds(i * span, span)
+        part = pl.ds(starts[i], (starts + (inner,))[i + 1] - starts[i])
         return pltpu.make_async_copy(
             (first_ref, second_ref)[k].at[part], (first, second)[k].at[part], sem.at[i, k]
         )
 
-    for i in range(loads):
+    for i in range(len(starts)):
         for k in range(2):
             load(i, k).start()
     sort = sorter(1 - core_ref[0], rows)
     for a in range(0, inner, 2):
-        if a % span == 0:
+        if a in starts:
             for k in range(2):
-                load(a // span, k).wait()
+                load(starts.index(a), k).wait()
         values = sort_two(sort, first, second, a).astype(bf16)
         for place, piece in places(values, a, y_far, width):
             send_ref[place] = piece
@@ -94,36 +93,51 @@
     shape = (x, 2, Z_NEAR, inner // x // 2, rows * outer // 2, width)
     return pl.pallas_call(
         send_kernel,
-        out_shape=jax.ShapeDtypeStruct(shape, bf16),
-        in_specs=[SCALAR, ANYWHERE, ANYWHERE],
-        out_specs=VECTOR,
-        scratch_shapes=[
+        out_shape=(
+            jax.ShapeDtypeStruct(shape, bf16),
             pltpu.VMEM(first.shape, bf16),
             pltpu.VMEM(first.shape, bf16),
-            pltpu.SemaphoreType.DMA((2, 2)),
-        ],
+        ),
+        in_specs=[SCALAR, ANYWHERE, ANYWHERE],
+        out_specs=(VECTOR, VECTOR, VECTOR),
+        scratch_shapes=[pltpu.SemaphoreType.DMA((2, 2))],
         compiler_params=pltpu.CompilerParams(vmem_limit_bytes=16 * 2**20),
     )(core, *(pltpu.with_memory_space_constraint(g, pltpu.HBM) for g in (first, second)))
 
 
-def add_kernel(core_ref, first_ref, second_ref, other_ref, out_ref):
+def keep_kernel(core_ref, first_ref, second_ref, keep_ref):
     inner, rows, _, width = first_ref.shape
-    y_far = other_ref.shape[3]
+    y_far = keep_ref.shape[3]
     sort = sorter(core_ref[0], rows)
     for a in range(0, inner, 2):
-        values = sort_two(sort, first_ref, second_ref, a)
+        values = sort_two(sort, first_ref, second_ref, a).astype(bf16)
         for place, piece in places(values, a, y_far, width):
-            out_ref[place] = (piece + other_ref[place].astype(f32)).astype(bf16)
-
-
-def add_own_rows(core, first, second, other):
-    return pl.pallas_call(
-        add_kernel,
-        out_shape=jax.ShapeDtypeStruct(other.shape, bf16),
-        in_specs=[SCALAR, VECTOR, VECTOR, VECTOR],
+            keep_ref[place] = piece
+
+
+def rows_to_keep(core, first, second, shape):
+    return pl.pallas_call(
+        keep_kernel,
+        out_shape=pltpu.VMEM(shape, bf16),
+        in_specs=[SCALAR, VECTOR, VECTOR],
         out_specs=VECTOR,
         compiler_params=pltpu.CompilerParams(vmem_limit_bytes=16 * 2**20),
-    )(core, first, second, other)
+    )(core, first, second)
+
+
+def add_kernel(own_ref, other_ref, out_ref):
+    for i in range(own_ref.shape[0]):
+        out_ref[i] = (own_ref[i].astype(f32) + other_ref[i].astype(f32)).astype(bf16)
+
+
+def add(own, other):
+    return pl.pallas_call(
+        add_kernel,
+        out_shape=jax.ShapeDtypeStruct(own.shape, bf16),
+        in_specs=[VECTOR, VECTOR],
+        out_specs=VECTOR,
+        compiler_params=pltpu.CompilerParams(vmem_limit_bytes=8 * 2**20),
+    )(own, other)
 
 
 def fold_kernel(terms_ref, out_ref):
@@ -222,8 +236,9 @@
     x = lax.axis_size("x")
     core = lax.axis_index("core")[None]
     grads = [g[0, 0].transpose(0, 2, 1, 3) for g in (grad_first, grad_second)]
-    other = lax.ppermute(rows_to_send(core, *grads, x), "core", [(0, 1), (1, 0)])
-    pair = add_own_rows(core, *grads, other)
+    send, *grads = rows_to_send(core, *grads, x)
+    other = lax.ppermute(send, "core", [(0, 1), (1, 0)])
+    pair = add(rows_to_keep(core, *grads, send.shape), other)
     near = exchange(pair.reshape(x * 2 * Z_NEAR, -1, width), ("x", "y_near", "z_near"))
     near = fold(near, (inner // x // 2 * Z_FAR, blocks, width))
     last = exchange(near, ("y_far", "z_far"))

time: 69 us -> 68.8 us (level)
    pallas_call x2 -> x3, Pallas kernels: 2.17 us -> 2.35 us  [the longest x1 1.8 us: rows_to_send(): pl.pallas_call(send_kernel, out_shape=(jax.ShapeDtypeStruct(shape, bf16),...]
  transfers between devices with their start and end apart: 1 -> 1, of which waited for: 1 -> 1; matrix products, arithmetic and copies ran while one was open for 0% -> 0% of each run, Pallas kernels for 0% -> 1%
where the time goes in v9:
time: 68.8 us; the launch traced here: 68.5 us
  blocking collectives  60.2 us (88%)
  Pallas kernels  3.84 us (6%)
  starting transfers between devices  1.92 us (3%)
  waiting for transfers between devices  1.87 us (3%)
  between operations  0.69 us (1%)
    all_to_all x3, blocking collectives, exchange(): return lax.all_to_all(pieces, axes, 0, 0, tiled=True)  60.2 us
    ppermute x1, starting transfers between devices, local(): other = lax.ppermute(send, 'core', [(0, 1), (1, 0)])  1.92 us
    ppermute x1, waiting for transfers between devices, local(): other = lax.ppermute(send, 'core', [(0, 1), (1, 0)])  1.87 us
    pallas_call x1, Pallas kernels, rows_to_send(): pl.pallas_call(send_kernel, out_shape=(jax.ShapeDtypeStruct(shape, bf16),...  1.8 us
  transfers between devices with their start and end apart: 1, of which 1 were waited for; matrix products, arithmetic and copies ran while one was open for 0% of the time, Pallas kernels for 1%

profile of v9, /device:TPU:8, one launch (start us, length us, event | category | flops | bytes accessed | tf_op | source)
XLA Modules:
  0.0 68.5 jit_solution(10125585517662601265)
XLA Ops:
  0.6 1.8 %shard_map.92 = (bf16[4,2,2,4,48,128]{5,4,3,2,1,0:T(8,128)(2,1)S(1)}, bf16[32,6,16,128]{3,2,1,0:T(8,128)(2,1)S(1)}, bf16[32,6,16,128]{3,2,1,0:T(8,128)(2,1)S(1)}) custom-call(s32[1]{0:T(128)} %bitcast.core_ref, bf16[32,6,16,128]{3,2,1,0:T(8,128)(2,1)} %bitcast.32, bf16[32,6,16,128]{3,2,1,0:T(8,128)(2,1)} %bitcast.33), custom_call_target="tpu_custom_call" | custom-call | tf_op jit(solution)/shard_map/pallas_call | solution.py:94
  2.4 1.9 %collective-permute-start = (bf16[4,2,2,4,48,128]{5,4,3,2,1,0:T(8,128)(2,1)S(1)}, bf16[4,2,2,4,48,128]{5,4,3,2,1,0:T(8,128)(2,1)S(1)}, u32[]{:S(2)}, u32[]{:S(2)}) collective-permute-start(bf16[4,2,2,4,48,128]{5,4,3,2,1,0:T(8,128)(2,1)S(1)} %get-tuple-element.16), channel_id=1, source_target_pairs={{0,1},{1,0},{2,3},{3,2},{4,5},{5,4},{6,7},{7,6},{8,9},{9,8},{10,11... | collective-permute-start | bytes 2359304 | tf_op jit(solution)/shard_map/ppermute | solution.py:240
  4.4 0.4 shard_map.93.own_ref
  4.8 1.9 %collective-permute-done.other_ref = bf16[4,2,2,4,48,128]{5,4,3,2,1,0:T(8,128)(2,1)S(1)} collective-permute-done((bf16[4,2,2,4,48,128]{5,4,3,2,1,0:T(8,128)(2,1)S(1)}, bf16[4,2,2,4,48,128]{5,4,3,2,1,0:T(8,128)(2,1)S(1)}, u32[]{:S(2)}, u32[]{:S(2)}) %collective-permute-start) | collective-permute-done | bytes 786464 | tf_op jit(solution)/shard_map/ppermute | solution.py:240
  6.6 0.2 shard_map.94
  6.8 21.2 %all_to_all.15.terms_ref = bf16[16,192,128]{2,1,0:T(8,128)(2,1)S(1)} all-to-all(bf16[16,192,128]{2,1,0:T(8,128)(2,1)S(1)} %bitcast.28), channel_id=1, replica_groups=mesh['x'=4,'y_far'=4,'y_near'=2,'z_far'=4,'z_near'=2,'core'=2] {'x','y_n..., dimensions={0} | all-to-all | bytes 1572864 | tf_op jit(solution)/shard_map/all_to_all | solution.py:230
  28.1 0.1 shard_map.95
  28.2 0.0 copy-start
  28.2 0.0 copy-start.1
  28.2 0.0 copy-start.2
  28.2 25.0 %all_to_all.16.terms_ref = bf16[16,12,128]{2,1,0:T(8,128)(2,1)S(1)} all-to-all(bf16[16,12,128]{2,1,0:T(8,128)(2,1)S(1)} %shard_map.95), channel_id=1, replica_groups=mesh['x'=4,'y_far'=4,'y_near'=2,'z_far'=4,'z_near'=2,'core'=2] {'y_far',..., dimensions={0} | all-to-all | bytes 98304 | tf_op jit(solution)/shard_map/all_to_all | solution.py:230
  53.3 0.0 copy-done
  53.3 0.0 copy-done.1
  53.3 0.0 copy-done.2
  53.3 0.6 shard_map.96
  53.9 13.9 %all_to_all.17.group_ref = bf16[32,16,128]{2,1,0:T(8,128)(2,1)S(1)} all-to-all(bf16[32,16,128]{2,1,0:T(8,128)(2,1)S(1)} %get-tuple-element.20), channel_id=1, replica_groups=mesh['x'=4,'y_far'=4,'y_near'=2,'z_far'=4,'z_near'=2,'core'=2] {'x','y_f..., dimensions={0} | all-to-all | bytes 262144 | tf_op jit(solution)/shard_map/all_to_all | solution.py:230
  67.8 0.7 %shard_map.97 = (bf16[12,32,128]{2,1,0:T(8,128)(2,1)}, bf16[6,2,32]{2,1,0:T(2,128)(2,1)}) custom-call(bf16[32,16,128]{2,1,0:T(8,128)(2,1)S(1)} %all_to_all.17.group_ref), custom_call_target="tpu_custom_call" | custom-call | tf_op jit(solution)/shard_map/pallas_call | solution.py:216
Async XLA Ops:
  2.4 4.2 %collective-permute-start = (bf16[4,2,2,4,48,128]{5,4,3,2,1,0:T(8,128)(2,1)S(1)}, bf16[4,2,2,4,48,128]{5,4,3,2,1,0:T(8,128)(2,1)S(1)}, u32[]{:S(2)}, u32[]{:S(2)}) collective-permute-start(bf16[4,2,2,4,48,128]{5,4,3,2,1,0:T(8,128)(2,1)S(1)} %get-tuple-element.16), channel_id=1, source_target_pairs={{0,1},{1,0},{2,3},{3,2},{4,5},{5,4},{6,7},{7,6},{8,9},{9,8},{10,11... | collective-permute-start | bytes 2359304 | tf_op jit(solution)/shard_map/ppermute | solution.py:240
  28.2 25.1 %copy-start = (f32[2,1,1,6,128]{4,2,3,1,0:T(1,128)S(1)}, f32[2,1,1,6,128]{4,2,3,1,0:T(1,128)}, u32[]{:S(2)}) copy-start(f32[2,1,1,6,128]{4,2,3,1,0:T(1,128)} %param.7) | copy-start | bytes 18436
  28.2 25.1 %copy-start.1 = (f32[2,1,1,6,128]{4,2,3,1,0:T(1,128)S(1)}, f32[2,1,1,6,128]{4,2,3,1,0:T(1,128)}, u32[]{:S(2)}) copy-start(f32[2,1,1,6,128]{4,2,3,1,0:T(1,128)} %param.8) | copy-start | bytes 18436
  28.2 25.1 %copy-start.2 = (f32[2,1,1,6,128]{4,2,3,1,0:T(1,128)S(1)}, f32[2,1,1,6,128]{4,2,3,1,0:T(1,128)}, u32[]{:S(2)}) copy-start(f32[2,1,1,6,128]{4,2,3,1,0:T(1,128)} %param.9) | copy-start | bytes 18436

commit v10 on v9

--- a/solution.py
+++ b/solution.py
@@ -1,3 +1,5 @@
+import functools
+
 import jax
 import jax.numpy as jnp
 from jax import lax
@@ -59,7 +61,7 @@
     for n in range(2):
         for z in range(Z_NEAR):
             yield (
-                (a // (2 * y_far), n, z, a // 2 % y_far),
+                (n, z, a // (2 * y_far), a // 2 % y_far),
                 values[z * part : (z + 1) * part, n * width : (n + 1) * width],
             )
 
@@ -90,7 +92,7 @@
 
 def rows_to_send(core, first, second, x):
     inner, rows, outer, width = first.shape
-    shape = (x, 2, Z_NEAR, inner // x // 2, rows * outer // 2, width)
+    shape = (2, Z_NEAR, x, inner // x // 2, rows * outer // 2, width)
     return pl.pallas_call(
         send_kernel,
         out_shape=(
@@ -193,13 +195,16 @@
     )(terms, master, first, second)
 
 
-def unpack_kernel(group_ref, codes_ref, scales_ref, wide):
+def unpack_kernel(xs, group_ref, codes_ref, scales_ref, wide):
     members, packed, width = group_ref.shape
     blocks = codes_ref.shape[0]
     wide[...] = group_ref[...].astype(f32).reshape(members * packed, width)
 
     def row(k):
-        return wide[pl.ds(k, members, stride=packed), :]
+        return jnp.concatenate(
+            [wide[pl.ds(x * packed + k, members // xs, stride=xs * packed), :] for x in range(xs)],
+            axis=0,
+        )
 
     for k in range(blocks):
         codes_ref[k] = row(k).astype(bf16)
@@ -211,10 +216,10 @@
         ).astype(bf16)
 
 
-def unpack(group, blocks):
+def unpack(group, blocks, xs):
     members, packed, width = group.shape
     return pl.pallas_call(
-        unpack_kernel,
+        functools.partial(unpack_kernel, xs),
         out_shape=(
             jax.ShapeDtypeStruct((blocks, members, width), bf16),
             jax.ShapeDtypeStruct((blocks // 2, 2, members), bf16),
@@ -239,12 +244,12 @@
     send, *grads = rows_to_send(core, *grads, x)
     other = lax.ppermute(send, "core", [(0, 1), (1, 0)])
     pair = add(rows_to_keep(core, *grads, send.shape), other)
-    near = exchange(pair.reshape(x * 2 * Z_NEAR, -1, width), ("x", "y_near", "z_near"))
+    near = exchange(pair.reshape(x * 2 * Z_NEAR, -1, width), ("y_near", "z_near", "x"))
     near = fold(near, (inner // x // 2 * Z_FAR, blocks, width))
     last = exchange(near, ("y_far", "z_far"))
     state = [v.reshape(blocks, 1, width) for v in (master, first_moment, second_moment)]
     *updated, spread = update(last, *state, inner)
-    codes, scales = unpack(exchange(spread, INNER), blocks)
+    codes, scales = unpack(exchange(spread, ("y_far", "y_near", "x")), blocks, x)
     codes = codes.reshape(2, rows, inner, width).transpose(0, 2, 1, 3)
     return (
         *(v.reshape(master.shape) for v in updated),

time: 68.8 us -> 69 us (level)
  no operation moved by 1% of the time
where the time goes in v10:
time: 69 us; the launch traced here: 68.7 us
  blocking collectives  60.3 us (87%)
  Pallas kernels  3.9 us (6%)
  starting transfers between devices  1.92 us (3%)
  waiting for transfers between devices  1.87 us (3%)
    all_to_all x3, blocking collectives, exchange(): return lax.all_to_all(pieces, axes, 0, 0, tiled=True)  60.3 us
    ppermute x1, starting transfers between devices, local(): other = lax.ppermute(send, 'core', [(0, 1), (1, 0)])  1.92 us
    ppermute x1, waiting for transfers between devices, local(): other = lax.ppermute(send, 'core', [(0, 1), (1, 0)])  1.87 us
    pallas_call x1, Pallas kernels, rows_to_send(): pl.pallas_call(send_kernel, out_shape=(jax.ShapeDtypeStruct(shape, bf16),...  1.8 us
  transfers between devices with their start and end apart: 1, of which 1 were waited for; matrix products, arithmetic and copies ran while one was open for 0% of the time, Pallas kernels for 1%

profile of v10, /device:TPU:8, one launch (start us, length us, event | category | flops | bytes accessed | tf_op | source)
XLA Modules:
  0.0 68.7 jit_solution(2660860141265822658)
XLA Ops:
  0.6 1.8 %shard_map.92 = (bf16[2,2,4,4,48,128]{5,4,3,2,1,0:T(8,128)(2,1)S(1)}, bf16[32,6,16,128]{3,2,1,0:T(8,128)(2,1)S(1)}, bf16[32,6,16,128]{3,2,1,0:T(8,128)(2,1)S(1)}) custom-call(s32[1]{0:T(128)} %bitcast.core_ref, bf16[32,6,16,128]{3,2,1,0:T(8,128)(2,1)} %bitcast.32, bf16[32,6,16,128]{3,2,1,0:T(8,128)(2,1)} %bitcast.33), custom_call_target="tpu_custom_call" | custom-call | tf_op jit(solution)/shard_map/pallas_call | solution.py:96
  2.4 1.9 %collective-permute-start = (bf16[2,2,4,4,48,128]{5,4,3,2,1,0:T(8,128)(2,1)S(1)}, bf16[2,2,4,4,48,128]{5,4,3,2,1,0:T(8,128)(2,1)S(1)}, u32[]{:S(2)}, u32[]{:S(2)}) collective-permute-start(bf16[2,2,4,4,48,128]{5,4,3,2,1,0:T(8,128)(2,1)S(1)} %get-tuple-element.16), channel_id=1, source_target_pairs={{0,1},{1,0},{2,3},{3,2},{4,5},{5,4},{6,7},{7,6},{8,9},{9,8},{10,11... | collective-permute-start | bytes 2359304 | tf_op jit(solution)/shard_map/ppermute | solution.py:245
  4.4 0.4 shard_map.93.own_ref
  4.8 1.9 %collective-permute-done.other_ref = bf16[2,2,4,4,48,128]{5,4,3,2,1,0:T(8,128)(2,1)S(1)} collective-permute-done((bf16[2,2,4,4,48,128]{5,4,3,2,1,0:T(8,128)(2,1)S(1)}, bf16[2,2,4,4,48,128]{5,4,3,2,1,0:T(8,128)(2,1)S(1)}, u32[]{:S(2)}, u32[]{:S(2)}) %collective-permute-start) | collective-permute-done | bytes 786464 | tf_op jit(solution)/shard_map/ppermute | solution.py:245
  6.6 0.2 shard_map.94
  6.8 21.5 %all_to_all.15.terms_ref = bf16[16,192,128]{2,1,0:T(8,128)(2,1)S(1)} all-to-all(bf16[16,192,128]{2,1,0:T(8,128)(2,1)S(1)} %bitcast.28), channel_id=1, replica_groups=mesh['x'=4,'y_far'=4,'y_near'=2,'z_far'=4,'z_near'=2,'core'=2] {'y_near'..., dimensions={0} | all-to-all | bytes 1572864 | tf_op jit(solution)/shard_map/all_to_all | solution.py:235
  28.3 0.1 shard_map.95
  28.4 0.0 copy-start
  28.4 0.0 copy-start.1
  28.4 0.0 copy-start.2
  28.4 25.0 %all_to_all.16.terms_ref = bf16[16,12,128]{2,1,0:T(8,128)(2,1)S(1)} all-to-all(bf16[16,12,128]{2,1,0:T(8,128)(2,1)S(1)} %shard_map.95), channel_id=1, replica_groups=mesh['x'=4,'y_far'=4,'y_near'=2,'z_far'=4,'z_near'=2,'core'=2] {'y_far',..., dimensions={0} | all-to-all | bytes 98304 | tf_op jit(solution)/shard_map/all_to_all | solution.py:235
  53.5 0.0 copy-done
  53.5 0.0 copy-done.1
  53.5 0.0 copy-done.2
  53.5 0.6 shard_map.96
  54.2 13.8 %all_to_all.17.group_ref = bf16[32,16,128]{2,1,0:T(8,128)(2,1)S(1)} all-to-all(bf16[32,16,128]{2,1,0:T(8,128)(2,1)S(1)} %get-tuple-element.20), channel_id=1, replica_groups=mesh['x'=4,'y_far'=4,'y_near'=2,'z_far'=4,'z_near'=2,'core'=2] {'y_far',..., dimensions={0} | all-to-all | bytes 262144 | tf_op jit(solution)/shard_map/all_to_all | solution.py:235
  67.9 0.8 %shard_map.97 = (bf16[12,32,128]{2,1,0:T(8,128)(2,1)}, bf16[6,2,32]{2,1,0:T(2,128)(2,1)}) custom-call(bf16[32,16,128]{2,1,0:T(8,128)(2,1)S(1)} %all_to_all.17.group_ref), custom_call_target="tpu_custom_call" | custom-call | tf_op jit(solution)/shard_map/pallas_call | solution.py:221
Async XLA Ops:
  2.4 4.2 %collective-permute-start = (bf16[2,2,4,4,48,128]{5,4,3,2,1,0:T(8,128)(2,1)S(1)}, bf16[2,2,4,4,48,128]{5,4,3,2,1,0:T(8,128)(2,1)S(1)}, u32[]{:S(2)}, u32[]{:S(2)}) collective-permute-start(bf16[2,2,4,4,48,128]{5,4,3,2,1,0:T(8,128)(2,1)S(1)} %get-tuple-element.16), channel_id=1, source_target_pairs={{0,1},{1,0},{2,3},{3,2},{4,5},{5,4},{6,7},{7,6},{8,9},{9,8},{10,11... | collective-permute-start | bytes 2359304 | tf_op jit(solution)/shard_map/ppermute | solution.py:245
  28.4 25.1 %copy-start = (f32[2,1,1,6,128]{4,2,3,1,0:T(1,128)S(1)}, f32[2,1,1,6,128]{4,2,3,1,0:T(1,128)}, u32[]{:S(2)}) copy-start(f32[2,1,1,6,128]{4,2,3,1,0:T(1,128)} %param.7) | copy-start | bytes 18436
  28.4 25.1 %copy-start.1 = (f32[2,1,1,6,128]{4,2,3,1,0:T(1,128)S(1)}, f32[2,1,1,6,128]{4,2,3,1,0:T(1,128)}, u32[]{:S(2)}) copy-start(f32[2,1,1,6,128]{4,2,3,1,0:T(1,128)} %param.8) | copy-start | bytes 18436
  28.4 25.1 %copy-start.2 = (f32[2,1,1,6,128]{4,2,3,1,0:T(1,128)S(1)}, f32[2,1,1,6,128]{4,2,3,1,0:T(1,128)}, u32[]{:S(2)}) copy-start(f32[2,1,1,6,128]{4,2,3,1,0:T(1,128)} %param.9) | copy-start | bytes 18436

commit v11 on v9

--- a/solution.py
+++ b/solution.py
@@ -182,7 +182,7 @@
 
 
 def update(terms, master, first, second, members):
-    state = jax.ShapeDtypeStruct(master.shape, f32)
+    state = pltpu.VMEM(master.shape, f32)
     spread = jax.ShapeDtypeStruct((members, PACKED, master.shape[-1]), bf16)
     return pl.pallas_call(
         update_kernel,

time: 68.8 us -> 69.6 us (1.012)
  blocking collectives: 60.2 us -> 46.3 us
  waiting for transfers between devices: 1.87 us -> 9.87 us
  starting transfers between devices: 1.92 us -> 6.67 us
  local copies, waits for them, and re-layouts: 0.02 us -> 1.8 us
    all_to_all x3 -> x2, blocking collectives: 60.2 us -> 46.3 us  [exchange(): return lax.all_to_all(pieces, axes, 0, 0, tiled=True)]
    all_to_all x0 -> x1, waiting for transfers between devices: none -> 8 us  [exchange(): return lax.all_to_all(pieces, axes, 0, 0, tiled=True)]
    all_to_all x0 -> x1, starting transfers between devices: none -> 4.75 us  [exchange(): return lax.all_to_all(pieces, axes, 0, 0, tiled=True)]
    unnamed x6 -> x9, local copies, waits for them, and re-layouts: 0.02 us -> 1.8 us
  transfers between devices with their start and end apart: 1 -> 2, of which waited for: 1 -> 2; matrix products, arithmetic and copies ran while one was open for 0% -> 3% of each run, Pallas kernels for 1% -> 1%
where the time goes in v11:
time: 69.6 us; the launch traced here: 69.3 us
  blocking collectives  46.3 us (67%)
  waiting for transfers between devices  9.87 us (14%)
  starting transfers between devices  6.67 us (10%)
  Pallas kernels  4 us (6%)
  local copies, waits for them, and re-layouts  1.8 us (3%)
  between operations  0.7 us (1%)
    all_to_all x2, blocking collectives, exchange(): return lax.all_to_all(pieces, axes, 0, 0, tiled=True)  46.3 us
    all_to_all x1, waiting for transfers between devices, exchange(): return lax.all_to_all(pieces, axes, 0, 0, tiled=True)  8 us
    all_to_all x1, starting transfers between devices, exchange(): return lax.all_to_all(pieces, axes, 0, 0, tiled=True)  4.75 us
    ppermute x1, starting transfers between devices, local(): other = lax.ppermute(send, 'core', [(0, 1), (1, 0)])  1.92 us
    ppermute x1, waiting for transfers between devices, local(): other = lax.ppermute(send, 'core', [(0, 1), (1, 0)])  1.87 us
    pallas_call x1, Pallas kernels, rows_to_send(): pl.pallas_call(send_kernel, out_shape=(jax.ShapeDtypeStruct(shape, bf16),...  1.8 us
    unnamed x9, local copies, waits for them, and re-layouts  1.8 us
  transfers between devices with their start and end apart: 2, of which 2 were waited for; matrix products, arithmetic and copies ran while one was open for 3% of the time, Pallas kernels for 1%

profile of v11, /device:TPU:8, one launch (start us, length us, event | category | flops | bytes accessed | tf_op | source)
XLA Modules:
  0.0 69.3 jit_solution(13589767296383914259)
XLA Ops:
  0.6 1.8 %shard_map.92 = (bf16[4,2,2,4,48,128]{5,4,3,2,1,0:T(8,128)(2,1)S(1)}, bf16[32,6,16,128]{3,2,1,0:T(8,128)(2,1)S(1)}, bf16[32,6,16,128]{3,2,1,0:T(8,128)(2,1)S(1)}) custom-call(s32[1]{0:T(128)} %bitcast.core_ref, bf16[32,6,16,128]{3,2,1,0:T(8,128)(2,1)} %bitcast.35, bf16[32,6,16,128]{3,2,1,0:T(8,128)(2,1)} %bitcast.36), custom_call_target="tpu_custom_call" | custom-call | tf_op jit(solution)/shard_map/pallas_call | solution.py:94
  2.4 1.9 %collective-permute-start = (bf16[4,2,2,4,48,128]{5,4,3,2,1,0:T(8,128)(2,1)S(1)}, bf16[4,2,2,4,48,128]{5,4,3,2,1,0:T(8,128)(2,1)S(1)}, u32[]{:S(2)}, u32[]{:S(2)}) collective-permute-start(bf16[4,2,2,4,48,128]{5,4,3,2,1,0:T(8,128)(2,1)S(1)} %get-tuple-element.16), channel_id=1, source_target_pairs={{0,1},{1,0},{2,3},{3,2},{4,5},{5,4},{6,7},{7,6},{8,9},{9,8},{10,11... | collective-permute-start | bytes 2359304 | tf_op jit(solution)/shard_map/ppermute | solution.py:240
  4.4 0.4 shard_map.93.own_ref
  4.8 1.9 %collective-permute-done.other_ref = bf16[4,2,2,4,48,128]{5,4,3,2,1,0:T(8,128)(2,1)S(1)} collective-permute-done((bf16[4,2,2,4,48,128]{5,4,3,2,1,0:T(8,128)(2,1)S(1)}, bf16[4,2,2,4,48,128]{5,4,3,2,1,0:T(8,128)(2,1)S(1)}, u32[]{:S(2)}, u32[]{:S(2)}) %collective-permute-start) | collective-permute-done | bytes 786464 | tf_op jit(solution)/shard_map/ppermute | solution.py:240
  6.6 0.2 shard_map.94
  6.8 21.2 %all_to_all.15.terms_ref = bf16[16,192,128]{2,1,0:T(8,128)(2,1)S(1)} all-to-all(bf16[16,192,128]{2,1,0:T(8,128)(2,1)S(1)} %bitcast.31), channel_id=1, replica_groups=mesh['x'=4,'y_far'=4,'y_near'=2,'z_far'=4,'z_near'=2,'core'=2] {'x','y_n..., dimensions={0} | all-to-all | bytes 1572864 | tf_op jit(solution)/shard_map/all_to_all | solution.py:230
  28.1 0.1 shard_map.95
  28.2 0.0 copy-start
  28.2 0.0 copy-start.1
  28.2 0.0 copy-start.2
  28.2 25.0 %all_to_all.16.terms_ref = bf16[16,12,128]{2,1,0:T(8,128)(2,1)S(1)} all-to-all(bf16[16,12,128]{2,1,0:T(8,128)(2,1)S(1)} %shard_map.95), channel_id=1, replica_groups=mesh['x'=4,'y_far'=4,'y_near'=2,'z_far'=4,'z_near'=2,'core'=2] {'y_far',..., dimensions={0} | all-to-all | bytes 98304 | tf_op jit(solution)/shard_map/all_to_all | solution.py:230
  53.3 0.0 copy-done
  53.3 0.0 copy-done.1
  53.3 0.0 copy-done.2
  53.3 0.8 %shard_map.96 = (f32[12,1,128]{2,1,0:T(1,128)S(1)}, f32[12,1,128]{2,1,0:T(1,128)S(1)}, f32[12,1,128]{2,1,0:T(1,128)S(1)}, bf16[32,16,128]{2,1,0:T(8,128)(2,1)}) custom-call(bf16[16,12,128]{2,1,0:T(8,128)(2,1)S(1)} %all_to_all.16.terms_ref, f32[12,1,128]{2,1,0:T(1,128)S(1)} %bitcast.32, f32[12,1,128]{2,1,0:T(1,128)S(1)} %bitcast.33, f32[12,1,128]{2,1,0:T(1,128)S(1)} %bitcast.34), custom_call_target="tpu_custom_call" | custom-call | tf_op jit(solution)/shard_map/pallas_call | solution.py:187
  54.1 4.7 %all-to-all-start.2 = ((bf16[32,16,128]{2,1,0:T(8,128)(2,1)}), bf16[32,16,128]{2,1,0:T(8,128)(2,1)S(1)}, u32[]{:S(2)}, u32[]{:S(2)}) async-start(bf16[32,16,128]{2,1,0:T(8,128)(2,1)} %get-tuple-element.20), calls=%async_computation.2 | async-start | bytes 262144 | tf_op jit(solution)/shard_map/all_to_all | solution.py:230
  58.8 0.6 copy.13
  59.4 0.6 copy.14
  60.0 0.6 copy.15
  60.6 8.0 %all-to-all-done.2.group_ref = bf16[32,16,128]{2,1,0:T(8,128)(2,1)S(1)} async-done(((bf16[32,16,128]{2,1,0:T(8,128)(2,1)}), bf16[32,16,128]{2,1,0:T(8,128)(2,1)S(1)}, u32[]{:S(2)}, u32[]{:S(2)}) %all-to-all-start.2) | async-done | bytes 131104 | tf_op jit(solution)/shard_map/all_to_all | solution.py:230
  68.6 0.7 %shard_map.97 = (bf16[12,32,128]{2,1,0:T(8,128)(2,1)}, bf16[6,2,32]{2,1,0:T(2,128)(2,1)}) custom-call(bf16[32,16,128]{2,1,0:T(8,128)(2,1)S(1)} %all-to-all-done.2.group_ref), custom_call_target="tpu_custom_call" | custom-call | tf_op jit(solution)/shard_map/pallas_call | solution.py:216
Async XLA Ops:
  2.4 4.2 %collective-permute-start = (bf16[4,2,2,4,48,128]{5,4,3,2,1,0:T(8,128)(2,1)S(1)}, bf16[4,2,2,4,48,128]{5,4,3,2,1,0:T(8,128)(2,1)S(1)}, u32[]{:S(2)}, u32[]{:S(2)}) collective-permute-start(bf16[4,2,2,4,48,128]{5,4,3,2,1,0:T(8,128)(2,1)S(1)} %get-tuple-element.16), channel_id=1, source_target_pairs={{0,1},{1,0},{2,3},{3,2},{4,5},{5,4},{6,7},{7,6},{8,9},{9,8},{10,11... | collective-permute-start | bytes 2359304 | tf_op jit(solution)/shard_map/ppermute | solution.py:240
  28.2 25.1 %copy-start = (f32[2,1,1,6,128]{4,2,3,1,0:T(1,128)S(1)}, f32[2,1,1,6,128]{4,2,3,1,0:T(1,128)}, u32[]{:S(2)}) copy-start(f32[2,1,1,6,128]{4,2,3,1,0:T(1,128)} %param.7) | copy-start | bytes 18436
  28.2 25.1 %copy-start.1 = (f32[2,1,1,6,128]{4,2,3,1,0:T(1,128)S(1)}, f32[2,1,1,6,128]{4,2,3,1,0:T(1,128)}, u32[]{:S(2)}) copy-start(f32[2,1,1,6,128]{4,2,3,1,0:T(1,128)} %param.8) | copy-start | bytes 18436
  28.2 25.1 %copy-start.2 = (f32[2,1,1,6,128]{4,2,3,1,0:T(1,128)S(1)}, f32[2,1,1,6,128]{4,2,3,1,0:T(1,128)}, u32[]{:S(2)}) copy-start(f32[2,1,1,6,128]{4,2,3,1,0:T(1,128)} %param.9) | copy-start | bytes 18436
  54.1 14.5 %all-to-all-start.2 = ((bf16[32,16,128]{2,1,0:T(8,128)(2,1)}), bf16[32,16,128]{2,1,0:T(8,128)(2,1)S(1)}, u32[]{:S(2)}, u32[]{:S(2)}) async-start(bf16[32,16,128]{2,1,0:T(8,128)(2,1)} %get-tuple-element.20), calls=%async_computation.2 | async-start | bytes 262144 | tf_op jit(solution)/shard_map/all_to_all | solution.py:230

commit v12 on v9

--- a/solution.py
+++ b/solution.py
@@ -54,19 +54,19 @@
     return jnp.dot(sort, jnp.concatenate(columns, axis=1), preferred_element_type=f32)
 
 
-def places(values, a, y_far, width):
+def places(values, a, ys, width):
     part = values.shape[0] // Z_NEAR
     for n in range(2):
         for z in range(Z_NEAR):
             yield (
-                (a // (2 * y_far), n, z, a // 2 % y_far),
+                ((a + n) // ys, z, (a + n) % ys),
                 values[z * part : (z + 1) * part, n * width : (n + 1) * width],
             )
 
 
 def send_kernel(core_ref, first_ref, second_ref, send_ref, first, second, sem):
     inner, rows, _, width = first_ref.shape
-    y_far = send_ref.shape[3]
+    ys = send_ref.shape[2]
     starts = (0, inner // 4 * 3)
 
     def load(i, k):
@@ -84,13 +84,13 @@
             for k in range(2):
                 load(starts.index(a), k).wait()
         values = sort_two(sort, first, second, a).astype(bf16)
-        for place, piece in places(values, a, y_far, width):
+        for place, piece in places(values, a, ys, width):
             send_ref[place] = piece
 
 
 def rows_to_send(core, first, second, x):
     inner, rows, outer, width = first.shape
-    shape = (x, 2, Z_NEAR, inner // x // 2, rows * outer // 2, width)
+    shape = (x, Z_NEAR, inner // x, rows * outer // 2, width)
     return pl.pallas_call(
         send_kernel,
         out_shape=(
@@ -107,11 +107,11 @@
 
 def keep_kernel(core_ref, first_ref, second_ref, keep_ref):
     inner, rows, _, width = first_ref.shape
-    y_far = keep_ref.shape[3]
+    ys = keep_ref.shape[2]
     sort = sorter(core_ref[0], rows)
     for a in range(0, inner, 2):
         values = sort_two(sort, first_ref, second_ref, a).astype(bf16)
-        for place, piece in places(values, a, y_far, width):
+        for place, piece in places(values, a, ys, width):
             keep_ref[place] = piece
 
 
@@ -239,9 +239,9 @@
     send, *grads = rows_to_send(core, *grads, x)
     other = lax.ppermute(send, "core", [(0, 1), (1, 0)])
     pair = add(rows_to_keep(core, *grads, send.shape), other)
-    near = exchange(pair.reshape(x * 2 * Z_NEAR, -1, width), ("x", "y_near", "z_near"))
-    near = fold(near, (inner // x // 2 * Z_FAR, blocks, width))
-    last = exchange(near, ("y_far", "z_far"))
+    cross = exchange(pair.reshape(x * Z_NEAR, -1, width), ("x", "z_near"))
+    cross = fold(cross, (inner // x * Z_FAR, blocks, width))
+    last = exchange(cross, ("y_far", "y_near", "z_far"))
     state = [v.reshape(blocks, 1, width) for v in (master, first_moment, second_moment)]
     *updated, spread = update(last, *state, inner)
     codes, scales = unpack(exchange(spread, INNER), blocks)

time: 68.8 us -> 68.7 us (level)
  no operation moved by 1% of the time
where the time goes in v12:
time: 68.7 us; the launch traced here: 68.4 us
  blocking collectives  60 us (87%)
  Pallas kernels  3.87 us (6%)
  starting transfers between devices  1.92 us (3%)
  waiting for transfers between devices  1.87 us (3%)
  between operations  0.7 us (1%)
    all_to_all x3, blocking collectives, exchange(): return lax.all_to_all(pieces, axes, 0, 0, tiled=True)  60 us
    ppermute x1, starting transfers between devices, local(): other = lax.ppermute(send, 'core', [(0, 1), (1, 0)])  1.92 us
    ppermute x1, waiting for transfers between devices, local(): other = lax.ppermute(send, 'core', [(0, 1), (1, 0)])  1.87 us
    pallas_call x1, Pallas kernels, rows_to_send(): pl.pallas_call(send_kernel, out_shape=(jax.ShapeDtypeStruct(shape, bf16),...  1.8 us
  transfers between devices with their start and end apart: 1, of which 1 were waited for; matrix products, arithmetic and copies ran while one was open for 0% of the time, Pallas kernels for 1%

profile of v12, /device:TPU:8, one launch (start us, length us, event | category | flops | bytes accessed | tf_op | source)
XLA Modules:
  0.0 68.4 jit_solution(4551927250080148416)
XLA Ops:
  0.6 1.8 %shard_map.92 = (bf16[4,2,8,48,128]{4,3,2,1,0:T(8,128)(2,1)S(1)}, bf16[32,6,16,128]{3,2,1,0:T(8,128)(2,1)S(1)}, bf16[32,6,16,128]{3,2,1,0:T(8,128)(2,1)S(1)}) custom-call(s32[1]{0:T(128)} %bitcast.core_ref, bf16[32,6,16,128]{3,2,1,0:T(8,128)(2,1)} %bitcast.32, bf16[32,6,16,128]{3,2,1,0:T(8,128)(2,1)} %bitcast.33), custom_call_target="tpu_custom_call" | custom-call | tf_op jit(solution)/shard_map/pallas_call | solution.py:94
  2.4 1.9 %collective-permute-start = (bf16[4,2,8,48,128]{4,3,2,1,0:T(8,128)(2,1)S(1)}, bf16[4,2,8,48,128]{4,3,2,1,0:T(8,128)(2,1)S(1)}, u32[]{:S(2)}, u32[]{:S(2)}) collective-permute-start(bf16[4,2,8,48,128]{4,3,2,1,0:T(8,128)(2,1)S(1)} %get-tuple-element.16), channel_id=1, source_target_pairs={{0,1},{1,0},{2,3},{3,2},{4,5},{5,4},{6,7},{7,6},{8,9},{9,8},{10,11... | collective-permute-start | bytes 2359304 | tf_op jit(solution)/shard_map/ppermute | solution.py:240
  4.4 0.4 shard_map.93.own_ref
  4.8 1.9 %collective-permute-done.other_ref = bf16[4,2,8,48,128]{4,3,2,1,0:T(8,128)(2,1)S(1)} collective-permute-done((bf16[4,2,8,48,128]{4,3,2,1,0:T(8,128)(2,1)S(1)}, bf16[4,2,8,48,128]{4,3,2,1,0:T(8,128)(2,1)S(1)}, u32[]{:S(2)}, u32[]{:S(2)}) %collective-permute-start) | collective-permute-done | bytes 786464 | tf_op jit(solution)/shard_map/ppermute | solution.py:240
  6.6 0.2 shard_map.94
  6.8 19.1 %all_to_all.15.terms_ref = bf16[8,384,128]{2,1,0:T(8,128)(2,1)S(1)} all-to-all(bf16[8,384,128]{2,1,0:T(8,128)(2,1)S(1)} %bitcast.28), channel_id=1, replica_groups=mesh['x'=4,'y_far'=4,'y_near'=2,'z_far'=4,'z_near'=2,'core'=2] {'x','z_n..., dimensions={0} | all-to-all | bytes 1572864 | tf_op jit(solution)/shard_map/all_to_all | solution.py:230
  25.9 0.1 shard_map.95
  26.0 0.0 copy-start
  26.1 0.0 copy-start.1
  26.1 0.0 copy-start.2
  26.1 27.2 %all_to_all.16.terms_ref = bf16[32,12,128]{2,1,0:T(8,128)(2,1)S(1)} all-to-all(bf16[32,12,128]{2,1,0:T(8,128)(2,1)S(1)} %shard_map.95), channel_id=1, replica_groups=mesh['x'=4,'y_far'=4,'y_near'=2,'z_far'=4,'z_near'=2,'core'=2] {'y_far',..., dimensions={0} | all-to-all | bytes 196608 | tf_op jit(solution)/shard_map/all_to_all | solution.py:230
  53.2 0.0 copy-done
  53.2 0.0 copy-done.1
  53.3 0.0 copy-done.2
  53.3 0.7 shard_map.96
  53.9 13.7 %all_to_all.17.group_ref = bf16[32,16,128]{2,1,0:T(8,128)(2,1)S(1)} all-to-all(bf16[32,16,128]{2,1,0:T(8,128)(2,1)S(1)} %get-tuple-element.20), channel_id=1, replica_groups=mesh['x'=4,'y_far'=4,'y_near'=2,'z_far'=4,'z_near'=2,'core'=2] {'x','y_f..., dimensions={0} | all-to-all | bytes 262144 | tf_op jit(solution)/shard_map/all_to_all | solution.py:230
  67.7 0.7 %shard_map.97 = (bf16[12,32,128]{2,1,0:T(8,128)(2,1)}, bf16[6,2,32]{2,1,0:T(2,128)(2,1)}) custom-call(bf16[32,16,128]{2,1,0:T(8,128)(2,1)S(1)} %all_to_all.17.group_ref), custom_call_target="tpu_custom_call" | custom-call | tf_op jit(solution)/shard_map/pallas_call | solution.py:216
Async XLA Ops:
  2.4 4.2 %collective-permute-start = (bf16[4,2,8,48,128]{4,3,2,1,0:T(8,128)(2,1)S(1)}, bf16[4,2,8,48,128]{4,3,2,1,0:T(8,128)(2,1)S(1)}, u32[]{:S(2)}, u32[]{:S(2)}) collective-permute-start(bf16[4,2,8,48,128]{4,3,2,1,0:T(8,128)(2,1)S(1)} %get-tuple-element.16), channel_id=1, source_target_pairs={{0,1},{1,0},{2,3},{3,2},{4,5},{5,4},{6,7},{7,6},{8,9},{9,8},{10,11... | collective-permute-start | bytes 2359304 | tf_op jit(solution)/shard_map/ppermute | solution.py:240
  26.0 27.2 %copy-start = (f32[2,1,1,6,128]{4,2,3,1,0:T(1,128)S(1)}, f32[2,1,1,6,128]{4,2,3,1,0:T(1,128)}, u32[]{:S(2)}) copy-start(f32[2,1,1,6,128]{4,2,3,1,0:T(1,128)} %param.7) | copy-start | bytes 18436
  26.1 27.2 %copy-start.1 = (f32[2,1,1,6,128]{4,2,3,1,0:T(1,128)S(1)}, f32[2,1,1,6,128]{4,2,3,1,0:T(1,128)}, u32[]{:S(2)}) copy-start(f32[2,1,1,6,128]{4,2,3,1,0:T(1,128)} %param.8) | copy-start | bytes 18436
  26.1 27.2 %copy-start.2 = (f32[2,1,1,6,128]{4,2,3,1,0:T(1,128)S(1)}, f32[2,1,1,6,128]{4,2,3,1,0:T(1,128)}, u32[]{:S(2)}) copy-start(f32[2,1,1,6,128]{4,2,3,1,0:T(1,128)} %param.9) | copy-start | bytes 18436

commit v13 on v11

--- a/solution.py
+++ b/solution.py
@@ -183,7 +183,7 @@
 
 def update(terms, master, first, second, members):
     state = pltpu.VMEM(master.shape, f32)
-    spread = jax.ShapeDtypeStruct((members, PACKED, master.shape[-1]), bf16)
+    spread = pltpu.VMEM((members, PACKED, master.shape[-1]), bf16)
     return pl.pallas_call(
         update_kernel,
         out_shape=(state, state, state, spread),
@@ -193,7 +193,10 @@
     )(terms, master, first, second)
 
 
-def unpack_kernel(group_ref, codes_ref, scales_ref, wide):
+def finish_kernel(group_ref, *refs):
+    state_refs, (codes_ref, scales_ref), stored_refs, wide = refs[:3], refs[3:5], refs[5:8], refs[8]
+    for new_ref, stored_ref in zip(state_refs, stored_refs):
+        stored_ref[...] = new_ref[...]
     members, packed, width = group_ref.shape
     blocks = codes_ref.shape[0]
     wide[...] = group_ref[...].astype(f32).reshape(members * packed, width)
@@ -211,19 +214,24 @@
         ).astype(bf16)
 
 
-def unpack(group, blocks):
+def finish(group, state):
     members, packed, width = group.shape
-    return pl.pallas_call(
-        unpack_kernel,
+    blocks = state[0].shape[0]
+    stored = jax.ShapeDtypeStruct(state[0].shape, f32)
+    return pl.pallas_call(
+        finish_kernel,
         out_shape=(
             jax.ShapeDtypeStruct((blocks, members, width), bf16),
             jax.ShapeDtypeStruct((blocks // 2, 2, members), bf16),
+            stored,
+            stored,
+            stored,
         ),
-        in_specs=[VECTOR],
-        out_specs=(VECTOR, VECTOR),
+        in_specs=[VECTOR] * 4,
+        out_specs=(VECTOR,) * 5,
         scratch_shapes=[pltpu.VMEM((members * packed, width), f32)],
         compiler_params=pltpu.CompilerParams(vmem_limit_bytes=8 * 2**20),
-    )(group)
+    )(group, *state)
 
 
 def exchange(pieces, axes):
@@ -244,7 +252,7 @@
     last = exchange(near, ("y_far", "z_far"))
     state = [v.reshape(blocks, 1, width) for v in (master, first_moment, second_moment)]
     *updated, spread = update(last, *state, inner)
-    codes, scales = unpack(exchange(spread, INNER), blocks)
+    codes, scales, *updated = finish(exchange(spread, INNER), updated)
     codes = codes.reshape(2, rows, inner, width).transpose(0, 2, 1, 3)
     return (
         *(v.reshape(master.shape) for v in updated),

time: 69.6 us -> 68.3 us (0.981)
  blocking collectives: 46.3 us -> 60.2 us
  waiting for transfers between devices: 9.87 us -> 1.87 us
  starting transfers between devices: 6.67 us -> 1.92 us
  local copies, waits for them, and re-layouts: 1.8 us -> 0.02 us
    all_to_all x2 -> x3, blocking collectives: 46.3 us -> 60.2 us  [exchange(): return lax.all_to_all(pieces, axes, 0, 0, tiled=True)]
    all_to_all x1 -> x0, waiting for transfers between devices: 8 us -> none  [exchange(): return lax.all_to_all(pieces, axes, 0, 0, tiled=True)]
    all_to_all x1 -> x0, starting transfers between devices: 4.75 us -> none  [exchange(): return lax.all_to_all(pieces, axes, 0, 0, tiled=True)]
    unnamed x9 -> x6, local copies, waits for them, and re-layouts: 1.8 us -> 0.02 us
  transfers between devices with their start and end apart: 2 -> 1, of which waited for: 2 -> 1; matrix products, arithmetic and copies ran while one was open for 3% -> 0% of each run, Pallas kernels for 1% -> 1%
where the time goes in v13:
time: 68.3 us; the launch traced here: 68.1 us
  blocking collectives  60.2 us (88%)
  Pallas kernels  3.35 us (5%)
  starting transfers between devices  1.92 us (3%)
  waiting for transfers between devices  1.87 us (3%)
  between operations  0.7 us (1%)
    all_to_all x3, blocking collectives, exchange(): return lax.all_to_all(pieces, axes, 0, 0, tiled=True)  60.2 us
    ppermute x1, starting transfers between devices, local(): other = lax.ppermute(send, 'core', [(0, 1), (1, 0)])  1.92 us
    ppermute x1, waiting for transfers between devices, local(): other = lax.ppermute(send, 'core', [(0, 1), (1, 0)])  1.87 us
    pallas_call x1, Pallas kernels, rows_to_send(): pl.pallas_call(send_kernel, out_shape=(jax.ShapeDtypeStruct(shape, bf16),...  1.81 us
  transfers between devices with their start and end apart: 1, of which 1 were waited for; matrix products, arithmetic and copies ran while one was open for 0% of the time, Pallas kernels for 1%

profile of v13, /device:TPU:8, one launch (start us, length us, event | category | flops | bytes accessed | tf_op | source)
XLA Modules:
  0.0 68.1 jit_solution(18098170265113701985)
XLA Ops:
  0.6 1.8 %shard_map.92 = (bf16[4,2,2,4,48,128]{5,4,3,2,1,0:T(8,128)(2,1)S(1)}, bf16[32,6,16,128]{3,2,1,0:T(8,128)(2,1)S(1)}, bf16[32,6,16,128]{3,2,1,0:T(8,128)(2,1)S(1)}) custom-call(s32[1]{0:T(128)} %bitcast.core_ref, bf16[32,6,16,128]{3,2,1,0:T(8,128)(2,1)} %bitcast.32, bf16[32,6,16,128]{3,2,1,0:T(8,128)(2,1)} %bitcast.33), custom_call_target="tpu_custom_call" | custom-call | tf_op jit(solution)/shard_map/pallas_call | solution.py:94
  2.4 1.9 %collective-permute-start = (bf16[4,2,2,4,48,128]{5,4,3,2,1,0:T(8,128)(2,1)S(1)}, bf16[4,2,2,4,48,128]{5,4,3,2,1,0:T(8,128)(2,1)S(1)}, u32[]{:S(2)}, u32[]{:S(2)}) collective-permute-start(bf16[4,2,2,4,48,128]{5,4,3,2,1,0:T(8,128)(2,1)S(1)} %get-tuple-element.19), channel_id=1, source_target_pairs={{0,1},{1,0},{2,3},{3,2},{4,5},{5,4},{6,7},{7,6},{8,9},{9,8},{10,11... | collective-permute-start | bytes 2359304 | tf_op jit(solution)/shard_map/ppermute | solution.py:248
  4.4 0.4 shard_map.93.own_ref
  4.8 1.9 %collective-permute-done.other_ref = bf16[4,2,2,4,48,128]{5,4,3,2,1,0:T(8,128)(2,1)S(1)} collective-permute-done((bf16[4,2,2,4,48,128]{5,4,3,2,1,0:T(8,128)(2,1)S(1)}, bf16[4,2,2,4,48,128]{5,4,3,2,1,0:T(8,128)(2,1)S(1)}, u32[]{:S(2)}, u32[]{:S(2)}) %collective-permute-start) | collective-permute-done | bytes 786464 | tf_op jit(solution)/shard_map/ppermute | solution.py:248
  6.6 0.2 shard_map.94
  6.8 21.2 %all_to_all.15.terms_ref = bf16[16,192,128]{2,1,0:T(8,128)(2,1)S(1)} all-to-all(bf16[16,192,128]{2,1,0:T(8,128)(2,1)S(1)} %bitcast.28), channel_id=1, replica_groups=mesh['x'=4,'y_far'=4,'y_near'=2,'z_far'=4,'z_near'=2,'core'=2] {'x','y_n..., dimensions={0} | all-to-all | bytes 1572864 | tf_op jit(solution)/shard_map/all_to_all | solution.py:238
  28.1 0.1 shard_map.95
  28.2 0.0 copy-start
  28.2 0.0 copy-start.1
  28.2 0.0 copy-start.2
  28.2 25.0 %all_to_all.16.terms_ref = bf16[16,12,128]{2,1,0:T(8,128)(2,1)S(1)} all-to-all(bf16[16,12,128]{2,1,0:T(8,128)(2,1)S(1)} %shard_map.95), channel_id=1, replica_groups=mesh['x'=4,'y_far'=4,'y_near'=2,'z_far'=4,'z_near'=2,'core'=2] {'y_far',..., dimensions={0} | all-to-all | bytes 98304 | tf_op jit(solution)/shard_map/all_to_all | solution.py:238
  53.3 0.0 copy-done
  53.3 0.0 copy-done.1
  53.3 0.0 copy-done.2
  53.3 0.1 shard_map.96
  53.4 13.9 %all_to_all.17.group_ref = bf16[32,16,128]{2,1,0:T(8,128)(2,1)S(1)} all-to-all(bf16[32,16,128]{2,1,0:T(8,128)(2,1)S(1)} %get-tuple-element.20), channel_id=1, replica_groups=mesh['x'=4,'y_far'=4,'y_near'=2,'z_far'=4,'z_near'=2,'core'=2] {'x','y_f..., dimensions={0} | all-to-all | bytes 262144 | tf_op jit(solution)/shard_map/all_to_all | solution.py:238
  67.3 0.7 %shard_map.97 = (bf16[12,32,128]{2,1,0:T(8,128)(2,1)}, bf16[6,2,32]{2,1,0:T(2,128)(2,1)}, f32[12,1,128]{2,1,0:T(1,128)}, f32[12,1,128]{2,1,0:T(1,128)}, f32[12,1,128]{2,1,0:T(1,128)}) custom-call(bf16[32,16,128]{2,1,0:T(8,128)(2,1)S(1)} %all_to_all.17.group_ref, f32[12,1,128]{2,1,0:T(1,128)S(1)} %get-tuple-element.21.refs_0_, ...), custom_call_target="tpu_custom_call" | custom-call | tf_op jit(solution)/shard_map/pallas_call | solution.py:221
Async XLA Ops:
  2.4 4.2 %collective-permute-start = (bf16[4,2,2,4,48,128]{5,4,3,2,1,0:T(8,128)(2,1)S(1)}, bf16[4,2,2,4,48,128]{5,4,3,2,1,0:T(8,128)(2,1)S(1)}, u32[]{:S(2)}, u32[]{:S(2)}) collective-permute-start(bf16[4,2,2,4,48,128]{5,4,3,2,1,0:T(8,128)(2,1)S(1)} %get-tuple-element.19), channel_id=1, source_target_pairs={{0,1},{1,0},{2,3},{3,2},{4,5},{5,4},{6,7},{7,6},{8,9},{9,8},{10,11... | collective-permute-start | bytes 2359304 | tf_op jit(solution)/shard_map/ppermute | solution.py:248
  28.2 25.1 %copy-start = (f32[2,1,1,6,128]{4,2,3,1,0:T(1,128)S(1)}, f32[2,1,1,6,128]{4,2,3,1,0:T(1,128)}, u32[]{:S(2)}) copy-start(f32[2,1,1,6,128]{4,2,3,1,0:T(1,128)} %param.7) | copy-start | bytes 18436
  28.2 25.1 %copy-start.1 = (f32[2,1,1,6,128]{4,2,3,1,0:T(1,128)S(1)}, f32[2,1,1,6,128]{4,2,3,1,0:T(1,128)}, u32[]{:S(2)}) copy-start(f32[2,1,1,6,128]{4,2,3,1,0:T(1,128)} %param.8) | copy-start | bytes 18436
  28.2 25.1 %copy-start.2 = (f32[2,1,1,6,128]{4,2,3,1,0:T(1,128)S(1)}, f32[2,1,1,6,128]{4,2,3,1,0:T(1,128)}, u32[]{:S(2)}) copy-start(f32[2,1,1,6,128]{4,2,3,1,0:T(1,128)} %param.9) | copy-start | bytes 18436

commit v14 on v13

--- a/solution.py
+++ b/solution.py
@@ -54,19 +54,19 @@
     return jnp.dot(sort, jnp.concatenate(columns, axis=1), preferred_element_type=f32)
 
 
-def places(values, a, y_far, width):
+def places(values, a, ys, width):
     part = values.shape[0] // Z_NEAR
     for n in range(2):
         for z in range(Z_NEAR):
             yield (
-                (a // (2 * y_far), n, z, a // 2 % y_far),
+                ((a + n) // ys, z, (a + n) % ys),
                 values[z * part : (z + 1) * part, n * width : (n + 1) * width],
             )
 
 
 def send_kernel(core_ref, first_ref, second_ref, send_ref, first, second, sem):
     inner, rows, _, width = first_ref.shape
-    y_far = send_ref.shape[3]
+    ys = send_ref.shape[2]
     starts = (0, inner // 4 * 3)
 
     def load(i, k):
@@ -84,13 +84,13 @@
             for k in range(2):
                 load(starts.index(a), k).wait()
         values = sort_two(sort, first, second, a).astype(bf16)
-        for place, piece in places(values, a, y_far, width):
+        for place, piece in places(values, a, ys, width):
             send_ref[place] = piece
 
 
 def rows_to_send(core, first, second, x):
     inner, rows, outer, width = first.shape
-    shape = (x, 2, Z_NEAR, inner // x // 2, rows * outer // 2, width)
+    shape = (x, Z_NEAR, inner // x, rows * outer // 2, width)
     return pl.pallas_call(
         send_kernel,
         out_shape=(
@@ -107,11 +107,11 @@
 
 def keep_kernel(core_ref, first_ref, second_ref, keep_ref):
     inner, rows, _, width = first_ref.shape
-    y_far = keep_ref.shape[3]
+    ys = keep_ref.shape[2]
     sort = sorter(core_ref[0], rows)
     for a in range(0, inner, 2):
         values = sort_two(sort, first_ref, second_ref, a).astype(bf16)
-        for place, piece in places(values, a, y_far, width):
+        for place, piece in places(values, a, ys, width):
             keep_ref[place] = piece
 
 
@@ -247,9 +247,9 @@
     send, *grads = rows_to_send(core, *grads, x)
     other = lax.ppermute(send, "core", [(0, 1), (1, 0)])
     pair = add(rows_to_keep(core, *grads, send.shape), other)
-    near = exchange(pair.reshape(x * 2 * Z_NEAR, -1, width), ("x", "y_near", "z_near"))
-    near = fold(near, (inner // x // 2 * Z_FAR, blocks, width))
-    last = exchange(near, ("y_far", "z_far"))
+    cross = exchange(pair.reshape(x * Z_NEAR, -1, width), ("x", "z_near"))
+    cross = fold(cross, (inner // x * Z_FAR, blocks, width))
+    last = exchange(cross, ("y_far", "y_near", "z_far"))
     state = [v.reshape(blocks, 1, width) for v in (master, first_moment, second_moment)]
     *updated, spread = update(last, *state, inner)
     codes, scales, *updated = finish(exchange(spread, INNER), updated)

time: 68.3 us -> 68.2 us (level)
  no operation moved by 1% of the time
where the time goes in v14:
time: 68.2 us; the launch traced here: 67.9 us
  blocking collectives  60 us (88%)
  Pallas kernels  3.37 us (5%)
  starting transfers between devices  1.92 us (3%)
  waiting for transfers between devices  1.87 us (3%)
  between operations  0.7 us (1%)
    all_to_all x3, blocking collectives, exchange(): return lax.all_to_all(pieces, axes, 0, 0, tiled=True)  60 us
    ppermute x1, starting transfers between devices, local(): other = lax.ppermute(send, 'core', [(0, 1), (1, 0)])  1.92 us
    ppermute x1, waiting for transfers between devices, local(): other = lax.ppermute(send, 'core', [(0, 1), (1, 0)])  1.87 us
    pallas_call x1, Pallas kernels, rows_to_send(): pl.pallas_call(send_kernel, out_shape=(jax.ShapeDtypeStruct(shape, bf16),...  1.81 us
  transfers between devices with their start and end apart: 1, of which 1 were waited for; matrix products, arithmetic and copies ran while one was open for 0% of the time, Pallas kernels for 1%

profile of v14, /device:TPU:8, one launch (start us, length us, event | category | flops | bytes accessed | tf_op | source)
XLA Modules:
  0.0 67.9 jit_solution(64476700913371794)
XLA Ops:
  0.6 1.8 %shard_map.92 = (bf16[4,2,8,48,128]{4,3,2,1,0:T(8,128)(2,1)S(1)}, bf16[32,6,16,128]{3,2,1,0:T(8,128)(2,1)S(1)}, bf16[32,6,16,128]{3,2,1,0:T(8,128)(2,1)S(1)}) custom-call(s32[1]{0:T(128)} %bitcast.core_ref, bf16[32,6,16,128]{3,2,1,0:T(8,128)(2,1)} %bitcast.32, bf16[32,6,16,128]{3,2,1,0:T(8,128)(2,1)} %bitcast.33), custom_call_target="tpu_custom_call" | custom-call | tf_op jit(solution)/shard_map/pallas_call | solution.py:94
  2.4 1.9 %collective-permute-start = (bf16[4,2,8,48,128]{4,3,2,1,0:T(8,128)(2,1)S(1)}, bf16[4,2,8,48,128]{4,3,2,1,0:T(8,128)(2,1)S(1)}, u32[]{:S(2)}, u32[]{:S(2)}) collective-permute-start(bf16[4,2,8,48,128]{4,3,2,1,0:T(8,128)(2,1)S(1)} %get-tuple-element.19), channel_id=1, source_target_pairs={{0,1},{1,0},{2,3},{3,2},{4,5},{5,4},{6,7},{7,6},{8,9},{9,8},{10,11... | collective-permute-start | bytes 2359304 | tf_op jit(solution)/shard_map/ppermute | solution.py:248
  4.4 0.4 shard_map.93.own_ref
  4.8 1.9 %collective-permute-done.other_ref = bf16[4,2,8,48,128]{4,3,2,1,0:T(8,128)(2,1)S(1)} collective-permute-done((bf16[4,2,8,48,128]{4,3,2,1,0:T(8,128)(2,1)S(1)}, bf16[4,2,8,48,128]{4,3,2,1,0:T(8,128)(2,1)S(1)}, u32[]{:S(2)}, u32[]{:S(2)}) %collective-permute-start) | collective-permute-done | bytes 786464 | tf_op jit(solution)/shard_map/ppermute | solution.py:248
  6.6 0.2 shard_map.94
  6.8 19.1 %all_to_all.15.terms_ref = bf16[8,384,128]{2,1,0:T(8,128)(2,1)S(1)} all-to-all(bf16[8,384,128]{2,1,0:T(8,128)(2,1)S(1)} %bitcast.28), channel_id=1, replica_groups=mesh['x'=4,'y_far'=4,'y_near'=2,'z_far'=4,'z_near'=2,'core'=2] {'x','z_n..., dimensions={0} | all-to-all | bytes 1572864 | tf_op jit(solution)/shard_map/all_to_all | solution.py:238
  25.9 0.1 shard_map.95
  26.0 0.0 copy-start
  26.0 0.0 copy-start.1
  26.1 0.0 copy-start.2
  26.1 27.2 %all_to_all.16.terms_ref = bf16[32,12,128]{2,1,0:T(8,128)(2,1)S(1)} all-to-all(bf16[32,12,128]{2,1,0:T(8,128)(2,1)S(1)} %shard_map.95), channel_id=1, replica_groups=mesh['x'=4,'y_far'=4,'y_near'=2,'z_far'=4,'z_near'=2,'core'=2] {'y_far',..., dimensions={0} | all-to-all | bytes 196608 | tf_op jit(solution)/shard_map/all_to_all | solution.py:238
  53.2 0.0 copy-done
  53.2 0.0 copy-done.1
  53.3 0.0 copy-done.2
  53.3 0.2 shard_map.96
  53.4 13.8 %all_to_all.17.group_ref = bf16[32,16,128]{2,1,0:T(8,128)(2,1)S(1)} all-to-all(bf16[32,16,128]{2,1,0:T(8,128)(2,1)S(1)} %get-tuple-element.20), channel_id=1, replica_groups=mesh['x'=4,'y_far'=4,'y_near'=2,'z_far'=4,'z_near'=2,'core'=2] {'x','y_f..., dimensions={0} | all-to-all | bytes 262144 | tf_op jit(solution)/shard_map/all_to_all | solution.py:238
  67.2 0.7 %shard_map.97 = (bf16[12,32,128]{2,1,0:T(8,128)(2,1)}, bf16[6,2,32]{2,1,0:T(2,128)(2,1)}, f32[12,1,128]{2,1,0:T(1,128)}, f32[12,1,128]{2,1,0:T(1,128)}, f32[12,1,128]{2,1,0:T(1,128)}) custom-call(bf16[32,16,128]{2,1,0:T(8,128)(2,1)S(1)} %all_to_all.17.group_ref, f32[12,1,128]{2,1,0:T(1,128)S(1)} %get-tuple-element.21.refs_0_, ...), custom_call_target="tpu_custom_call" | custom-call | tf_op jit(solution)/shard_map/pallas_call | solution.py:221
Async XLA Ops:
  2.4 4.2 %collective-permute-start = (bf16[4,2,8,48,128]{4,3,2,1,0:T(8,128)(2,1)S(1)}, bf16[4,2,8,48,128]{4,3,2,1,0:T(8,128)(2,1)S(1)}, u32[]{:S(2)}, u32[]{:S(2)}) collective-permute-start(bf16[4,2,8,48,128]{4,3,2,1,0:T(8,128)(2,1)S(1)} %get-tuple-element.19), channel_id=1, source_target_pairs={{0,1},{1,0},{2,3},{3,2},{4,5},{5,4},{6,7},{7,6},{8,9},{9,8},{10,11... | collective-permute-start | bytes 2359304 | tf_op jit(solution)/shard_map/ppermute | solution.py:248
  26.0 27.2 %copy-start = (f32[2,1,1,6,128]{4,2,3,1,0:T(1,128)S(1)}, f32[2,1,1,6,128]{4,2,3,1,0:T(1,128)}, u32[]{:S(2)}) copy-start(f32[2,1,1,6,128]{4,2,3,1,0:T(1,128)} %param.7) | copy-start | bytes 18436
  26.0 27.2 %copy-start.1 = (f32[2,1,1,6,128]{4,2,3,1,0:T(1,128)S(1)}, f32[2,1,1,6,128]{4,2,3,1,0:T(1,128)}, u32[]{:S(2)}) copy-start(f32[2,1,1,6,128]{4,2,3,1,0:T(1,128)} %param.8) | copy-start | bytes 18436
  26.1 27.2 %copy-start.2 = (f32[2,1,1,6,128]{4,2,3,1,0:T(1,128)S(1)}, f32[2,1,1,6,128]{4,2,3,1,0:T(1,128)}, u32[]{:S(2)}) copy-start(f32[2,1,1,6,128]{4,2,3,1,0:T(1,128)} %param.9) | copy-start | bytes 18436

commit v15 on v14

--- a/solution.py
+++ b/solution.py
@@ -67,7 +67,7 @@
 def send_kernel(core_ref, first_ref, second_ref, send_ref, first, second, sem):
     inner, rows, _, width = first_ref.shape
     ys = send_ref.shape[2]
-    starts = (0, inner // 4 * 3)
+    starts = (0, inner // 2, inner // 8 * 7)
 
     def load(i, k):
         part = pl.ds(starts[i], (starts + (inner,))[i + 1] - starts[i])
@@ -100,7 +100,7 @@
         ),
         in_specs=[SCALAR, ANYWHERE, ANYWHERE],
         out_specs=(VECTOR, VECTOR, VECTOR),
-        scratch_shapes=[pltpu.SemaphoreType.DMA((2, 2))],
+        scratch_shapes=[pltpu.SemaphoreType.DMA((3, 2))],
         compiler_params=pltpu.CompilerParams(vmem_limit_bytes=16 * 2**20),
     )(core, *(pltpu.with_memory_space_constraint(g, pltpu.HBM) for g in (first, second)))
 

time: 68.2 us -> 68.2 us (level)
  no operation moved by 1% of the time
where the time goes in v15:
time: 68.2 us; the launch traced here: 67.9 us
  blocking collectives  60 us (88%)
  Pallas kernels  3.41 us (5%)
  starting transfers between devices  1.92 us (3%)
  waiting for transfers between devices  1.88 us (3%)
  between operations  0.7 us (1%)
    all_to_all x3, blocking collectives, exchange(): return lax.all_to_all(pieces, axes, 0, 0, tiled=True)  60 us
    ppermute x1, starting transfers between devices, local(): other = lax.ppermute(send, 'core', [(0, 1), (1, 0)])  1.92 us
    ppermute x1, waiting for transfers between devices, local(): other = lax.ppermute(send, 'core', [(0, 1), (1, 0)])  1.88 us
    pallas_call x1, Pallas kernels, rows_to_send(): pl.pallas_call(send_kernel, out_shape=(jax.ShapeDtypeStruct(shape, bf16),...  1.85 us
  transfers between devices with their start and end apart: 1, of which 1 were waited for; matrix products, arithmetic and copies ran while one was open for 0% of the time, Pallas kernels for 1%

profile of v15, /device:TPU:8, one launch (start us, length us, event | category | flops | bytes accessed | tf_op | source)
XLA Modules:
  0.0 67.9 jit_solution(3802538965577742305)
XLA Ops:
  0.6 1.8 %shard_map.92 = (bf16[4,2,8,48,128]{4,3,2,1,0:T(8,128)(2,1)S(1)}, bf16[32,6,16,128]{3,2,1,0:T(8,128)(2,1)S(1)}, bf16[32,6,16,128]{3,2,1,0:T(8,128)(2,1)S(1)}) custom-call(s32[1]{0:T(128)} %bitcast.core_ref, bf16[32,6,16,128]{3,2,1,0:T(8,128)(2,1)} %bitcast.32, bf16[32,6,16,128]{3,2,1,0:T(8,128)(2,1)} %bitcast.33), custom_call_target="tpu_custom_call" | custom-call | tf_op jit(solution)/shard_map/pallas_call | solution.py:94
  2.5 1.9 %collective-permute-start = (bf16[4,2,8,48,128]{4,3,2,1,0:T(8,128)(2,1)S(1)}, bf16[4,2,8,48,128]{4,3,2,1,0:T(8,128)(2,1)S(1)}, u32[]{:S(2)}, u32[]{:S(2)}) collective-permute-start(bf16[4,2,8,48,128]{4,3,2,1,0:T(8,128)(2,1)S(1)} %get-tuple-element.19), channel_id=1, source_target_pairs={{0,1},{1,0},{2,3},{3,2},{4,5},{5,4},{6,7},{7,6},{8,9},{9,8},{10,11... | collective-permute-start | bytes 2359304 | tf_op jit(solution)/shard_map/ppermute | solution.py:248
  4.4 0.4 shard_map.93.own_ref
  4.8 1.9 %collective-permute-done.other_ref = bf16[4,2,8,48,128]{4,3,2,1,0:T(8,128)(2,1)S(1)} collective-permute-done((bf16[4,2,8,48,128]{4,3,2,1,0:T(8,128)(2,1)S(1)}, bf16[4,2,8,48,128]{4,3,2,1,0:T(8,128)(2,1)S(1)}, u32[]{:S(2)}, u32[]{:S(2)}) %collective-permute-start) | collective-permute-done | bytes 786464 | tf_op jit(solution)/shard_map/ppermute | solution.py:248
  6.7 0.2 shard_map.94
  6.9 19.1 %all_to_all.15.terms_ref = bf16[8,384,128]{2,1,0:T(8,128)(2,1)S(1)} all-to-all(bf16[8,384,128]{2,1,0:T(8,128)(2,1)S(1)} %bitcast.28), channel_id=1, replica_groups=mesh['x'=4,'y_far'=4,'y_near'=2,'z_far'=4,'z_near'=2,'core'=2] {'x','z_n..., dimensions={0} | all-to-all | bytes 1572864 | tf_op jit(solution)/shard_map/all_to_all | solution.py:238
  26.0 0.1 shard_map.95
  26.1 0.0 copy-start
  26.1 0.0 copy-start.1
  26.1 0.0 copy-start.2
  26.1 27.2 %all_to_all.16.terms_ref = bf16[32,12,128]{2,1,0:T(8,128)(2,1)S(1)} all-to-all(bf16[32,12,128]{2,1,0:T(8,128)(2,1)S(1)} %shard_map.95), channel_id=1, replica_groups=mesh['x'=4,'y_far'=4,'y_near'=2,'z_far'=4,'z_near'=2,'core'=2] {'y_far',..., dimensions={0} | all-to-all | bytes 196608 | tf_op jit(solution)/shard_map/all_to_all | solution.py:238
  53.3 0.0 copy-done
  53.3 0.0 copy-done.1
  53.3 0.0 copy-done.2
  53.3 0.2 shard_map.96
  53.5 13.8 %all_to_all.17.group_ref = bf16[32,16,128]{2,1,0:T(8,128)(2,1)S(1)} all-to-all(bf16[32,16,128]{2,1,0:T(8,128)(2,1)S(1)} %get-tuple-element.20), channel_id=1, replica_groups=mesh['x'=4,'y_far'=4,'y_near'=2,'z_far'=4,'z_near'=2,'core'=2] {'x','y_f..., dimensions={0} | all-to-all | bytes 262144 | tf_op jit(solution)/shard_map/all_to_all | solution.py:238
  67.2 0.7 %shard_map.97 = (bf16[12,32,128]{2,1,0:T(8,128)(2,1)}, bf16[6,2,32]{2,1,0:T(2,128)(2,1)}, f32[12,1,128]{2,1,0:T(1,128)}, f32[12,1,128]{2,1,0:T(1,128)}, f32[12,1,128]{2,1,0:T(1,128)}) custom-call(bf16[32,16,128]{2,1,0:T(8,128)(2,1)S(1)} %all_to_all.17.group_ref, f32[12,1,128]{2,1,0:T(1,128)S(1)} %get-tuple-element.21.refs_0_, ...), custom_call_target="tpu_custom_call" | custom-call | tf_op jit(solution)/shard_map/pallas_call | solution.py:221
Async XLA Ops:
  2.5 4.2 %collective-permute-start = (bf16[4,2,8,48,128]{4,3,2,1,0:T(8,128)(2,1)S(1)}, bf16[4,2,8,48,128]{4,3,2,1,0:T(8,128)(2,1)S(1)}, u32[]{:S(2)}, u32[]{:S(2)}) collective-permute-start(bf16[4,2,8,48,128]{4,3,2,1,0:T(8,128)(2,1)S(1)} %get-tuple-element.19), channel_id=1, source_target_pairs={{0,1},{1,0},{2,3},{3,2},{4,5},{5,4},{6,7},{7,6},{8,9},{9,8},{10,11... | collective-permute-start | bytes 2359304 | tf_op jit(solution)/shard_map/ppermute | solution.py:248
  26.1 27.2 %copy-start = (f32[2,1,1,6,128]{4,2,3,1,0:T(1,128)S(1)}, f32[2,1,1,6,128]{4,2,3,1,0:T(1,128)}, u32[]{:S(2)}) copy-start(f32[2,1,1,6,128]{4,2,3,1,0:T(1,128)} %param.7) | copy-start | bytes 18436
  26.1 27.2 %copy-start.1 = (f32[2,1,1,6,128]{4,2,3,1,0:T(1,128)S(1)}, f32[2,1,1,6,128]{4,2,3,1,0:T(1,128)}, u32[]{:S(2)}) copy-start(f32[2,1,1,6,128]{4,2,3,1,0:T(1,128)} %param.8) | copy-start | bytes 18436
  26.1 27.2 %copy-start.2 = (f32[2,1,1,6,128]{4,2,3,1,0:T(1,128)S(1)}, f32[2,1,1,6,128]{4,2,3,1,0:T(1,128)}, u32[]{:S(2)}) copy-start(f32[2,1,1,6,128]{4,2,3,1,0:T(1,128)} %param.9) | copy-start | bytes 18436
